TPU v7x, 32 devices: a whole 2x2x4 slice. The times are simulated.
32 devices in a mesh: ka: 16 (over z, y, x), orb: 2 (over core).
Axes of the slice: x: 2, y: 2, z: 4, core: 2. Of those that a mesh axis runs over, the one named last changes fastest.
Arguments:
- coeffs: bfloat16 [32, 8192, 256], P('ka', 'orb'), may hold values from -0.62890625 to 0.62890625
- perturbation: bfloat16 [2, 64, 8, 128, 128], P(None, 'orb'), may hold values from -0.1875 to 0.1875
- columns: int32 [64, 8], P('orb'), may hold values from 0 to 63, as said below
- images: int32 [3, 64, 8], P(None, 'orb'), may hold values from -2 to 2
- kpoints: int32 [32], P('ka'), may hold values from 0 to 32767
- matching: int32 [2, 32], replicated, may hold values from 0 to 31, each once within a row
Outputs:
- elph: float32 [32, 2, 2, 128, 128], P('ka', None, None, 'orb')
Inputs may be any that keep to these rules, and one draw needn't show every extreme that they name: `columns`: row block i names 8 distinct column blocks in increasing order, always including i itself, all within the 9 consecutive blocks centred on i, the run moved inward at the two ends of the orbital range. `matching`: each row is a permutation of the k-points.
All inputs are finite; a program needn't handle non-finite values.
Results may differ from a plain program's by a relative error of at most 0.0039.
Values may be sent and summed in bfloat16 or wider, within the bound.
No kernel may reach another device: no remote copies, remote signals or barrier semaphores. Data moves between devices by JAX's collectives and lax.ppermute only.
A program may use at most 256 MiB of HBM per device.

v0:
```python
import math

import jax
import jax.numpy as jnp
from jax import lax
from jax.sharding import PartitionSpec as P

BLK = 128
HALO = 4
KGRID = 32


def extended(x, sides, width):
    for axis, dim in sides:
        size, length = (lax.axis_size(axis), x.shape[dim])
        up = [(i, (i + 1) % size) for i in range(size - 1)]
        down = [(j, i) for i, j in up]
        last = lax.slice_in_dim(x, length - width, length, axis=dim)
        first = lax.slice_in_dim(x, 0, width, axis=dim)
        before = lax.ppermute(last, axis, up)
        after = lax.ppermute(first, axis, down)
        x = jnp.concatenate([before, x, after], axis=dim)
    return x


def phases(kpoints, images):
    first_coord = kpoints // (KGRID * KGRID)
    second_coord = kpoints // KGRID % KGRID
    third_coord = kpoints % KGRID
    turn_count = (
        first_coord[:, None, None] * images[0][None]
        + second_coord[:, None, None] * images[1][None]
        + third_coord[:, None, None] * images[2][None]
    ) % KGRID
    angles = turn_count.astype(jnp.float32) * (2.0 * math.pi / KGRID)
    return (jnp.cos(angles), jnp.sin(angles))


def per_device(coeffs, perturbation, columns, images, kpoints, matching):
    points, row_count, pair_width = coeffs.shape
    band_count = pair_width // 2
    block_count = row_count // BLK
    momenta = perturbation.shape[0]
    padded = extended(coeffs, (("orb", 1),), HALO * BLK)
    first_block = lax.axis_index("orb") * block_count
    local_columns = columns - first_block + HALO
    blocks = padded.reshape(points, block_count + 2 * HALO, BLK, pair_width)
    picked = jnp.take(blocks, local_columns, axis=1)
    cosine, sine_part = phases(kpoints, images)
    cos_k = cosine[..., None, None]
    sin_k = sine_part[..., None, None]
    real_part = picked[..., :band_count].astype(jnp.float32)
    imag_part = picked[..., band_count:].astype(jnp.float32)
    phased = jnp.concatenate(
        [cos_k * real_part - sin_k * imag_part, sin_k * real_part + cos_k * imag_part], axis=-1
    ).astype(jnp.bfloat16)
    ket_image = jnp.einsum(
        "qistu,kisuc->qkitc", perturbation, phased, preferred_element_type=jnp.float32
    )
    ket_image = ket_image.reshape(momenta, points, row_count, pair_width).astype(jnp.bfloat16)
    spread_rows = lax.all_to_all(coeffs, "ka", split_axis=1, concat_axis=0, tiled=True)

    def fetch_bra(matched_order):
        return lax.all_to_all(
            jnp.take(spread_rows, matched_order, axis=0),
            "ka",
            split_axis=0,
            concat_axis=1,
            tiled=True,
        )

    bra_slabs = jnp.stack([fetch_bra(matching[moment]) for moment in range(momenta)])
    product = jnp.einsum(
        "qkrb,qkrc->kqbc", bra_slabs, ket_image, preferred_element_type=jnp.float32
    )
    matrix_real = product[..., :band_count, :band_count] + product[..., band_count:, band_count:]
    matrix_imag = product[..., :band_count, band_count:] - product[..., band_count:, :band_count]
    partial_value = jnp.stack([matrix_real, matrix_imag], axis=2)
    return lax.psum_scatter(partial_value, "orb", scatter_dimension=3, tiled=True)


def solution(mesh):
    in_specs = (
        P("ka", "orb", None),
        P(None, "orb", None, None, None),
        P("orb", None),
        P(None, "orb", None),
        P("ka"),
        P(),
    )
    out_specs = P("ka", None, None, "orb", None)
    return jax.shard_map(
        per_device, mesh=mesh, in_specs=in_specs, out_specs=out_specs, check_vma=False
    )
```

profile of v0, /device:TPU:0, one launch (start us, length us, event | category | flops | bytes accessed | tf_op | source)
XLA Modules:
  0.0 375.7 jit_solution(5447405335019225329)
XLA Ops:
  6.5 0.0 copy-start.2
  6.5 10.1 %copy.53 = bf16[2,4096,256]{2,0,1:T(2,128)(2,1)} copy(bf16[2,4096,256]{2,1,0:T(8,128)(2,1)} %param.8) | data formatting | bytes 8388608 | tf_op args[0]
  16.7 8.4 %all-to-all-start = ((bf16[2,4096,256]{2,0,1:T(2,128)(2,1)}), bf16[2,4096,256]{2,0,1:T(2,128)(2,1)}, u32[]{:S(2)}, u32[]{:S(2)}) async-start(bf16[2,4096,256]{2,0,1:T(2,128)(2,1)} %copy.53), calls=%async_computation | async-start | bytes 8388608 | tf_op jit(solution)/shard_map/all_to_all | solution.py:61
  25.0 0.0 copy-done.2
  25.1 79.7 %all-to-all-done = bf16[2,4096,256]{2,0,1:T(2,128)(2,1)} async-done(((bf16[2,4096,256]{2,0,1:T(2,128)(2,1)}), bf16[2,4096,256]{2,0,1:T(2,128)(2,1)}, u32[]{:S(2)}, u32[]{:S(2)}) %all-to-all-start) | async-done | bytes 4194336 | tf_op jit(solution)/shard_map/all_to_all | solution.py:61
  104.8 2.7 copy.54
  107.5 2.2 copy.55
  109.7 5.0 %gather_fusion.1 = bf16[32,256,256]{2,1,0:T(8,128)(2,1)} fusion(bf16[32,256,256]{2,1,0:T(8,128)(2,1)} %bitcast.59, s32[1024]{0:T(1024)S(1)} %pad_clamp_fusion.2), kind=kCustom, calls=%fused_computation.clone | custom fusion | bytes 8388736 | tf_op jit(solution)/shard_map/jit(_take)/gather | solution.py:65
  114.7 0.0 copy-start.3
  114.7 0.0 copy-start
  114.7 4.7 %broadcast_select_fusion.1 = bf16[32,256,256]{2,1,0:T(8,128)(2,1)} fusion(bf16[32,256,256]{2,1,0:T(8,128)(2,1)} %gather_fusion.1, pred[32]{0:T(512)(128)(4,1)S(1)} %get-tuple-element.8), kind=kLoop, calls=%fused_computation.27 | loop fusion | flops 2097152 | bytes 8388640 | tf_op jit(solution)/shard_map/jit(_take)/select_n | solution.py:65
  119.4 20.1 %all-to-all-start.1 = ((bf16[32,256,256]{2,1,0:T(8,128)(2,1)}), bf16[32,256,256]{2,1,0:T(8,128)(2,1)}, u32[]{:S(2)}, u32[]{:S(2)}) async-start(bf16[32,256,256]{2,1,0:T(8,128)(2,1)} %broadcast_select_fusion.1), calls=%async_computation.1 | async-start | bytes 8388608 | tf_op jit(solution)/shard_map/all_to_all | solution.py:64
  139.4 1.3 fusion.27
  140.7 1.3 collective-permute-start
  142.1 1.3 collective-permute-start.1
  143.4 0.0 copy-done.3
  143.4 0.0 copy-done
  143.4 0.1 fusion.23
  143.6 0.1 copy.58
  143.6 0.1 copy.62
  143.7 0.0 copy-done.1
  143.8 0.1 copy.60
  143.8 0.1 reshape.59
  143.9 0.1 copy.59
  144.0 0.0 collective-permute-done
  144.1 1.8 collective-permute-done.1
  145.9 9.0 %pad_maximum_fusion = bf16[2,5120,256]{2,1,0:T(8,128)(2,1)} fusion(bf16[2,512,256]{2,1,0:T(8,128)(2,1)S(1)} %collective-permute-done.1, bf16[2,4096,256]{2,1,0:T(8,128)(2,1)} %param.8, bf16[2,512,256]{2,1,0:T(8,128)(2,1)S(1)} %collective-permute-done), kind=kLoop, calls=%fused_computation.25 | loop fusion | flops 15728640 | bytes 10485760 | tf_op jit(solution)/shard_map/concatenate | solution.py:22
  154.9 16.4 %gather_fusion = bf16[256,2,128,256]{3,2,1,0:T(8,128)(2,1)} fusion(bf16[2,40,128,256]{3,2,1,0:T(8,128)(2,1)} %bitcast.57, s32[1024]{0:T(1024)S(1)} %pad_clamp_fusion), kind=kCustom, calls=%fused_computation.2 | custom fusion | bytes 67109888 | tf_op jit(solution)/shard_map/jit(_take)/gather | solution.py:48
  171.3 5.0 %gather_fusion.2 = bf16[32,256,256]{2,1,0:T(8,128)(2,1)} fusion(bf16[32,256,256]{2,1,0:T(8,128)(2,1)} %bitcast.60, s32[1024]{0:T(1024)S(1)} %pad_clamp_fusion.1), kind=kCustom, calls=%fused_computation.1.clone | custom fusion | bytes 8388736 | tf_op jit(solution)/shard_map/jit(_take)/gather | solution.py:65
  176.3 4.6 %broadcast_select_fusion = bf16[32,256,256]{2,1,0:T(8,128)(2,1)} fusion(bf16[32,256,256]{2,1,0:T(8,128)(2,1)} %gather_fusion.2, pred[32]{0:T(512)(128)(4,1)S(1)} %get-tuple-element.23), kind=kLoop, calls=%fused_computation.26 | loop fusion | flops 2097152 | bytes 8388640 | tf_op jit(solution)/shard_map/jit(_take)/select_n | solution.py:65
  180.9 37.0 %all-to-all-done.1 = bf16[32,256,256]{2,1,0:T(8,128)(2,1)} async-done(((bf16[32,256,256]{2,1,0:T(8,128)(2,1)}), bf16[32,256,256]{2,1,0:T(8,128)(2,1)}, u32[]{:S(2)}, u32[]{:S(2)}) %all-to-all-start.1) | async-done | bytes 4194336 | tf_op jit(solution)/shard_map/all_to_all | solution.py:64
  217.9 19.3 %all-to-all-start.2 = ((bf16[32,256,256]{2,1,0:T(8,128)(2,1)}), bf16[32,256,256]{2,1,0:T(8,128)(2,1)}, u32[]{:S(2)}, u32[]{:S(2)}) async-start(bf16[32,256,256]{2,1,0:T(8,128)(2,1)} %broadcast_select_fusion), calls=%async_computation.2 | async-start | bytes 8388608 | tf_op jit(solution)/shard_map/all_to_all | solution.py:64
  237.2 0.2 reduce-scatter.2.cloned.1.call-start
  237.5 22.8 %fusion.7 = bf16[2,32,8,128,256]{4,3,2,0,1:T(8,128)(2,1)} fusion(bf16[32,8,2,128,256]{4,3,2,1,0:T(8,128)(2,1)} %bitcast.58, pred[32,8]{1,0:T(8,128)(4,1)S(1)} %copy.59), kind=kLoop, calls=%fused_computation.16 | loop fusion | flops 16777216 | bytes 67109120 | tf_op jit(solution)/shard_map/jit(_take)/select_n | solution.py:48
  260.3 30.2 %fusion.1 = (bf16[2,32,8,128,128]{4,3,2,0,1:T(8,128)(2,1)}, bf16[2,32,8,128,128]{4,3,2,0,1:T(8,128)(2,1)}) fusion(f32[2,32,8]{2,0,1:T(2,128)S(1)} %copy.62, f32[2,32,8]{2,0,1:T(2,128)S(1)} %copy.58, bf16[2,32,8,128,256]{4,3,2,0,1:T(8,128)(2,1)} %fusion.7), kind=kLoop, calls=%fused_computation.8 | loop fusion | flops 83886080 | bytes 67112960 | tf_op jit(solution)/shard_map/convert
  290.5 21.0 %fusion.9 = bf16[2,2,32,128,256]{4,3,0,1,2:T(8,128)(2,1)} fusion(bf16[2,32,8,128,128]{4,3,2,0,1:T(8,128)(2,1)} %get-tuple-element.13, bf16[2,32,8,128,128]{4,3,2,0,1:T(8,128)(2,1)} %get-tuple-element.12, bf16[2,32,8,128,128]{4,3,2,1,0:T(8,128)(2,1)} %param.9), kind=kOutput, calls=%fused_computation.19 | convolution fusion | flops 8661237760 | bytes 58720256 | tf_op jit(solution)/shard_map/qistu,kisuc->qkitc/dot_general | solution.py:57
  311.5 7.7 %copy.64 = bf16[2,2,32,128,256]{4,3,2,1,0:T(8,128)(2,1)} copy(bf16[2,2,32,128,256]{4,3,0,1,2:T(8,128)(2,1)} %fusion.9) | data formatting | bytes 16777216 | tf_op jit(solution)/shard_map/convert_element_type | solution.py:60
  319.2 7.9 %copy.56 = bf16[2,16,256,256]{2,1,3,0:T(8,128)(2,1)} copy(bf16[2,16,256,256]{3,2,0,1:T(8,128)(2,1)} %bitcast.5) | data formatting | bytes 8388608 | tf_op jit(solution)/shard_map/all_to_all | solution.py:64
  327.1 7.4 %stack.18 = bf16[1,2,4096,256]{2,3,0,1:T(8,128)(2,1)} reshape(bf16[2,16,256,256]{2,1,3,0:T(8,128)(2,1)} %copy.56) | data formatting | bytes 8388608 | tf_op jit(solution)/shard_map/stack | solution.py:72
  334.5 0.0 all-to-all-done.2
  334.5 7.9 %copy.57 = bf16[2,16,256,256]{2,1,3,0:T(8,128)(2,1)} copy(bf16[2,16,256,256]{3,2,0,1:T(8,128)(2,1)} %bitcast.8) | data formatting | bytes 8388608 | tf_op jit(solution)/shard_map/all_to_all | solution.py:64
  342.4 7.4 %stack.19 = bf16[1,2,4096,256]{2,3,0,1:T(8,128)(2,1)} reshape(bf16[2,16,256,256]{2,1,3,0:T(8,128)(2,1)} %copy.57) | data formatting | bytes 8388608 | tf_op jit(solution)/shard_map/stack | solution.py:72
  349.8 7.1 %fusion.10 = f32[2,2,256,256]{3,2,1,0:T(8,128)S(1)} fusion(bf16[1,2,4096,256]{2,3,0,1:T(8,128)(2,1)} %stack.19, bf16[1,2,4096,256]{2,3,0,1:T(8,128)(2,1)} %stack.18, bf16[2,2,4096,256]{3,2,1,0:T(8,128)(2,1)} %bitcast.62), kind=kOutput, calls=%fused_computation.20 | convolution fusion | flops 2151677952 | bytes 17825792 | tf_op jit(solution)/shard_map/qkrb,qkrc->kqbc/dot_general | solution.py:73
  356.9 0.1 fusion.18
  357.0 0.8 pad_maximum_fusion.1
  357.8 0.0 reduce-scatter.2.cloned.1.call-update
  357.8 9.3 %reduce-scatter.2.cloned.1.call-done = f32[2,2,2,64,128]{4,3,1,0,2:T(8,128)} async-done(((f32[2,2,2,128,128]{4,3,1,0,2:T(8,128)}), f32[2,2,2,64,128]{4,3,1,0,2:T(8,128)}) %reduce-scatter.2.cloned.1.call-update) | async-done | bytes 262160 | tf_op jit(solution)/shard_map/reduce_scatter | solution.py:79
  367.2 1.7 copy.66
  (8 shorter events, 0.1 us)
Async XLA Ops:
  6.5 18.5 %copy-start.2 = (s32[2,32]{1,0:T(2,128)S(1)}, s32[2,32]{1,0:T(2,128)}, u32[]{:S(2)}) copy-start(s32[2,32]{1,0:T(2,128)} %param.13) | copy-start | bytes 772
  16.7 88.1 %all-to-all-start = ((bf16[2,4096,256]{2,0,1:T(2,128)(2,1)}), bf16[2,4096,256]{2,0,1:T(2,128)(2,1)}, u32[]{:S(2)}, u32[]{:S(2)}) async-start(bf16[2,4096,256]{2,0,1:T(2,128)(2,1)} %copy.53), calls=%async_computation | async-start | bytes 8388608 | tf_op jit(solution)/shard_map/all_to_all | solution.py:61
  114.7 28.6 %copy-start.3 = (s32[2]{0:T(128)S(1)}, s32[2]{0:T(128)}, u32[]{:S(2)}) copy-start(s32[2]{0:T(128)} %param.12) | copy-start | bytes 28
  114.7 28.7 %copy-start = (s32[3,32,8]{1,2,0:T(8,128)S(1)}, s32[3,32,8]{1,2,0:T(8,128)}, u32[]{:S(2)}) copy-start(s32[3,32,8]{1,2,0:T(8,128)} %param.11) | copy-start | bytes 9220
  114.7 29.0 %copy-start.1 = (s32[32,8]{0,1:T(8,128)S(1)}, s32[32,8]{0,1:T(8,128)}, u32[]{:S(2)}) copy-start(s32[32,8]{0,1:T(8,128)} %param.10) | copy-start | bytes 3076
  119.4 98.5 %all-to-all-start.1 = ((bf16[32,256,256]{2,1,0:T(8,128)(2,1)}), bf16[32,256,256]{2,1,0:T(8,128)(2,1)}, u32[]{:S(2)}, u32[]{:S(2)}) async-start(bf16[32,256,256]{2,1,0:T(8,128)(2,1)} %broadcast_select_fusion.1), calls=%async_computation.1 | async-start | bytes 8388608 | tf_op jit(solution)/shard_map/all_to_all | solution.py:64
  140.7 3.3 collective-permute-start
  142.1 3.8 %collective-permute-start.1 = (bf16[2,512,256]{2,1,0:T(8,128)(2,1)S(1)}, bf16[2,512,256]{2,1,0:T(8,128)(2,1)S(1)}, u32[]{:S(2)}, u32[]{:S(2)}) collective-permute-start(bf16[2,512,256]{2,1,0:T(8,128)(2,1)S(1)} %get-tuple-element.15), channel_id=1, source_target_pairs={{1,0},{3,2},{5,4},{7,6},{9,8},{11,10},{13,12},{15,14},{17,16},{19,... | collective-permute-start | bytes 1572872 | tf_op jit(solution)/shard_map/ppermute | solution.py:21
  217.9 116.6 %all-to-all-start.2 = ((bf16[32,256,256]{2,1,0:T(8,128)(2,1)}), bf16[32,256,256]{2,1,0:T(8,128)(2,1)}, u32[]{:S(2)}, u32[]{:S(2)}) async-start(bf16[32,256,256]{2,1,0:T(8,128)(2,1)} %broadcast_select_fusion), calls=%async_computation.2 | async-start | bytes 8388608 | tf_op jit(solution)/shard_map/all_to_all | solution.py:64
  237.2 130.0 %reduce-scatter.2.cloned.1.call-start = ((), (), s32[]{:S(2)}) async-start(), calls=%async_computation.4 | async-start | bytes 786432 | tf_op jit(solution)/shard_map/reduce_scatter | solution.py:79
Sparse Core Ops, SparseCore 0:
  358.0 9.1 reduce-scatter.1
where the time goes:
time: 377 us; the launch traced here: 376 us
  waiting for transfers between devices  128 us (34%)
  local copies, waits for them, and re-layouts  83.2 us (22%)
  other arithmetic  72.5 us (19%)
  starting transfers between devices  50.6 us (13%)
  matrix products  28.1 us (7%)
  between operations  13.6 us (4%)
    all_to_all x1, waiting for transfers between devices, per_device(): lax.all_to_all(coeffs, 'ka', split_axis=1, concat_axis=0, tiled=True)  79.7 us
    all_to_all x2, starting transfers between devices, fetch_bra(): lax.all_to_all(jnp.take(spread_rows, matched_order, axis=0), 'ka', split_...  39.4 us
    all_to_all x2, waiting for transfers between devices, fetch_bra(): lax.all_to_all(jnp.take(spread_rows, matched_order, axis=0), 'ka', split_...  37 us
    another operation x1, other arithmetic  30.2 us
    select_n x1, other arithmetic, per_device(): picked = jnp.take(blocks, local_columns, axis=1)  22.8 us
    dot_general x1, matrix products, per_device(): jnp.einsum('qistu,kisuc->qkitc', perturbation, phased, preferred_element_...  21 us
    gather x1, local copies, waits for them, and re-layouts, per_device(): picked = jnp.take(blocks, local_columns, axis=1)  16.4 us
    all_to_all x2, local copies, waits for them, and re-layouts, fetch_bra(): lax.all_to_all(jnp.take(spread_rows, matched_order, axis=0), 'ka', split_...  15.8 us
  transfers between devices with their start and end apart: 6, of which 4 were waited for; matrix products, arithmetic and copies ran while one was open for 36% of the time, Pallas kernels for 0%

commit v1 on v0

v1 whole, which is shorter than its diff:
```python
import functools
import math

import jax
import jax.numpy as jnp
from jax import lax
from jax.experimental import pallas as pl
from jax.experimental.pallas import tpu as pltpu
from jax.sharding import PartitionSpec as P

BLK = 128
HALO = 4
KGRID = 32
VMEM = 48 * 1024 * 1024


def phases(kpoints, images):
    first_coord = kpoints // (KGRID * KGRID)
    second_coord = kpoints // KGRID % KGRID
    third_coord = kpoints % KGRID
    turn_count = (
        first_coord[:, None, None] * images[0][None]
        + second_coord[:, None, None] * images[1][None]
        + third_coord[:, None, None] * images[2][None]
    ) % KGRID
    angles = turn_count.astype(jnp.float32) * (2.0 * math.pi / KGRID)
    return (jnp.cos(angles), jnp.sin(angles))


def image_kernel(columns, cosine, sine, ket_ref, weight_ref, out_ref):
    block = pl.program_id(0)
    momenta, _, slots, size, _ = weight_ref.shape
    points, _, width = ket_ref.shape
    bands = width // 2
    weights = jnp.concatenate(
        [
            jnp.concatenate([weight_ref[q, 0, s] for s in range(slots)], axis=1)
            for q in range(momenta)
        ],
        axis=0,
    )
    for point in range(points):
        parts = []
        for s in range(slots):
            start = pl.multiple_of(columns[block, s] * size, size)
            real = ket_ref[point, pl.ds(start, size), :bands].astype(jnp.float32)
            imag = ket_ref[point, pl.ds(start, size), bands:].astype(jnp.float32)
            c, d = cosine[point, block, s], sine[point, block, s]
            turned = jnp.concatenate([c * real - d * imag, d * real + c * imag], axis=1)
            parts.append(turned.astype(jnp.bfloat16))
        image = jnp.dot(
            weights, jnp.concatenate(parts, axis=0), preferred_element_type=jnp.float32
        )
        for q in range(momenta):
            out_ref[point, q] = image[q * size : (q + 1) * size].astype(out_ref.dtype)


def ket_images(columns, cosine, sine, kets, weights):
    momenta, blocks, slots, size, _ = weights.shape
    points, rows, width = kets.shape
    flops = 2 * points * momenta * blocks * slots * size * size * width
    return pl.pallas_call(
        image_kernel,
        grid_spec=pltpu.PrefetchScalarGridSpec(
            num_scalar_prefetch=3,
            grid=(blocks,),
            in_specs=[
                pl.BlockSpec((points, rows, width), lambda i, *_: (0, 0, 0)),
                pl.BlockSpec((momenta, 1, slots, size, size), lambda i, *_: (0, i, 0, 0, 0)),
            ],
            out_specs=pl.BlockSpec((points, momenta, size, width), lambda i, *_: (0, 0, i, 0)),
        ),
        out_shape=jax.ShapeDtypeStruct((points, momenta, blocks * size, width), jnp.bfloat16),
        compiler_params=pltpu.CompilerParams(vmem_limit_bytes=VMEM),
        cost_estimate=pl.CostEstimate(
            flops=flops, bytes_accessed=weights.size * 2 + kets.size * 4, transcendentals=0
        ),
        name="ket_images",
    )(columns, cosine, sine, kets, weights)


def product_kernel(groups, bras, choice, *refs):
    image_refs, bra_refs = refs[:groups], refs[groups : groups + bras]
    out_ref, image_buf, bra_buf, image_sem, bra_sem = refs[groups + bras :]
    pairs = choice.shape[0]
    per_group = pairs // groups
    halves, half = out_ref.shape[0], out_ref.shape[3]
    bands = halves * half

    @pl.loop(0, pairs)
    def _(pair):
        wanted = choice[pair]
        for number, ref in enumerate(bra_refs):

            @pl.when(wanted == number)
            def _():
                pltpu.make_async_copy(ref, bra_buf.at[pair], bra_sem.at[pair]).start()

    def image_copy(group):
        spot = pl.ds(group * per_group, per_group)
        return pltpu.make_async_copy(image_refs[group], image_buf.at[spot], image_sem.at[group])

    for group in range(groups):
        image_copy(group).start()
    for group in range(groups):
        image_copy(group).wait()

        @pl.loop(group * per_group, (group + 1) * per_group)
        def _(pair):
            pltpu.make_async_copy(bra_refs[0], bra_buf.at[pair], bra_sem.at[pair]).wait()
            value = lax.dot_general(
                bra_buf[pair],
                image_buf[pair],
                (((0,), (0,)), ((), ())),
                preferred_element_type=jnp.float32,
            )
            real = value[:bands, :bands] + value[bands:, bands:]
            imag = value[:bands, bands:] - value[bands:, :bands]
            for h in range(halves):
                out_ref[h, pair, 0] = real[h * half : (h + 1) * half]
                out_ref[h, pair, 1] = imag[h * half : (h + 1) * half]


def products(choice, images, bras, halves):
    groups = len(images)
    rows, width = bras[0].shape
    pairs = choice.shape[0]
    bands = width // 2
    images = [image.reshape(pairs // groups, rows, width) for image in images]
    return pl.pallas_call(
        functools.partial(product_kernel, groups, len(bras)),
        in_specs=[pl.BlockSpec(memory_space=pltpu.SMEM)]
        + [pl.BlockSpec(memory_space=pl.ANY)] * (groups + len(bras)),
        out_specs=pl.BlockSpec(memory_space=pltpu.VMEM),
        out_shape=jax.ShapeDtypeStruct((halves, pairs, 2, bands // halves, bands), jnp.float32),
        scratch_shapes=[
            pltpu.VMEM((pairs, rows, width), jnp.bfloat16),
            pltpu.VMEM((pairs, rows, width), jnp.bfloat16),
            pltpu.SemaphoreType.DMA((groups,)),
            pltpu.SemaphoreType.DMA((pairs,)),
        ],
        compiler_params=pltpu.CompilerParams(vmem_limit_bytes=VMEM),
        cost_estimate=pl.CostEstimate(
            flops=2 * pairs * rows * width * width,
            bytes_accessed=4 * pairs * rows * width,
            transcendentals=0,
        ),
        name="products",
    )(choice, *images, *bras)


def per_device(coeffs, perturbation, columns, images, kpoints, matching):
    n_ka, n_orb = lax.axis_size("ka"), lax.axis_size("orb")
    points, row_count, width = coeffs.shape
    block_count = row_count // BLK
    momenta = perturbation.shape[0]
    bits_of = lambda n: n.bit_length() - 1
    n_rows = min(n_ka, block_count // (2 * HALO))
    n_side = n_ka // n_rows
    share = n_rows // n_orb
    blocks = block_count // n_rows
    rows = blocks * BLK
    me, core = lax.axis_index("ka"), lax.axis_index("orb")
    z, side = me // n_side, me % n_side

    def flat(zi, gi, ci):
        return (zi * n_side + gi) * n_orb + ci

    every = [(zi, gi, ci) for zi in range(n_rows) for gi in range(n_side) for ci in range(n_orb)]

    def send(x, to):
        moves = [(flat(*spot), to(*spot)) for spot in every]
        return lax.ppermute(x, ("ka", "orb"), [(a, flat(*b)) for a, b in moves if b is not None])

    def on_core(x, d):
        return send(x, lambda zi, gi, ci: (zi, gi, (ci + d) % n_orb))

    def across_rows(x, s):
        return send(x, lambda zi, gi, ci: (zi ^ s, gi, ci))

    def across_side(x, bit):
        return send(x, lambda zi, gi, ci: (zi, gi ^ (1 << bit), ci))

    def along(x, step):
        def to(zi, gi, ci):
            spot = zi * n_orb + ci + step
            return (spot // n_orb, gi, spot % n_orb) if 0 <= spot < n_rows * n_orb else None

        return send(x, to)

    def pick(x, index, axis):
        return lax.dynamic_index_in_dim(x, index, axis, keepdims=False)

    held = coeffs.reshape(points, share, n_orb, rows, width)
    mine = [pick(held, core, 2)]
    mine += [on_core(pick(held, (core + d) % n_orb, 2), d) for d in range(1, n_orb)]

    def slice_for(zi):
        source, index = zi // share, zi % share
        out = pick(mine[0], index, 1)
        for d in range(1, n_orb):
            out = jnp.where((core - source) % n_orb == d, pick(mine[d], index, 1), out)
        return out

    def own_rows(x, axis):
        def part(ci):
            index = (n_orb * z + ci) % n_rows
            return lax.dynamic_slice_in_dim(x, index * blocks, blocks, axis)

        source = (n_orb * z + core) // n_rows
        out = part(core)
        for d in range(1, n_orb):
            came = on_core(part((core + d) % n_orb), d)
            out = jnp.where((core - source) % n_orb == d, came, out)
        return out

    groups = [slice_for(z)]
    for s in range(1, n_rows):
        wanted = z ^ s
        if s > 2:
            token = groups[s - 2][0, 0, 0]
            wanted = wanted + (token != token).astype(wanted.dtype)
        groups.append(across_rows(slice_for(wanted), s))

    bits = list(range(bits_of(n_side)))
    bras = []
    for group in groups:
        have = []
        for point in range(points):
            found = {0: group[point]}
            turn = point % max(1, len(bits))
            for bit in bits[turn:] + bits[:turn]:
                found.update({p ^ (1 << bit): across_side(x, bit) for p, x in list(found.items())})
            have.append(found)
        bras += [have[point][p] for p in range(n_side) for point in range(points)]

    weights = own_rows(perturbation, 1)
    table = own_rows(jnp.concatenate([columns[None], images]), 1)
    local_columns = table[0] - (n_orb * z + core) * blocks + HALO
    reach = HALO * BLK

    def towards(s, step, start):
        edge = core == (n_orb - 1 if step > 0 else 0)
        out = groups[s][:, start : start + reach]
        for x in sorted({a ^ (a + 1) for a in range(n_rows - 1)}):
            other = groups[s ^ x][:, start : start + reach]
            out = jnp.where(edge & ((z ^ (z + step)) == x), other, out)
        return out

    ket_list, choices = [], []
    for s, group in enumerate(groups):
        before = along(towards(s, 1, rows - reach), 1)
        after = along(towards(s, -1, 0), -1)
        kets = jnp.concatenate([before, group, after], axis=1)
        k_here = kpoints if s == 0 else across_rows(kpoints, s)
        cosine, sine = phases(k_here, table[1:])
        ket_list.append(ket_images(local_columns, cosine, sine, kets, weights))
        first = ((z ^ s) * n_side + side) * points
        found = lax.dynamic_slice_in_dim(matching, first, points, 1).T
        owner = found // points
        number = ((owner // n_side) ^ z) * n_side + ((owner % n_side) ^ side)
        choices.append((number * points + found % points).reshape(-1))

    value = products(jnp.concatenate(choices), ket_list, bras, n_orb)
    total = pick(value, core, 0)
    for d in range(1, n_orb):
        total = total + on_core(pick(value, (core + d) % n_orb, 0), d)
    total = total.reshape(n_rows, points, momenta, *total.shape[1:])
    out = total[0]
    for s in range(1, n_rows):
        out = out + across_rows(total[s], s)
    return out


def solution(mesh):
    in_specs = (
        P("ka", "orb", None),
        P(None, "orb", None, None, None),
        P("orb", None),
        P(None, "orb", None),
        P("ka"),
        P(),
    )
    out_specs = P("ka", None, None, "orb", None)
    return jax.shard_map(
        per_device, mesh=mesh, in_specs=in_specs, out_specs=out_specs, check_vma=False
    )
```

time: 377 us -> 324 us (0.86)
  local copies, waits for them, and re-layouts: 83.2 us -> 18.3 us
  waiting for transfers between devices: 128 us -> 187 us
  other arithmetic: 72.5 us -> 14.5 us
  Pallas kernels: 0 us -> 42.8 us
  matrix products: 28.1 us -> 0 us
  between operations: 13.6 us -> 2.04 us
  starting transfers between devices: 50.6 us -> 54.6 us
    ppermute x2 -> x45, waiting for transfers between devices: 1.81 us -> 187 us  [send(): lax.ppermute(x, ('ka', 'orb'), [(a, flat(*b)) for a, b in moves if b is n...]
    all_to_all x3 -> x0, waiting for transfers between devices: 117 us -> none  [the longest x1 79.7 us: per_device(): lax.all_to_all(coeffs, 'ka', split_axis=1, concat_axis=0, tiled=True)]
    ppermute x2 -> x45, starting transfers between devices: 2.61 us -> 54.6 us  [send(): lax.ppermute(x, ('ka', 'orb'), [(a, flat(*b)) for a, b in moves if b is n...]
    all_to_all x3 -> x0, starting transfers between devices: 47.7 us -> none  [the longest x2 39.4 us: fetch_bra(): lax.all_to_all(jnp.take(spread_rows, matched_order, axis=0), 'ka', split_...]
    pallas_call x0 -> x5, Pallas kernels: none -> 42.8 us  [the longest x4 31.5 us: ket_images(): pl.pallas_call(image_kernel, grid_spec=pltpu.PrefetchScalarGridSpec(num_s...]
    another operation x3 -> x0, other arithmetic: 31.1 us -> none
    dot_general x2 -> x0, matrix products: 28.1 us -> none  [the longest x1 21 us: per_device(): jnp.einsum('qistu,kisuc->qkitc', perturbation, phased, preferred_element_...]
    gather x3 -> x0, local copies, waits for them, and re-layouts: 26.3 us -> none  [the longest x1 16.4 us: per_device(): picked = jnp.take(blocks, local_columns, axis=1)]
  transfers between devices with their start and end apart: 6 -> 45, of which waited for: 4 -> 18; matrix products, arithmetic and copies ran while one was open for 36% -> 6% of each run, Pallas kernels for 0% -> 10%
where the time goes in v1:
time: 324 us; the launch traced here: 320 us
  waiting for transfers between devices  187 us (58%)
  starting transfers between devices  54.6 us (17%)
  Pallas kernels  42.8 us (13%)
  local copies, waits for them, and re-layouts  18.3 us (6%)
  other arithmetic  14.5 us (4%)
    ppermute x45, waiting for transfers between devices, send(): lax.ppermute(x, ('ka', 'orb'), [(a, flat(*b)) for a, b in moves if b is n...  187 us
    ppermute x45, starting transfers between devices, send(): lax.ppermute(x, ('ka', 'orb'), [(a, flat(*b)) for a, b in moves if b is n...  54.6 us
    pallas_call x4, Pallas kernels, ket_images(): pl.pallas_call(image_kernel, grid_spec=pltpu.PrefetchScalarGridSpec(num_s...  31.5 us
    pallas_call x1, Pallas kernels, products(): pl.pallas_call(functools.partial(product_kernel, groups, len(bras)), in_s...  11.3 us
    unnamed x70, local copies, waits for them, and re-layouts  6.72 us
  transfers between devices with their start and end apart: 45, of which 18 were waited for; matrix products, arithmetic and copies ran while one was open for 6% of the time, Pallas kernels for 10%

profile of v1, /device:TPU:0, one launch (start us, length us, event | category | flops | bytes accessed | tf_op | source)
XLA Modules:
  0.0 319.5 jit_solution(528573756514724388)
XLA Ops:
  0.0 3.0 copy_bitcast_fusion
  3.5 4.8 %constant_dynamic-slice_fusion = bf16[2,8,8,128,128]{4,3,2,1,0:T(8,128)(2,1)} fusion(bf16[2,32,8,128,128]{4,3,2,1,0:T(8,128)(2,1)} %param.7, s32[]{:T(128)S(6)} %select_n.425), kind=kLoop, calls=%fused_computation.60 | loop fusion | bytes 8388612 | tf_op jit(solution)/shard_map/dynamic_slice | solution.py:208
  8.4 2.3 bitcast_select_fusion.3
  10.7 3.0 collective-permute-start.2
  13.8 2.5 collective-permute-start.14
  17.7 19.6 %collective-permute-done.2 = bf16[2,1024,256]{2,1,0:T(8,128)(2,1)S(1)} collective-permute-done((bf16[2,1024,256]{2,1,0:T(8,128)(2,1)}, bf16[2,1024,256]{2,1,0:T(8,128)(2,1)S(1)}, u32[]{:S(2)}, u32[]{:S(2)}) %collective-permute-start.2) | collective-permute-done | bytes 1048608 | tf_op jit(solution)/shard_map/ppermute | solution.py:173
  39.2 2.3 bitcast_select_fusion
  41.5 1.7 collective-permute-start.17
  43.3 1.5 collective-permute-start.20
  44.8 1.6 collective-permute-start.7
  46.4 2.0 collective-permute-done.7
  48.4 3.5 %collective-permute-start.3 = (bf16[2,1024,256]{2,1,0:T(8,128)(2,1)S(1)}, bf16[2,1024,256]{2,1,0:T(8,128)(2,1)S(1)}, u32[]{:S(2)}, u32[]{:S(2)}) collective-permute-start(bf16[2,1024,256]{2,1,0:T(8,128)(2,1)S(1)} %get-tuple-element.7), channel_id=1, source_target_pairs={{0,24},{1,25},{2,26},{3,27},{4,28},{5,29},{6,30},{7,31},{8,16},{9,... | collective-permute-start | bytes 3145736 | tf_op jit(solution)/shard_map/ppermute | solution.py:173
  52.0 2.8 collective-permute-done.17.refs_6_
  54.8 1.3 collective-permute-start.18
  56.2 1.5 collective-permute-start.19
  57.8 9.4 %collective-permute-done.18.refs_7_ = bf16[1024,256]{1,0:T(8,128)(2,1)S(1)} collective-permute-done((bf16[1024,256]{1,0:T(8,128)(2,1)S(1)}, bf16[1024,256]{1,0:T(8,128)(2,1)S(1)}, u32[]{:S(2)}, u32[]{:S(2)}) %collective-permute-start.18) | collective-permute-done | bytes 524320 | tf_op jit(solution)/shard_map/ppermute | solution.py:173
  69.7 6.7 %collective-permute-done.3 = bf16[2,1024,256]{2,1,0:T(8,128)(2,1)S(1)} collective-permute-done((bf16[2,1024,256]{2,1,0:T(8,128)(2,1)S(1)}, bf16[2,1024,256]{2,1,0:T(8,128)(2,1)S(1)}, u32[]{:S(2)}, u32[]{:S(2)}) %collective-permute-start.3) | collective-permute-done | bytes 1048608 | tf_op jit(solution)/shard_map/ppermute | solution.py:173
  76.9 62.7 %collective-permute-done.8 = bf16[2,1024,256]{2,1,0:T(8,128)(2,1)S(1)} collective-permute-done((bf16[2,1024,256]{2,1,0:T(8,128)(2,1)S(1)}, bf16[2,1024,256]{2,1,0:T(8,128)(2,1)S(1)}, u32[]{:S(2)}, u32[]{:S(2)}) %collective-permute-start.8) | collective-permute-done | bytes 1048608 | tf_op jit(solution)/shard_map/ppermute | solution.py:173
  140.4 1.9 collective-permute-start.21
  143.0 11.5 %collective-permute-done.25.refs_16_ = bf16[1024,256]{1,0:T(8,128)(2,1)S(1)} collective-permute-done((bf16[1024,256]{1,0:T(8,128)(2,1)S(1)}, bf16[1024,256]{1,0:T(8,128)(2,1)S(1)}, u32[]{:S(2)}, u32[]{:S(2)}) %collective-permute-start.25) | collective-permute-done | bytes 524320 | tf_op jit(solution)/shard_map/ppermute | solution.py:173
  155.3 10.4 %collective-permute-done.21.refs_10_ = bf16[1024,256]{1,0:T(8,128)(2,1)S(1)} collective-permute-done((bf16[1024,256]{1,0:T(8,128)(2,1)S(1)}, bf16[1024,256]{1,0:T(8,128)(2,1)S(1)}, u32[]{:S(2)}, u32[]{:S(2)}) %collective-permute-start.21) | collective-permute-done | bytes 524320 | tf_op jit(solution)/shard_map/ppermute | solution.py:173
  168.3 6.7 %collective-permute-done.27.refs_18_ = bf16[1024,256]{1,0:T(8,128)(2,1)S(1)} collective-permute-done((bf16[1024,256]{1,0:T(8,128)(2,1)S(1)}, bf16[1024,256]{1,0:T(8,128)(2,1)S(1)}, u32[]{:S(2)}, u32[]{:S(2)}) %collective-permute-start.27) | collective-permute-done | bytes 524320 | tf_op jit(solution)/shard_map/ppermute | solution.py:173
  175.0 2.1 collective-permute-start.12
  180.6 4.8 %dynamic-slice_select_fusion.weight_ref = bf16[2,8,8,128,128]{4,3,2,1,0:T(8,128)(2,1)} fusion(bf16[2,8,8,128,128]{4,3,2,1,0:T(8,128)(2,1)} %collective-permute-done.6, bf16[2,32,8,128,128]{4,3,2,1,0:T(8,128)(2,1)} %param.7, s32[]{:T(128)S(6)} %select_n.427, pred[]{:T(512)S(6)} %eq.95), kind=kLoop, calls=%fused_computation | loop fusion | flops 2097152 | bytes 12582917 | tf_op jit(solution)/shard_map/jit(_where)/select_n | solution.py:214
  185.4 5.0 %collective-permute-start.9 = (bf16[2,512,256]{2,1,0:T(8,128)(2,1)S(1)}, bf16[2,512,256]{2,1,0:T(8,128)(2,1)S(1)}, u32[]{:S(2)}, u32[]{:S(2)}) collective-permute-start(bf16[2,512,256]{2,1,0:T(8,128)(2,1)S(1)} %get-tuple-element.17), channel_id=1, source_target_pairs={{0,1},{1,8},{2,3},{3,10},{4,5},{5,12},{6,7},{7,14},{8,9},{9,16},{1... | collective-permute-start | bytes 1572872 | tf_op jit(solution)/shard_map/ppermute | solution.py:173
  190.4 2.4 collective-permute-start.4
  195.1 1.3 pad_maximum_fusion.2.ket_ref
  196.4 1.6 collective-permute-start.30
  198.1 1.8 collective-permute-start.31
  200.2 8.6 %collective-permute-done.29.refs_22_ = bf16[1024,256]{1,0:T(8,128)(2,1)S(1)} collective-permute-done((bf16[1024,256]{1,0:T(8,128)(2,1)S(1)}, bf16[1024,256]{1,0:T(8,128)(2,1)S(1)}, u32[]{:S(2)}, u32[]{:S(2)}) %collective-permute-start.29) | collective-permute-done | bytes 524320 | tf_op jit(solution)/shard_map/ppermute | solution.py:173
  209.2 1.8 collective-permute-start.35
  211.0 7.9 %ket_images.7 = bf16[2,2,1024,256]{3,2,1,0:T(8,128)(2,1)S(1)} custom-call(s32[8,8]{1,0:T(8,128)S(1)} %get-tuple-element.35.columns, f32[2,8,8]{2,1,0:T(8,128)S(1)} %get-tuple-element.39.cosine, f32[2,8,8]{2,1,0:T(8,128)S(1)} %get-tuple-element.38.sine, bf16[2,2048,256]{2,1,0:T(8,128)(2,1)S(1)} %pad_maximum_fusion.3.ket_ref, ...), custom_call_target="tpu_custom_call" | custom-call | flops 2147483648 | bytes 8388608 | tf_op jit(solution)/shard_map/ket_images/pallas_call | solution.py:62
  218.9 1.4 copy-done
  220.3 7.9 %ket_images.6 = bf16[2,2,1024,256]{3,2,1,0:T(8,128)(2,1)S(1)} custom-call(s32[8,8]{1,0:T(8,128)S(1)} %get-tuple-element.35.columns, f32[2,8,8]{2,1,0:T(8,128)S(1)} %get-tuple-element.50.cosine, f32[2,8,8]{2,1,0:T(8,128)S(1)} %get-tuple-element.51.sine, bf16[2,2048,256]{2,1,0:T(8,128)(2,1)S(1)} %pad_maximum_fusion.2.ket_ref, ...), custom_call_target="tpu_custom_call" | custom-call | flops 2147483648 | bytes 8388608 | tf_op jit(solution)/shard_map/ket_images/pallas_call | solution.py:62
  229.7 13.0 %collective-permute-done.35.refs_30_ = bf16[1024,256]{1,0:T(8,128)(2,1)} collective-permute-done((bf16[1024,256]{1,0:T(8,128)(2,1)}, bf16[1024,256]{1,0:T(8,128)(2,1)}, u32[]{:S(2)}, u32[]{:S(2)}) %collective-permute-start.35) | collective-permute-done | bytes 524320 | tf_op jit(solution)/shard_map/ppermute | solution.py:173
  242.9 1.7 collective-permute-start.33
  245.4 1.6 collective-permute-start.40
  247.0 7.9 %ket_images.5 = bf16[2,2,1024,256]{3,2,1,0:T(8,128)(2,1)S(1)} custom-call(s32[8,8]{1,0:T(8,128)S(1)} %get-tuple-element.35.columns, f32[2,8,8]{2,1,0:T(8,128)S(1)} %get-tuple-element.48.cosine, f32[2,8,8]{2,1,0:T(8,128)S(1)} %get-tuple-element.49.sine, bf16[2,2048,256]{2,1,0:T(8,128)(2,1)S(1)} %pad_maximum_fusion.1.ket_ref, ...), custom_call_target="tpu_custom_call" | custom-call | flops 2147483648 | bytes 8388608 | tf_op jit(solution)/shard_map/ket_images/pallas_call | solution.py:62
  256.3 7.9 %ket_images.4 = bf16[2,2,1024,256]{3,2,1,0:T(8,128)(2,1)S(1)} custom-call(s32[8,8]{1,0:T(8,128)S(1)} %get-tuple-element.35.columns, f32[2,8,8]{2,1,0:T(8,128)S(1)} %get-tuple-element.46.cosine, f32[2,8,8]{2,1,0:T(8,128)S(1)} %get-tuple-element.47.sine, bf16[2,2048,256]{2,1,0:T(8,128)(2,1)S(1)} %pad_maximum_fusion.ket_ref, ...), custom_call_target="tpu_custom_call" | custom-call | flops 2147483648 | bytes 8388608 | tf_op jit(solution)/shard_map/ket_images/pallas_call | solution.py:62
  265.5 3.3 %collective-permute-done.33.refs_26_ = bf16[1024,256]{1,0:T(8,128)(2,1)S(1)} collective-permute-done((bf16[1024,256]{1,0:T(8,128)(2,1)S(1)}, bf16[1024,256]{1,0:T(8,128)(2,1)S(1)}, u32[]{:S(2)}, u32[]{:S(2)}) %collective-permute-start.33) | collective-permute-done | bytes 524320 | tf_op jit(solution)/shard_map/ppermute | solution.py:173
  268.9 10.4 %collective-permute-done.39.refs_34_ = bf16[1024,256]{1,0:T(8,128)(2,1)S(1)} collective-permute-done((bf16[1024,256]{1,0:T(8,128)(2,1)}, bf16[1024,256]{1,0:T(8,128)(2,1)S(1)}, u32[]{:S(2)}, u32[]{:S(2)}) %collective-permute-start.39) | collective-permute-done | bytes 524320 | tf_op jit(solution)/shard_map/ppermute | solution.py:173
  280.3 11.3 %products.1 = f32[2,16,2,64,128]{4,3,2,1,0:T(8,128)} custom-call(s32[16]{0:T(128)S(1)} %pad_add_fusion.choice, bf16[4,1024,256]{2,1,0:T(8,128)(2,1)} %bitcast.84, bf16[4,1024,256]{2,1,0:T(8,128)(2,1)} %bitcast.83, bf16[4,1024,256]{2,1,0:T(8,128)(2,1)} %bitcast.82, bf16[4,1024,256]{2,1,0:T(8,128)(2,1)} %bitcast.81, ...), custom_call_target="tpu_custom_call" | custom-call | flops 2147483648 | bytes 16777216 | tf_op jit(solution)/shard_map/products/pallas_call | solution.py:130
  293.0 2.6 collective-permute-done.41
  295.6 1.4 bitcast_add_fusion
  297.4 2.3 collective-permute-start.43
  299.7 1.9 collective-permute-start.44
  301.6 9.6 %collective-permute-done.42 = f32[2,2,2,64,128]{4,3,2,1,0:T(8,128)S(1)} collective-permute-done((f32[2,2,2,64,128]{4,3,2,1,0:T(8,128)S(1)}, f32[2,2,2,64,128]{4,3,2,1,0:T(8,128)S(1)}, u32[]{:S(2)}, u32[]{:S(2)}) %collective-permute-start.42) | collective-permute-done | bytes 262176 | tf_op jit(solution)/shard_map/ppermute | solution.py:173
  311.2 7.6 %collective-permute-done.43 = f32[2,2,2,64,128]{4,3,2,1,0:T(8,128)S(1)} collective-permute-done((f32[2,2,2,64,128]{4,3,2,1,0:T(8,128)S(1)}, f32[2,2,2,64,128]{4,3,2,1,0:T(8,128)S(1)}, u32[]{:S(2)}, u32[]{:S(2)}) %collective-permute-start.43) | collective-permute-done | bytes 262176 | tf_op jit(solution)/shard_map/ppermute | solution.py:173
  (155 shorter events, 25.7 us)
Async XLA Ops:
  3.0 5.4 %collective-permute-start.1 = (bf16[2,2,1024,256]{3,2,0,1:T(8,128)(2,1)}, bf16[2,2,1024,256]{3,2,0,1:T(8,128)(2,1)S(1)}, u32[]{:S(2)}, u32[]{:S(2)}) collective-permute-start(bf16[2,2,1024,256]{3,2,0,1:T(8,128)(2,1)} %copy_bitcast_fusion), channel_id=1, source_target_pairs={{0,1},{1,0},{2,3},{3,2},{4,5},{5,4},{6,7},{7,6},{8,9},{9,8},{10,11... | collective-permute-start | bytes 6291464 | tf_op jit(solution)/shard_map/ppermute | solution.py:173
  8.3 170.1 %collective-permute-start.6 = (bf16[2,8,8,128,128]{4,3,2,1,0:T(8,128)(2,1)}, bf16[2,8,8,128,128]{4,3,2,1,0:T(8,128)(2,1)}, u32[]{:S(2)}, u32[]{:S(2)}) collective-permute-start(bf16[2,8,8,128,128]{4,3,2,1,0:T(8,128)(2,1)} %constant_dynamic-slice_fusion), channel_id=1, source_target_pairs={{0,1},{1,0},{2,3},{3,2},{4,5},{5,4},{6,7},{7,6},{8,9},{9,8},{10,11... | collective-permute-start | bytes 12582920 | tf_op jit(solution)/shard_map/ppermute | solution.py:173
  10.7 26.6 %collective-permute-start.2 = (bf16[2,1024,256]{2,1,0:T(8,128)(2,1)}, bf16[2,1024,256]{2,1,0:T(8,128)(2,1)S(1)}, u32[]{:S(2)}, u32[]{:S(2)}) collective-permute-start(bf16[2,1024,256]{2,1,0:T(8,128)(2,1)} %bitcast_select_fusion.3), channel_id=1, source_target_pairs={{0,8},{1,9},{2,10},{3,11},{4,12},{5,13},{6,14},{7,15},{8,0},{9,1},... | collective-permute-start | bytes 3145736 | tf_op jit(solution)/shard_map/ppermute | solution.py:173
  13.8 29.5 %collective-permute-start.14 = (s32[2]{0:T(128)S(1)}, s32[2]{0:T(128)S(1)}, u32[]{:S(2)}, u32[]{:S(2)}) collective-permute-start(s32[2]{0:T(128)S(1)} %copy-done.33), channel_id=1, source_target_pairs={{0,24},{1,25},{2,26},{3,27},{4,28},{5,29},{6,30},{7,31},{8,16},{9,... | collective-permute-start | bytes 32 | tf_op jit(solution)/shard_map/ppermute | solution.py:173
  16.2 28.6 %collective-permute-start.11 = (s32[2]{0:T(128)S(1)}, s32[2]{0:T(128)S(1)}, u32[]{:S(2)}, u32[]{:S(2)}) collective-permute-start(s32[2]{0:T(128)S(1)} %copy-done.33), channel_id=1, source_target_pairs={{0,16},{1,17},{2,18},{3,19},{4,20},{5,21},{6,22},{7,23},{8,24},{9,... | collective-permute-start | bytes 32 | tf_op jit(solution)/shard_map/ppermute | solution.py:173
  16.5 35.4 %collective-permute-start = (s32[4,8,8]{2,1,0:T(8,128)S(1)}, s32[4,8,8]{2,1,0:T(8,128)S(1)}, u32[]{:S(2)}, u32[]{:S(2)}) collective-permute-start(s32[4,8,8]{2,1,0:T(8,128)S(1)} %copy.29), channel_id=1, source_target_pairs={{0,1},{1,0},{2,3},{3,2},{4,5},{5,4},{6,7},{7,6},{8,9},{9,8},{10,11... | collective-permute-start | bytes 3080 | tf_op jit(solution)/shard_map/ppermute | solution.py:173
  41.5 13.3 %collective-permute-start.17 = (bf16[1024,256]{1,0:T(8,128)(2,1)S(1)}, bf16[1024,256]{1,0:T(8,128)(2,1)S(1)}, u32[]{:S(2)}, u32[]{:S(2)}) collective-permute-start(bf16[1024,256]{1,0:T(8,128)(2,1)S(1)} %get-tuple-element.31.refs_4_), channel_id=1, source_target_pairs={{0,2},{1,3},{2,0},{3,1},{4,6},{5,7},{6,4},{7,5},{8,10},{9,11},{10,... | collective-permute-start | bytes 1572872 | tf_op jit(solution)/shard_map/ppermute | solution.py:173
  43.3 12.9 %collective-permute-start.20 = (bf16[1024,256]{1,0:T(8,128)(2,1)S(1)}, bf16[1024,256]{1,0:T(8,128)(2,1)S(1)}, u32[]{:S(2)}, u32[]{:S(2)}) collective-permute-start(bf16[1024,256]{1,0:T(8,128)(2,1)S(1)} %get-tuple-element.30.refs_5_), channel_id=1, source_target_pairs={{0,4},{1,5},{2,6},{3,7},{4,0},{5,1},{6,2},{7,3},{8,12},{9,13},{10,... | collective-permute-start | bytes 1572872 | tf_op jit(solution)/shard_map/ppermute | solution.py:173
  44.8 3.6 %collective-permute-start.7 = (s32[2]{0:T(128)S(1)}, s32[2]{0:T(128)S(1)}, u32[]{:S(2)}, u32[]{:S(2)}) collective-permute-start(s32[2]{0:T(128)S(1)} %copy-done.33), channel_id=1, source_target_pairs={{0,8},{1,9},{2,10},{3,11},{4,12},{5,13},{6,14},{7,15},{8,0},{9,1},... | collective-permute-start | bytes 32 | tf_op jit(solution)/shard_map/ppermute | solution.py:173
  48.4 27.9 %collective-permute-start.3 = (bf16[2,1024,256]{2,1,0:T(8,128)(2,1)S(1)}, bf16[2,1024,256]{2,1,0:T(8,128)(2,1)S(1)}, u32[]{:S(2)}, u32[]{:S(2)}) collective-permute-start(bf16[2,1024,256]{2,1,0:T(8,128)(2,1)S(1)} %get-tuple-element.7), channel_id=1, source_target_pairs={{0,24},{1,25},{2,26},{3,27},{4,28},{5,29},{6,30},{7,31},{8,16},{9,... | collective-permute-start | bytes 3145736 | tf_op jit(solution)/shard_map/ppermute | solution.py:173
  52.0 87.7 %collective-permute-start.8 = (bf16[2,1024,256]{2,1,0:T(8,128)(2,1)S(1)}, bf16[2,1024,256]{2,1,0:T(8,128)(2,1)S(1)}, u32[]{:S(2)}, u32[]{:S(2)}) collective-permute-start(bf16[2,1024,256]{2,1,0:T(8,128)(2,1)S(1)} %get-tuple-element.5), channel_id=1, source_target_pairs={{0,16},{1,17},{2,18},{3,19},{4,20},{5,21},{6,22},{7,23},{8,24},{9,... | collective-permute-start | bytes 3145736 | tf_op jit(solution)/shard_map/ppermute | solution.py:173
  54.8 12.3 %collective-permute-start.18 = (bf16[1024,256]{1,0:T(8,128)(2,1)S(1)}, bf16[1024,256]{1,0:T(8,128)(2,1)S(1)}, u32[]{:S(2)}, u32[]{:S(2)}) collective-permute-start(bf16[1024,256]{1,0:T(8,128)(2,1)S(1)} %get-tuple-element.30.refs_5_), channel_id=1, source_target_pairs={{0,2},{1,3},{2,0},{3,1},{4,6},{5,7},{6,4},{7,5},{8,10},{9,11},{10,... | collective-permute-start | bytes 1572872 | tf_op jit(solution)/shard_map/ppermute | solution.py:173
  56.2 12.2 %collective-permute-start.19 = (bf16[1024,256]{1,0:T(8,128)(2,1)S(1)}, bf16[1024,256]{1,0:T(8,128)(2,1)S(1)}, u32[]{:S(2)}, u32[]{:S(2)}) collective-permute-start(bf16[1024,256]{1,0:T(8,128)(2,1)S(1)} %get-tuple-element.31.refs_4_), channel_id=1, source_target_pairs={{0,4},{1,5},{2,6},{3,7},{4,0},{5,1},{6,2},{7,3},{8,12},{9,13},{10,... | collective-permute-start | bytes 1572872 | tf_op jit(solution)/shard_map/ppermute | solution.py:173
  67.1 75.1 %collective-permute-start.26 = (bf16[1024,256]{1,0:T(8,128)(2,1)S(1)}, bf16[1024,256]{1,0:T(8,128)(2,1)S(1)}, u32[]{:S(2)}, u32[]{:S(2)}) collective-permute-start(bf16[1024,256]{1,0:T(8,128)(2,1)S(1)} %get-tuple-element.28.refs_13_), channel_id=1, source_target_pairs={{0,4},{1,5},{2,6},{3,7},{4,0},{5,1},{6,2},{7,3},{8,12},{9,13},{10,... | collective-permute-start | bytes 1572872 | tf_op jit(solution)/shard_map/ppermute | solution.py:173
  68.4 74.1 %collective-permute-start.24 = (bf16[1024,256]{1,0:T(8,128)(2,1)S(1)}, bf16[1024,256]{1,0:T(8,128)(2,1)S(1)}, u32[]{:S(2)}, u32[]{:S(2)}) collective-permute-start(bf16[1024,256]{1,0:T(8,128)(2,1)S(1)} %get-tuple-element.28.refs_13_), channel_id=1, source_target_pairs={{0,2},{1,3},{2,0},{3,1},{4,6},{5,7},{6,4},{7,5},{8,10},{9,11},{10,... | collective-permute-start | bytes 1572872 | tf_op jit(solution)/shard_map/ppermute | solution.py:173
  76.4 64.0 %collective-permute-start.23 = (bf16[1024,256]{1,0:T(8,128)(2,1)S(1)}, bf16[1024,256]{1,0:T(8,128)(2,1)S(1)}, u32[]{:S(2)}, u32[]{:S(2)}) collective-permute-start(bf16[1024,256]{1,0:T(8,128)(2,1)S(1)} %get-tuple-element.29.refs_12_), channel_id=1, source_target_pairs={{0,2},{1,3},{2,0},{3,1},{4,6},{5,7},{6,4},{7,5},{8,10},{9,11},{10,... | collective-permute-start | bytes 1572872 | tf_op jit(solution)/shard_map/ppermute | solution.py:173
  139.6 14.9 %collective-permute-start.25 = (bf16[1024,256]{1,0:T(8,128)(2,1)S(1)}, bf16[1024,256]{1,0:T(8,128)(2,1)S(1)}, u32[]{:S(2)}, u32[]{:S(2)}) collective-permute-start(bf16[1024,256]{1,0:T(8,128)(2,1)S(1)} %get-tuple-element.29.refs_12_), channel_id=1, source_target_pairs={{0,4},{1,5},{2,6},{3,7},{4,0},{5,1},{6,2},{7,3},{8,12},{9,13},{10,... | collective-permute-start | bytes 1572872 | tf_op jit(solution)/shard_map/ppermute | solution.py:173
  140.4 25.4 %collective-permute-start.21 = (bf16[1024,256]{1,0:T(8,128)(2,1)S(1)}, bf16[1024,256]{1,0:T(8,128)(2,1)S(1)}, u32[]{:S(2)}, u32[]{:S(2)}) collective-permute-start(bf16[1024,256]{1,0:T(8,128)(2,1)S(1)} %collective-permute-done.17.refs_6_), channel_id=1, source_target_pairs={{0,4},{1,5},{2,6},{3,7},{4,0},{5,1},{6,2},{7,3},{8,12},{9,13},{10,... | collective-permute-start | bytes 1572872 | tf_op jit(solution)/shard_map/ppermute | solution.py:173
  142.2 24.8 %collective-permute-start.22 = (bf16[1024,256]{1,0:T(8,128)(2,1)S(1)}, bf16[1024,256]{1,0:T(8,128)(2,1)S(1)}, u32[]{:S(2)}, u32[]{:S(2)}) collective-permute-start(bf16[1024,256]{1,0:T(8,128)(2,1)S(1)} %collective-permute-done.20.refs_9_), channel_id=1, source_target_pairs={{0,2},{1,3},{2,0},{3,1},{4,6},{5,7},{6,4},{7,5},{8,10},{9,11},{10,... | collective-permute-start | bytes 1572872 | tf_op jit(solution)/shard_map/ppermute | solution.py:173
  142.5 32.5 %collective-permute-start.27 = (bf16[1024,256]{1,0:T(8,128)(2,1)S(1)}, bf16[1024,256]{1,0:T(8,128)(2,1)S(1)}, u32[]{:S(2)}, u32[]{:S(2)}) collective-permute-start(bf16[1024,256]{1,0:T(8,128)(2,1)S(1)} %collective-permute-done.23.refs_14_), channel_id=1, source_target_pairs={{0,4},{1,5},{2,6},{3,7},{4,0},{5,1},{6,2},{7,3},{8,12},{9,13},{10,... | collective-permute-start | bytes 1572872 | tf_op jit(solution)/shard_map/ppermute | solution.py:173
  154.5 22.6 %collective-permute-start.28 = (bf16[1024,256]{1,0:T(8,128)(2,1)S(1)}, bf16[1024,256]{1,0:T(8,128)(2,1)S(1)}, u32[]{:S(2)}, u32[]{:S(2)}) collective-permute-start(bf16[1024,256]{1,0:T(8,128)(2,1)S(1)} %collective-permute-done.26.refs_17_), channel_id=1, source_target_pairs={{0,2},{1,3},{2,0},{3,1},{4,6},{5,7},{6,4},{7,5},{8,10},{9,11},{10,... | collective-permute-start | bytes 1572872 | tf_op jit(solution)/shard_map/ppermute | solution.py:173
  154.8 41.6 %copy-start.4 = (bf16[1024,256]{1,0:T(8,128)(2,1)}, bf16[1024,256]{1,0:T(8,128)(2,1)S(1)}, u32[]{:S(2)}) copy-start(bf16[1024,256]{1,0:T(8,128)(2,1)S(1)} %get-tuple-element.26.refs_21_) | copy-start | bytes 1572868
  154.8 43.3 %copy-start.5 = (bf16[1024,256]{1,0:T(8,128)(2,1)}, bf16[1024,256]{1,0:T(8,128)(2,1)S(1)}, u32[]{:S(2)}) copy-start(bf16[1024,256]{1,0:T(8,128)(2,1)S(1)} %get-tuple-element.27.refs_20_) | copy-start | bytes 1572868
  165.7 19.7 %collective-permute-start.15 = (bf16[2,512,256]{2,1,0:T(8,128)(2,1)S(1)}, bf16[2,512,256]{2,1,0:T(8,128)(2,1)S(1)}, u32[]{:S(2)}, u32[]{:S(2)}) collective-permute-start(bf16[2,512,256]{2,1,0:T(8,128)(2,1)S(1)} %get-tuple-element.8), channel_id=1, source_target_pairs={{0,1},{1,8},{2,3},{3,10},{4,5},{5,12},{6,7},{7,14},{8,9},{9,16},{1... | collective-permute-start | bytes 1572872 | tf_op jit(solution)/shard_map/ppermute | solution.py:173
  167.0 23.3 %collective-permute-start.16 = (bf16[2,512,256]{2,1,0:T(8,128)(2,1)S(1)}, bf16[2,512,256]{2,1,0:T(8,128)(2,1)S(1)}, u32[]{:S(2)}, u32[]{:S(2)}) collective-permute-start(bf16[2,512,256]{2,1,0:T(8,128)(2,1)S(1)} %get-tuple-element.9), channel_id=1, source_target_pairs={{1,0},{3,2},{5,4},{7,6},{8,1},{9,8},{10,3},{11,10},{12,5},{13,12},... | collective-permute-start | bytes 1572872 | tf_op jit(solution)/shard_map/ppermute | solution.py:173
  175.0 17.8 %collective-permute-start.12 = (bf16[2,512,256]{2,1,0:T(8,128)(2,1)S(1)}, bf16[2,512,256]{2,1,0:T(8,128)(2,1)}, u32[]{:S(2)}, u32[]{:S(2)}) collective-permute-start(bf16[2,512,256]{2,1,0:T(8,128)(2,1)S(1)} %get-tuple-element.10), channel_id=1, source_target_pairs={{0,1},{1,8},{2,3},{3,10},{4,5},{5,12},{6,7},{7,14},{8,9},{9,16},{1... | collective-permute-start | bytes 1572872 | tf_op jit(solution)/shard_map/ppermute | solution.py:173
  177.1 17.0 %collective-permute-start.13 = (bf16[2,512,256]{2,1,0:T(8,128)(2,1)S(1)}, bf16[2,512,256]{2,1,0:T(8,128)(2,1)S(1)}, u32[]{:S(2)}, u32[]{:S(2)}) collective-permute-start(bf16[2,512,256]{2,1,0:T(8,128)(2,1)S(1)} %get-tuple-element.11), channel_id=1, source_target_pairs={{1,0},{3,2},{5,4},{7,6},{8,1},{9,8},{10,3},{11,10},{12,5},{13,12},... | collective-permute-start | bytes 1572872 | tf_op jit(solution)/shard_map/ppermute | solution.py:173
  178.4 16.0 %collective-permute-start.10 = (bf16[2,512,256]{2,1,0:T(8,128)(2,1)S(1)}, bf16[2,512,256]{2,1,0:T(8,128)(2,1)S(1)}, u32[]{:S(2)}, u32[]{:S(2)}) collective-permute-start(bf16[2,512,256]{2,1,0:T(8,128)(2,1)S(1)} %get-tuple-element.16), channel_id=1, source_target_pairs={{1,0},{3,2},{5,4},{7,6},{8,1},{9,8},{10,3},{11,10},{12,5},{13,12},... | collective-permute-start | bytes 1572872 | tf_op jit(solution)/shard_map/ppermute | solution.py:173
  180.6 28.2 %copy-start.6 = (bf16[1024,256]{1,0:T(8,128)(2,1)}, bf16[1024,256]{1,0:T(8,128)(2,1)S(1)}, u32[]{:S(2)}) copy-start(bf16[1024,256]{1,0:T(8,128)(2,1)S(1)} %get-tuple-element.24.refs_29_) | copy-start | bytes 1572868
  185.4 11.0 %collective-permute-start.9 = (bf16[2,512,256]{2,1,0:T(8,128)(2,1)S(1)}, bf16[2,512,256]{2,1,0:T(8,128)(2,1)S(1)}, u32[]{:S(2)}, u32[]{:S(2)}) collective-permute-start(bf16[2,512,256]{2,1,0:T(8,128)(2,1)S(1)} %get-tuple-element.17), channel_id=1, source_target_pairs={{0,1},{1,8},{2,3},{3,10},{4,5},{5,12},{6,7},{7,14},{8,9},{9,16},{1... | collective-permute-start | bytes 1572872 | tf_op jit(solution)/shard_map/ppermute | solution.py:173
  190.4 7.7 %collective-permute-start.4 = (bf16[2,512,256]{2,1,0:T(8,128)(2,1)S(1)}, bf16[2,512,256]{2,1,0:T(8,128)(2,1)S(1)}, u32[]{:S(2)}, u32[]{:S(2)}) collective-permute-start(bf16[2,512,256]{2,1,0:T(8,128)(2,1)S(1)} %get-tuple-element.19), channel_id=1, source_target_pairs={{0,1},{1,8},{2,3},{3,10},{4,5},{5,12},{6,7},{7,14},{8,9},{9,16},{1... | collective-permute-start | bytes 1572872 | tf_op jit(solution)/shard_map/ppermute | solution.py:173
  192.8 7.1 %collective-permute-start.5 = (bf16[2,512,256]{2,1,0:T(8,128)(2,1)S(1)}, bf16[2,512,256]{2,1,0:T(8,128)(2,1)S(1)}, u32[]{:S(2)}, u32[]{:S(2)}) collective-permute-start(bf16[2,512,256]{2,1,0:T(8,128)(2,1)S(1)} %get-tuple-element.18), channel_id=1, source_target_pairs={{1,0},{3,2},{5,4},{7,6},{8,1},{9,8},{10,3},{11,10},{12,5},{13,12},... | collective-permute-start | bytes 1572872 | tf_op jit(solution)/shard_map/ppermute | solution.py:173
  194.1 14.7 %collective-permute-start.29 = (bf16[1024,256]{1,0:T(8,128)(2,1)S(1)}, bf16[1024,256]{1,0:T(8,128)(2,1)S(1)}, u32[]{:S(2)}, u32[]{:S(2)}) collective-permute-start(bf16[1024,256]{1,0:T(8,128)(2,1)S(1)} %get-tuple-element.27.refs_20_), channel_id=1, source_target_pairs={{0,2},{1,3},{2,0},{3,1},{4,6},{5,7},{6,4},{7,5},{8,10},{9,11},{10,... | collective-permute-start | bytes 1572872 | tf_op jit(solution)/shard_map/ppermute | solution.py:173
  194.4 14.8 %collective-permute-start.32 = (bf16[1024,256]{1,0:T(8,128)(2,1)S(1)}, bf16[1024,256]{1,0:T(8,128)(2,1)S(1)}, u32[]{:S(2)}, u32[]{:S(2)}) collective-permute-start(bf16[1024,256]{1,0:T(8,128)(2,1)S(1)} %get-tuple-element.26.refs_21_), channel_id=1, source_target_pairs={{0,4},{1,5},{2,6},{3,7},{4,0},{5,1},{6,2},{7,3},{8,12},{9,13},{10,... | collective-permute-start | bytes 1572872 | tf_op jit(solution)/shard_map/ppermute | solution.py:173
  196.4 48.2 %collective-permute-start.30 = (bf16[1024,256]{1,0:T(8,128)(2,1)S(1)}, bf16[1024,256]{1,0:T(8,128)(2,1)}, u32[]{:S(2)}, u32[]{:S(2)}) collective-permute-start(bf16[1024,256]{1,0:T(8,128)(2,1)S(1)} %get-tuple-element.26.refs_21_), channel_id=1, source_target_pairs={{0,2},{1,3},{2,0},{3,1},{4,6},{5,7},{6,4},{7,5},{8,10},{9,11},{10,... | collective-permute-start | bytes 1572872 | tf_op jit(solution)/shard_map/ppermute | solution.py:173
  198.1 46.8 %collective-permute-start.31 = (bf16[1024,256]{1,0:T(8,128)(2,1)S(1)}, bf16[1024,256]{1,0:T(8,128)(2,1)}, u32[]{:S(2)}, u32[]{:S(2)}) collective-permute-start(bf16[1024,256]{1,0:T(8,128)(2,1)S(1)} %get-tuple-element.27.refs_20_), channel_id=1, source_target_pairs={{0,4},{1,5},{2,6},{3,7},{4,0},{5,1},{6,2},{7,3},{8,12},{9,13},{10,... | collective-permute-start | bytes 1572872 | tf_op jit(solution)/shard_map/ppermute | solution.py:173
  199.9 43.0 %collective-permute-start.38 = (bf16[1024,256]{1,0:T(8,128)(2,1)S(1)}, bf16[1024,256]{1,0:T(8,128)(2,1)}, u32[]{:S(2)}, u32[]{:S(2)}) collective-permute-start(bf16[1024,256]{1,0:T(8,128)(2,1)S(1)} %get-tuple-element.24.refs_29_), channel_id=1, source_target_pairs={{0,4},{1,5},{2,6},{3,7},{4,0},{5,1},{6,2},{7,3},{8,12},{9,13},{10,... | collective-permute-start | bytes 1572872 | tf_op jit(solution)/shard_map/ppermute | solution.py:173
  208.8 36.6 %collective-permute-start.36 = (bf16[1024,256]{1,0:T(8,128)(2,1)S(1)}, bf16[1024,256]{1,0:T(8,128)(2,1)}, u32[]{:S(2)}, u32[]{:S(2)}) collective-permute-start(bf16[1024,256]{1,0:T(8,128)(2,1)S(1)} %get-tuple-element.24.refs_29_), channel_id=1, source_target_pairs={{0,2},{1,3},{2,0},{3,1},{4,6},{5,7},{6,4},{7,5},{8,10},{9,11},{10,... | collective-permute-start | bytes 1572872 | tf_op jit(solution)/shard_map/ppermute | solution.py:173
  209.2 33.4 %collective-permute-start.35 = (bf16[1024,256]{1,0:T(8,128)(2,1)}, bf16[1024,256]{1,0:T(8,128)(2,1)}, u32[]{:S(2)}, u32[]{:S(2)}) collective-permute-start(bf16[1024,256]{1,0:T(8,128)(2,1)} %get-tuple-element.25.refs_28_), channel_id=1, source_target_pairs={{0,2},{1,3},{2,0},{3,1},{4,6},{5,7},{6,4},{7,5},{8,10},{9,11},{10,... | collective-permute-start | bytes 1572872 | tf_op jit(solution)/shard_map/ppermute | solution.py:173
  242.6 22.9 %collective-permute-start.37 = (bf16[1024,256]{1,0:T(8,128)(2,1)}, bf16[1024,256]{1,0:T(8,128)(2,1)S(1)}, u32[]{:S(2)}, u32[]{:S(2)}) collective-permute-start(bf16[1024,256]{1,0:T(8,128)(2,1)} %get-tuple-element.25.refs_28_), channel_id=1, source_target_pairs={{0,4},{1,5},{2,6},{3,7},{4,0},{5,1},{6,2},{7,3},{8,12},{9,13},{10,... | collective-permute-start | bytes 1572872 | tf_op jit(solution)/shard_map/ppermute | solution.py:173
  242.9 25.9 %collective-permute-start.33 = (bf16[1024,256]{1,0:T(8,128)(2,1)S(1)}, bf16[1024,256]{1,0:T(8,128)(2,1)S(1)}, u32[]{:S(2)}, u32[]{:S(2)}) collective-permute-start(bf16[1024,256]{1,0:T(8,128)(2,1)S(1)} %copy-done.13), channel_id=1, source_target_pairs={{0,4},{1,5},{2,6},{3,7},{4,0},{5,1},{6,2},{7,3},{8,12},{9,13},{10,... | collective-permute-start | bytes 1572872 | tf_op jit(solution)/shard_map/ppermute | solution.py:173
  244.7 24.2 %collective-permute-start.34 = (bf16[1024,256]{1,0:T(8,128)(2,1)S(1)}, bf16[1024,256]{1,0:T(8,128)(2,1)S(1)}, u32[]{:S(2)}, u32[]{:S(2)}) collective-permute-start(bf16[1024,256]{1,0:T(8,128)(2,1)S(1)} %copy-done.15), channel_id=1, source_target_pairs={{0,2},{1,3},{2,0},{3,1},{4,6},{5,7},{6,4},{7,5},{8,10},{9,11},{10,... | collective-permute-start | bytes 1572872 | tf_op jit(solution)/shard_map/ppermute | solution.py:173
  244.9 34.4 %collective-permute-start.39 = (bf16[1024,256]{1,0:T(8,128)(2,1)}, bf16[1024,256]{1,0:T(8,128)(2,1)S(1)}, u32[]{:S(2)}, u32[]{:S(2)}) collective-permute-start(bf16[1024,256]{1,0:T(8,128)(2,1)} %collective-permute-done.35.refs_30_), channel_id=1, source_target_pairs={{0,4},{1,5},{2,6},{3,7},{4,0},{5,1},{6,2},{7,3},{8,12},{9,13},{10,... | collective-permute-start | bytes 1572872 | tf_op jit(solution)/shard_map/ppermute | solution.py:173
  245.4 33.9 %collective-permute-start.40 = (bf16[1024,256]{1,0:T(8,128)(2,1)}, bf16[1024,256]{1,0:T(8,128)(2,1)S(1)}, u32[]{:S(2)}, u32[]{:S(2)}) collective-permute-start(bf16[1024,256]{1,0:T(8,128)(2,1)} %collective-permute-done.38.refs_33_), channel_id=1, source_target_pairs={{0,2},{1,3},{2,0},{3,1},{4,6},{5,7},{6,4},{7,5},{8,10},{9,11},{10,... | collective-permute-start | bytes 1572872 | tf_op jit(solution)/shard_map/ppermute | solution.py:173
  292.9 2.7 collective-permute-start.41
  297.2 14.0 %collective-permute-start.42 = (f32[2,2,2,64,128]{4,3,2,1,0:T(8,128)S(1)}, f32[2,2,2,64,128]{4,3,2,1,0:T(8,128)S(1)}, u32[]{:S(2)}, u32[]{:S(2)}) collective-permute-start(f32[2,2,2,64,128]{4,3,2,1,0:T(8,128)S(1)} %bitcast.91), channel_id=1, source_target_pairs={{0,8},{1,9},{2,10},{3,11},{4,12},{5,13},{6,14},{7,15},{8,0},{9,1},... | collective-permute-start | bytes 786440 | tf_op jit(solution)/shard_map/ppermute | solution.py:173
  297.4 21.3 %collective-permute-start.43 = (f32[2,2,2,64,128]{4,3,2,1,0:T(8,128)S(1)}, f32[2,2,2,64,128]{4,3,2,1,0:T(8,128)S(1)}, u32[]{:S(2)}, u32[]{:S(2)}) collective-permute-start(f32[2,2,2,64,128]{4,3,2,1,0:T(8,128)S(1)} %bitcast.90), channel_id=1, source_target_pairs={{0,16},{1,17},{2,18},{3,19},{4,20},{5,21},{6,22},{7,23},{8,24},{9,... | collective-permute-start | bytes 786440 | tf_op jit(solution)/shard_map/ppermute | solution.py:173
  299.7 19.1 %collective-permute-start.44 = (f32[2,2,2,64,128]{4,3,2,1,0:T(8,128)S(1)}, f32[2,2,2,64,128]{4,3,2,1,0:T(8,128)S(1)}, u32[]{:S(2)}, u32[]{:S(2)}) collective-permute-start(f32[2,2,2,64,128]{4,3,2,1,0:T(8,128)S(1)} %bitcast.89), channel_id=1, source_target_pairs={{0,24},{1,25},{2,26},{3,27},{4,28},{5,29},{6,30},{7,31},{8,16},{9,... | collective-permute-start | bytes 786440 | tf_op jit(solution)/shard_map/ppermute | solution.py:173
  (31 other events, 246.9 us)

commit v2 on v1

v2 whole, which is shorter than its diff:
```python
import functools
import math

import jax
import jax.numpy as jnp
from jax import lax
from jax.experimental import pallas as pl
from jax.experimental.pallas import tpu as pltpu
from jax.sharding import PartitionSpec as P

BLK = 128
HALO = 4
KGRID = 32
VMEM = 48 * 1024 * 1024


def phases(kpoints, images):
    first_coord = kpoints // (KGRID * KGRID)
    second_coord = kpoints // KGRID % KGRID
    third_coord = kpoints % KGRID
    turn_count = (
        first_coord[:, None, None] * images[0][None]
        + second_coord[:, None, None] * images[1][None]
        + third_coord[:, None, None] * images[2][None]
    ) % KGRID
    angles = turn_count.astype(jnp.float32) * (2.0 * math.pi / KGRID)
    return (jnp.cos(angles), jnp.sin(angles))


def image_kernel(core, columns, cosine, sine, outer_ref, ket_ref, inner_ref, weight_ref, out_ref, all_ref):
    block = pl.program_id(0)
    momenta, _, slots, size, _ = weight_ref.shape
    points, rows, width = ket_ref.shape
    reach = outer_ref.shape[2]
    bands = width // 2

    @pl.when(block == 0)
    def _():
        all_ref[:, reach : reach + rows] = ket_ref[...]
        outer_at = pl.multiple_of(core[0] * (reach + rows), size)
        inner_at = pl.multiple_of((1 - core[0]) * (reach + rows), size)
        all_ref[:, pl.ds(outer_at, reach)] = outer_ref[0]
        all_ref[:, pl.ds(inner_at, reach)] = inner_ref[0]

    weights = jnp.concatenate(
        [
            jnp.concatenate([weight_ref[q, 0, s] for s in range(slots)], axis=1)
            for q in range(momenta)
        ],
        axis=0,
    )
    for point in range(points):
        parts = []
        for s in range(slots):
            start = pl.multiple_of(columns[block, s] * size, size)
            real = all_ref[point, pl.ds(start, size), :bands].astype(jnp.float32)
            imag = all_ref[point, pl.ds(start, size), bands:].astype(jnp.float32)
            c, d = cosine[point, block, s], sine[point, block, s]
            turned = jnp.concatenate([c * real - d * imag, d * real + c * imag], axis=1)
            parts.append(turned.astype(jnp.bfloat16))
        image = jnp.dot(
            weights, jnp.concatenate(parts, axis=0), preferred_element_type=jnp.float32
        )
        for q in range(momenta):
            out_ref[point, q] = image[q * size : (q + 1) * size].astype(out_ref.dtype)


def ket_images(core, columns, cosine, sine, outer, kets, inner, weights):
    momenta, blocks, slots, size, _ = weights.shape
    points, rows, width = kets.shape
    reach = outer[0].shape[2]
    flops = 2 * points * momenta * blocks * slots * size * size * width

    def end(place):
        return pl.BlockSpec((1, points, reach, width), lambda i, *_: (place, 0, 0, 0))

    return pl.pallas_call(
        image_kernel,
        grid_spec=pltpu.PrefetchScalarGridSpec(
            num_scalar_prefetch=4,
            grid=(blocks,),
            in_specs=[
                end(outer[1]),
                pl.BlockSpec((points, rows, width), lambda i, *_: (0, 0, 0)),
                end(inner[1]),
                pl.BlockSpec((momenta, 1, slots, size, size), lambda i, *_: (0, i, 0, 0, 0)),
            ],
            out_specs=pl.BlockSpec((points, momenta, size, width), lambda i, *_: (0, 0, i, 0)),
            scratch_shapes=[pltpu.VMEM((points, rows + 2 * reach, width), jnp.bfloat16)],
        ),
        out_shape=jax.ShapeDtypeStruct((points, momenta, blocks * size, width), jnp.bfloat16),
        compiler_params=pltpu.CompilerParams(vmem_limit_bytes=VMEM),
        cost_estimate=pl.CostEstimate(
            flops=flops, bytes_accessed=weights.size * 2 + kets.size * 4, transcendentals=0
        ),
        name="ket_images",
    )(core, columns, cosine, sine, outer[0], kets, inner[0], weights)


def product_kernel(groups, places, choice, *refs):
    image_refs, bra_refs = refs[:groups], refs[groups:-5]
    out_ref, image_buf, bra_buf, image_sem, bra_sem = refs[-5:]
    pairs = choice.shape[0]
    per_group = pairs // groups
    halves, half = out_ref.shape[0], out_ref.shape[3]
    bands = halves * half

    @pl.loop(0, pairs)
    def _(pair):
        wanted = choice[pair]
        for number, (array, point) in enumerate(places):

            @pl.when(wanted == number)
            def _():
                source = bra_refs[array].at[point]
                pltpu.make_async_copy(source, bra_buf.at[pair], bra_sem.at[pair]).start()

    def image_copy(group):
        spot = pl.ds(group * per_group, per_group)
        return pltpu.make_async_copy(image_refs[group], image_buf.at[spot], image_sem.at[group])

    for group in range(groups):
        image_copy(group).start()
    for group in range(groups):
        image_copy(group).wait()

        @pl.loop(group * per_group, (group + 1) * per_group)
        def _(pair):
            pltpu.make_async_copy(bra_refs[0].at[0], bra_buf.at[pair], bra_sem.at[pair]).wait()
            value = lax.dot_general(
                bra_buf[pair],
                image_buf[pair],
                (((0,), (0,)), ((), ())),
                preferred_element_type=jnp.float32,
            )
            real = value[:bands, :bands] + value[bands:, bands:]
            imag = value[:bands, bands:] - value[bands:, :bands]
            for h in range(halves):
                out_ref[h, pair, 0] = real[h * half : (h + 1) * half]
                out_ref[h, pair, 1] = imag[h * half : (h + 1) * half]


def products(choice, images, bras, places, halves):
    groups = len(images)
    _, rows, width = bras[0].shape
    pairs = choice.shape[0]
    bands = width // 2
    images = [image.reshape(pairs // groups, rows, width) for image in images]
    return pl.pallas_call(
        functools.partial(product_kernel, groups, places),
        in_specs=[pl.BlockSpec(memory_space=pltpu.SMEM)]
        + [pl.BlockSpec(memory_space=pl.ANY)] * (groups + len(bras)),
        out_specs=pl.BlockSpec(memory_space=pltpu.VMEM),
        out_shape=jax.ShapeDtypeStruct((halves, pairs, 2, bands // halves, bands), jnp.float32),
        scratch_shapes=[
            pltpu.VMEM((pairs, rows, width), jnp.bfloat16),
            pltpu.VMEM((pairs, rows, width), jnp.bfloat16),
            pltpu.SemaphoreType.DMA((groups,)),
            pltpu.SemaphoreType.DMA((pairs,)),
        ],
        compiler_params=pltpu.CompilerParams(vmem_limit_bytes=VMEM),
        cost_estimate=pl.CostEstimate(
            flops=2 * pairs * rows * width * width,
            bytes_accessed=4 * pairs * rows * width,
            transcendentals=0,
        ),
        name="products",
    )(choice, *images, *bras)


def per_device(coeffs, perturbation, columns, images, kpoints, matching):
    n_ka, n_orb = lax.axis_size("ka"), lax.axis_size("orb")
    points, row_count, width = coeffs.shape
    block_count = row_count // BLK
    momenta = perturbation.shape[0]
    bits_of = lambda n: n.bit_length() - 1
    n_rows = min(n_ka, block_count // (2 * HALO))
    n_side = n_ka // n_rows
    blocks = block_count // n_rows
    rows = blocks * BLK
    me, core = lax.axis_index("ka"), lax.axis_index("orb")
    z, side = me // n_side, me % n_side

    def flat(zi, gi, ci):
        return (zi * n_side + gi) * n_orb + ci

    every = [(zi, gi, ci) for zi in range(n_rows) for gi in range(n_side) for ci in range(n_orb)]

    def send(x, to):
        moves = [(flat(*spot), to(*spot)) for spot in every]
        return lax.ppermute(x, ("ka", "orb"), [(a, flat(*b)) for a, b in moves if b is not None])

    def on_core(x, d):
        return send(x, lambda zi, gi, ci: (zi, gi, (ci + d) % n_orb))

    def across_rows(x, s):
        return send(x, lambda zi, gi, ci: (zi ^ s, gi, ci))

    def across_side(x, bit):
        return send(x, lambda zi, gi, ci: (zi, gi ^ (1 << bit), ci))

    def pick(x, index, axis):
        return lax.dynamic_index_in_dim(x, index, axis, keepdims=False)

    def after(x, *arrived):
        return lax.optimization_barrier((x, *arrived))[0] if arrived else x

    held = coeffs.reshape(points, n_rows, rows, width)

    def group_part(s, first, count, *arrived):
        target = z ^ s
        came = []
        source = after(held, *arrived)
        for ci in range(n_orb):
            part = pick(source[first : first + count], (n_orb * target + ci) % n_rows, 1)

            def to(zi, gi, cj, ci=ci):
                zt = zi ^ s
                return (zt, gi, ci) if (n_orb * zt + ci) // n_rows == cj else None

            came.append(send(part, to))
        return came

    def settle(came, *arrived):
        out = after(came[0], *arrived)
        for ci in range(1, n_orb):
            out = jnp.where(core == ci, came[ci], out)
        return out

    def own_group():
        source = (n_orb * z + core) // n_rows
        out = pick(held, (n_orb * z + core) % n_rows, 1)
        for d in range(1, n_orb):
            index = (n_orb * z + (core + d) % n_orb) % n_rows
            came = on_core(pick(held, index, 1), d)
            out = jnp.where((core - source) % n_orb == d, came, out)
        return out

    bits = list(range(bits_of(n_side)))

    def gather_side(group):
        near = [across_side(group, bit) for bit in bits]
        arrays = [group, *near]
        have, far = [], []
        for point in range(points):
            found = {0: (0, point), **{1 << bit: (1 + bit, point) for bit in bits}}
            for p in sorted(range(n_side), key=lambda n: n.bit_count()):
                if p not in found:
                    set_bits = [bit for bit in bits if p >> bit & 1]
                    bit = set_bits[-1 if point % 2 == 0 else 0]
                    array, place = found[p ^ (1 << bit)]
                    arrays.append(across_side(arrays[array][place : place + 1], bit))
                    far.append(arrays[-1])
                    found[p] = (len(arrays) - 1, 0)
            have.append(found)
        return arrays, have, near, far

    pieces = {}
    for s in range(1, n_rows):
        pieces[s] = group_part(s, 0, points, *([] if s < 3 else [pieces[s - 1][-1]]))
    groups, bras, places, near, far = [], [], [], [], []
    for s in range(n_rows):
        gates = (near[s - 1] if s > 0 else []) + (far[s - 2] if s > 1 else [])
        groups.append(settle(pieces[s], *gates) if s else own_group())
        arrays, have, came_near, came_far = gather_side(groups[s])
        for p in range(n_side):
            places += [(len(bras) + have[point][p][0], have[point][p][1]) for point in range(points)]
        bras += arrays
        near.append(came_near)
        far.append(came_far)

    def own_rows(x, axis, *arrived):
        def part(ci):
            index = (n_orb * z + ci) % n_rows
            return lax.dynamic_slice_in_dim(x, index * blocks, blocks, axis)

        x = after(x, *arrived)
        source = (n_orb * z + core) // n_rows
        out = part(core)
        for d in range(1, n_orb):
            came = on_core(part((core + d) % n_orb), d)
            out = jnp.where((core - source) % n_orb == d, came, out)
        return out

    weights = own_rows(perturbation, 1, *near[0])
    table = own_rows(jnp.concatenate([columns[None], images]), 1)
    local_columns = table[0] - (n_orb * z + core) * blocks + HALO
    reach = HALO * BLK
    lead = rows - reach

    def ends(members, start):
        return jnp.stack([lax.dynamic_slice_in_dim(x, start, reach, 1) for x in members])

    def outer_ends(wanted):
        step = jnp.where(core == 0, z ^ (z - 1), z ^ (z + 1))
        options = sorted({a ^ (a + 1) for a in range(n_rows - 1)})
        members = []
        for s in wanted:
            out = groups[s ^ options[0]]
            for x in options[1:]:
                out = jnp.where(step == x, groups[s ^ x], out)
            members.append(out)

        def to(zi, gi, ci):
            zt = zi + 2 * ci - 1
            return (zt, gi, 1 - ci) if 0 <= zt < n_rows else None

        return send(ends(members, core * lead), to)

    def inner_ends(wanted):
        return on_core(ends([groups[s] for s in wanted], (1 - core) * lead), 1)

    ket_list, choices = [None] * n_rows, []
    odd, even = list(range(1, n_rows, 2)), list(range(0, n_rows, 2))
    low, high = list(range(n_rows // 2)), list(range(n_rows // 2, n_rows))
    outer = {s: (x, i) for part in (odd, even) for x in [outer_ends(part)] for i, s in enumerate(part)}
    inner = {s: (x, i) for part in (low, high) for x in [inner_ends(part)] for i, s in enumerate(part)}
    for s in odd + even:
        k_here = kpoints if s == 0 else across_rows(kpoints, s)
        cosine, sine = phases(k_here, table[1:])
        ket_list[s] = ket_images(
            core[None], local_columns, cosine, sine, outer[s], groups[s], inner[s], weights
        )
    for s in range(n_rows):
        first = ((z ^ s) * n_side + side) * points
        found = lax.dynamic_slice_in_dim(matching, first, points, 1).T
        owner = found // points
        number = ((owner // n_side) ^ z) * n_side + ((owner % n_side) ^ side)
        choices.append((number * points + found % points).reshape(-1))

    value = products(jnp.concatenate(choices), ket_list, bras, places, n_orb)
    total = pick(value, core, 0)
    for d in range(1, n_orb):
        total = total + on_core(pick(value, (core + d) % n_orb, 0), d)
    total = total.reshape(n_rows, points, momenta, *total.shape[1:])
    out = total[0]
    for s in range(1, n_rows):
        out = out + across_rows(total[s], s)
    return out


def solution(mesh):
    in_specs = (
        P("ka", "orb", None),
        P(None, "orb", None, None, None),
        P("orb", None),
        P(None, "orb", None),
        P("ka"),
        P(),
    )
    out_specs = P("ka", None, None, "orb", None)
    return jax.shard_map(
        per_device, mesh=mesh, in_specs=in_specs, out_specs=out_specs, check_vma=False
    )
```

time: 324 us -> 271 us (0.84)
  waiting for transfers between devices: 187 us -> 130 us
  local copies, waits for them, and re-layouts: 18.3 us -> 27.2 us
    ppermute x45 -> x36, waiting for transfers between devices: 187 us -> 130 us  [send(): lax.ppermute(x, ('ka', 'orb'), [(a, flat(*b)) for a, b in moves if b is n...]
    slice x1 -> x8, local copies, waits for them, and re-layouts: 0.51 us -> 6.82 us  [gather_side(): arrays.append(across_side(arrays[array][place:place + 1], bit))]
    squeeze x2 -> x3, local copies, waits for them, and re-layouts: 4.37 us -> 6.97 us  [pick(): return lax.dynamic_index_in_dim(x, index, axis, keepdims=False)]
    ppermute x45 -> x36, starting transfers between devices: 54.6 us -> 53.6 us  [send(): lax.ppermute(x, ('ka', 'orb'), [(a, flat(*b)) for a, b in moves if b is n...]
    unnamed x70 -> x50, local copies, waits for them, and re-layouts: 6.72 us -> 7.53 us
  transfers between devices with their start and end apart: 45 -> 36, of which waited for: 18 -> 12; matrix products, arithmetic and copies ran while one was open for 6% -> 10% of each run, Pallas kernels for 10% -> 12%
where the time goes in v2:
time: 271 us; the launch traced here: 270 us
  waiting for transfers between devices  130 us (48%)
  starting transfers between devices  53.6 us (20%)
  Pallas kernels  43.3 us (16%)
  local copies, waits for them, and re-layouts  27.2 us (10%)
  other arithmetic  15.5 us (6%)
    ppermute x36, waiting for transfers between devices, send(): lax.ppermute(x, ('ka', 'orb'), [(a, flat(*b)) for a, b in moves if b is n...  130 us
    ppermute x36, starting transfers between devices, send(): lax.ppermute(x, ('ka', 'orb'), [(a, flat(*b)) for a, b in moves if b is n...  53.6 us
    pallas_call x4, Pallas kernels, ket_images(): pl.pallas_call(image_kernel, grid_spec=pltpu.PrefetchScalarGridSpec(num_s...  32 us
    pallas_call x1, Pallas kernels, products(): pl.pallas_call(functools.partial(product_kernel, groups, places), in_spec...  11.3 us
    unnamed x50, local copies, waits for them, and re-layouts  7.53 us
    squeeze x3, local copies, waits for them, and re-layouts, pick(): return lax.dynamic_index_in_dim(x, index, axis, keepdims=False)  6.97 us
    slice x8, local copies, waits for them, and re-layouts, gather_side(): arrays.append(across_side(arrays[array][place:place + 1], bit))  6.82 us
  transfers between devices with their start and end apart: 36, of which 12 were waited for; matrix products, arithmetic and copies ran while one was open for 10% of the time, Pallas kernels for 12%

profile of v2, /device:TPU:0, one launch (start us, length us, event | category | flops | bytes accessed | tf_op | source)
XLA Modules:
  0.0 269.6 jit_solution(3456952929720099852)
XLA Ops:
  0.0 4.5 %dynamic-slice_bitcast_fusion.4 = (bf16[2,1024,256]{2,1,0:T(8,128)(2,1)}, bf16[2,1024,256]{2,1,0:T(8,128)(2,1)S(1)}, bf16[2,1024,256]{2,1,0:T(8,128)(2,1)}, bf16...) fusion(bf16[2,4,1024,256]{3,2,1,0:T(8,128)(2,1)} %bitcast.87, s32[]{:T(128)S(6)} %select_n.382, s32[]{:T(128)S(6)} %select_n.388, ...), kind=kLoop, calls=%fused_computation.11 | loop fusion | bytes 10485780 | tf_op jit(solution)/shard_map/jit(dynamic_index_in_dim)/squeeze | solution.py:203
  5.0 4.5 %collective-permute-start.6 = (bf16[2,1024,256]{2,1,0:T(8,128)(2,1)}, bf16[2,1024,256]{2,1,0:T(8,128)(2,1)}, u32[]{:S(2)}, u32[]{:S(2)}) collective-permute-start(bf16[2,1024,256]{2,1,0:T(8,128)(2,1)} %get-tuple-element.17), channel_id=1, source_target_pairs={{0,8},{2,10},{4,12},{6,14},{8,0},{10,2},{12,4},{14,6},{17,24},{19,... | collective-permute-start | bytes 3145736 | tf_op jit(solution)/shard_map/ppermute | solution.py:191
  9.5 1.6 collective-permute-start.1
  11.1 1.3 bitcast_select_fusion.ket_ref.refs_4_
  12.4 1.6 collective-permute-start.8
  14.0 1.5 collective-permute-start.9
  15.5 6.2 %collective-permute-start.5 = (bf16[2,1024,256]{2,1,0:T(8,128)(2,1)}, bf16[2,1024,256]{2,1,0:T(8,128)(2,1)}, u32[]{:S(2)}, u32[]{:S(2)}) collective-permute-start(bf16[2,1024,256]{2,1,0:T(8,128)(2,1)} %get-tuple-element.18), channel_id=1, source_target_pairs={{0,9},{2,11},{4,13},{6,15},{8,1},{10,3},{12,5},{14,7},{17,25},{19,... | collective-permute-start | bytes 3145736 | tf_op jit(solution)/shard_map/ppermute | solution.py:191
  23.0 10.7 %collective-permute-done.6 = bf16[2,1024,256]{2,1,0:T(8,128)(2,1)} collective-permute-done((bf16[2,1024,256]{2,1,0:T(8,128)(2,1)}, bf16[2,1024,256]{2,1,0:T(8,128)(2,1)}, u32[]{:S(2)}, u32[]{:S(2)}) %collective-permute-start.6) | collective-permute-done | bytes 1048608 | tf_op jit(solution)/shard_map/ppermute | solution.py:191
  33.8 1.9 collective-permute-done.8.refs_5_
  35.6 1.8 collective-permute-done.9.refs_6_
  38.4 10.5 %collective-permute-done.5 = bf16[2,1024,256]{2,1,0:T(8,128)(2,1)} collective-permute-done((bf16[2,1024,256]{2,1,0:T(8,128)(2,1)}, bf16[2,1024,256]{2,1,0:T(8,128)(2,1)}, u32[]{:S(2)}, u32[]{:S(2)}) %collective-permute-start.5) | collective-permute-done | bytes 1048608 | tf_op jit(solution)/shard_map/ppermute | solution.py:191
  48.9 1.3 broadcast_select_fusion.2.ket_ref.refs_9_
  50.2 1.6 collective-permute-start.10
  51.8 1.5 collective-permute-start.11
  53.9 5.1 %constant_dynamic-slice_fusion = bf16[2,8,8,128,128]{4,3,2,1,0:T(8,128)(2,1)} fusion(bf16[2,32,8,128,128]{4,3,2,1,0:T(8,128)(2,1)} %param.7, s32[]{:T(128)S(6)} %select_n.363), kind=kLoop, calls=%fused_computation.58 | loop fusion | bytes 8388612 | tf_op jit(solution)/shard_map/dynamic_slice | solution.py:275
  59.1 4.3 %collective-permute-start.20 = (bf16[2,8,8,128,128]{4,3,2,1,0:T(8,128)(2,1)}, bf16[2,8,8,128,128]{4,3,2,1,0:T(8,128)(2,1)}, u32[]{:S(2)}, u32[]{:S(2)}) collective-permute-start(bf16[2,8,8,128,128]{4,3,2,1,0:T(8,128)(2,1)} %constant_dynamic-slice_fusion), channel_id=1, source_target_pairs={{0,1},{1,0},{2,3},{3,2},{4,5},{5,4},{6,7},{7,6},{8,9},{9,8},{10,11... | collective-permute-start | bytes 12582920 | tf_op jit(solution)/shard_map/ppermute | solution.py:191
  65.8 19.5 %collective-permute-done.12.refs_7_ = bf16[1,1024,256]{2,1,0:T(8,128)(2,1)S(1)} collective-permute-done((bf16[1,1024,256]{2,1,0:T(8,128)(2,1)S(1)}, bf16[1,1024,256]{2,1,0:T(8,128)(2,1)S(1)}, u32[]{:S(2)}, u32[]{:S(2)}) %collective-permute-start.12) | collective-permute-done | bytes 524320 | tf_op jit(solution)/shard_map/ppermute | solution.py:191
  85.3 11.8 %collective-permute-done.13.refs_8_ = bf16[1,1024,256]{2,1,0:T(8,128)(2,1)S(1)} collective-permute-done((bf16[1,1024,256]{2,1,0:T(8,128)(2,1)S(1)}, bf16[1,1024,256]{2,1,0:T(8,128)(2,1)S(1)}, u32[]{:S(2)}, u32[]{:S(2)}) %collective-permute-start.13) | collective-permute-done | bytes 524320 | tf_op jit(solution)/shard_map/ppermute | solution.py:191
  97.1 4.5 %collective-permute-start.21 = (s32[2]{0:T(128)S(1)}, s32[2]{0:T(128)S(1)}, u32[]{:S(2)}, u32[]{:S(2)}) collective-permute-start(s32[2]{0:T(128)S(1)} %copy-done.23), channel_id=1, source_target_pairs={{0,8},{1,9},{2,10},{3,11},{4,12},{5,13},{6,14},{7,15},{8,0},{9,1},... | collective-permute-start | bytes 32 | tf_op jit(solution)/shard_map/ppermute | solution.py:191
  102.5 1.7 collective-permute-start.16
  104.2 1.3 broadcast_select_fusion.1.ket_ref.refs_14_
  107.3 1.6 collective-permute-start.2
  111.1 6.6 %collective-permute-done.16.refs_12_ = bf16[1,1024,256]{2,1,0:T(8,128)(2,1)} collective-permute-done((bf16[1,1024,256]{2,1,0:T(8,128)(2,1)}, bf16[1,1024,256]{2,1,0:T(8,128)(2,1)}, u32[]{:S(2)}, u32[]{:S(2)}) %collective-permute-start.16) | collective-permute-done | bytes 524320 | tf_op jit(solution)/shard_map/ppermute | solution.py:191
  118.1 22.3 %collective-permute-done.17.refs_13_ = bf16[1,1024,256]{2,1,0:T(8,128)(2,1)S(1)} collective-permute-done((bf16[1,1024,256]{2,1,0:T(8,128)(2,1)S(1)}, bf16[1,1024,256]{2,1,0:T(8,128)(2,1)S(1)}, u32[]{:S(2)}, u32[]{:S(2)}) %collective-permute-start.17) | collective-permute-done | bytes 524320 | tf_op jit(solution)/shard_map/ppermute | solution.py:191
  140.4 3.6 %collective-permute-start.23 = (s32[2]{0:T(128)S(1)}, s32[2]{0:T(128)S(1)}, u32[]{:S(2)}, u32[]{:S(2)}) collective-permute-start(s32[2]{0:T(128)S(1)} %copy-done.23), channel_id=1, source_target_pairs={{0,16},{1,17},{2,18},{3,19},{4,20},{5,21},{6,22},{7,23},{8,24},{9,... | collective-permute-start | bytes 32 | tf_op jit(solution)/shard_map/ppermute | solution.py:191
  144.1 1.4 broadcast_select_fusion.ket_ref.refs_19_
  148.3 1.4 collective-permute-start.19
  150.7 20.3 %collective-permute-done.28.refs_20_ = bf16[2,1024,256]{2,1,0:T(8,128)(2,1)S(1)} collective-permute-done((bf16[2,1024,256]{2,1,0:T(8,128)(2,1)S(1)}, bf16[2,1024,256]{2,1,0:T(8,128)(2,1)S(1)}, u32[]{:S(2)}, u32[]{:S(2)}) %collective-permute-start.28) | collective-permute-done | bytes 1048608 | tf_op jit(solution)/shard_map/ppermute | solution.py:191
  172.9 1.6 collective-permute-start.24
  174.7 1.9 slice.92
  176.7 1.9 slice.93
  179.9 4.6 %dynamic-slice_select_fusion.weight_ref = bf16[2,8,8,128,128]{4,3,2,1,0:T(8,128)(2,1)} fusion(bf16[2,8,8,128,128]{4,3,2,1,0:T(8,128)(2,1)} %collective-permute-done.20, bf16[2,32,8,128,128]{4,3,2,1,0:T(8,128)(2,1)} %param.7, s32[]{:T(128)S(6)} %select_n.365, pred[]{:T(512)S(6)} %eq.64), kind=kLoop, calls=%fused_computation | loop fusion | flops 2097152 | bytes 12582917 | tf_op jit(solution)/shard_map/jit(_where)/select_n | solution.py:282
  184.9 1.7 collective-permute-start.30
  186.6 8.0 %ket_images.4 = bf16[2,2,1024,256]{3,2,1,0:T(8,128)(2,1)S(1)} custom-call(s32[1]{0:T(128)} %bitcast.4.core, s32[8,8]{1,0:T(8,128)S(1)} %get-tuple-element.37.columns, f32[2,8,8]{2,1,0:T(8,128)S(1)} %get-tuple-element.48.cosine, f32[2,8,8]{2,1,0:T(8,128)S(1)} %get-tuple-element.49.sine, bf16[2,2,512,256]{3,2,1,0:T(8,128)(2,1)S(1)} %collective-permute-done.18.outer_ref, ...), custom_call_target="tpu_custom_call" | custom-call | flops 2147483648 | bytes 6291456 | tf_op jit(solution)/shard_map/ket_images/pallas_call | solution.py:77
  195.9 1.7 collective-permute-start.31
  197.7 8.0 %ket_images.5 = bf16[2,2,1024,256]{3,2,1,0:T(8,128)(2,1)S(1)} custom-call(s32[1]{0:T(128)} %bitcast.4.core, s32[8,8]{1,0:T(8,128)S(1)} %get-tuple-element.37.columns, f32[2,8,8]{2,1,0:T(8,128)S(1)} %get-tuple-element.50.cosine, f32[2,8,8]{2,1,0:T(8,128)S(1)} %get-tuple-element.51.sine, bf16[2,2,512,256]{3,2,1,0:T(8,128)(2,1)S(1)} %collective-permute-done.22.outer_ref, ...), custom_call_target="tpu_custom_call" | custom-call | flops 2147483648 | bytes 6291456 | tf_op jit(solution)/shard_map/ket_images/pallas_call | solution.py:77
  205.7 1.3 copy-done.4
  207.0 8.0 %ket_images.6 = bf16[2,2,1024,256]{3,2,1,0:T(8,128)(2,1)S(1)} custom-call(s32[1]{0:T(128)} %bitcast.4.core, s32[8,8]{1,0:T(8,128)S(1)} %get-tuple-element.37.columns, f32[2,8,8]{2,1,0:T(8,128)S(1)} %get-tuple-element.52.cosine, f32[2,8,8]{2,1,0:T(8,128)S(1)} %get-tuple-element.53.sine, bf16[2,2,512,256]{3,2,1,0:T(8,128)(2,1)S(1)} %collective-permute-done.18.outer_ref, ...), custom_call_target="tpu_custom_call" | custom-call | flops 2147483648 | bytes 6291456 | tf_op jit(solution)/shard_map/ket_images/pallas_call | solution.py:77
  216.4 8.0 %ket_images.7 = bf16[2,2,1024,256]{3,2,1,0:T(8,128)(2,1)S(1)} custom-call(s32[1]{0:T(128)} %bitcast.4.core, s32[8,8]{1,0:T(8,128)S(1)} %get-tuple-element.37.columns, f32[2,8,8]{2,1,0:T(8,128)S(1)} %get-tuple-element.41.cosine, f32[2,8,8]{2,1,0:T(8,128)S(1)} %get-tuple-element.40.sine, bf16[2,2,512,256]{3,2,1,0:T(8,128)(2,1)S(1)} %collective-permute-done.22.outer_ref, ...), custom_call_target="tpu_custom_call" | custom-call | flops 2147483648 | bytes 6291456 | tf_op jit(solution)/shard_map/ket_images/pallas_call | solution.py:77
  224.4 1.3 copy-done.6
  225.8 11.3 %products.1 = f32[2,16,2,64,128]{4,3,2,1,0:T(8,128)} custom-call(s32[16]{0:T(128)S(1)} %pad_add_fusion.choice, bf16[4,1024,256]{2,1,0:T(8,128)(2,1)} %bitcast.83, bf16[4,1024,256]{2,1,0:T(8,128)(2,1)} %bitcast.84, bf16[4,1024,256]{2,1,0:T(8,128)(2,1)} %bitcast.85, bf16[4,1024,256]{2,1,0:T(8,128)(2,1)} %bitcast.86, ...), custom_call_target="tpu_custom_call" | custom-call | flops 2147483648 | bytes 16777216 | tf_op jit(solution)/shard_map/products/pallas_call | solution.py:149
  237.1 1.3 dynamic-slice_bitcast_fusion
  238.8 2.4 collective-permute-done.32
  241.2 1.4 bitcast_add_fusion
  242.6 1.9 collective-permute-start.35
  245.5 1.6 collective-permute-start.33
  247.1 6.7 %collective-permute-done.35 = f32[2,2,2,64,128]{4,3,2,1,0:T(8,128)S(1)} collective-permute-done((f32[2,2,2,64,128]{4,3,2,1,0:T(8,128)S(1)}, f32[2,2,2,64,128]{4,3,2,1,0:T(8,128)S(1)}, u32[]{:S(2)}, u32[]{:S(2)}) %collective-permute-start.35) | collective-permute-done | bytes 262176 | tf_op jit(solution)/shard_map/ppermute | solution.py:191
  253.8 15.1 %collective-permute-done.34 = f32[2,2,2,64,128]{4,3,2,1,0:T(8,128)S(1)} collective-permute-done((f32[2,2,2,64,128]{4,3,2,1,0:T(8,128)S(1)}, f32[2,2,2,64,128]{4,3,2,1,0:T(8,128)S(1)}, u32[]{:S(2)}, u32[]{:S(2)}) %collective-permute-start.34) | collective-permute-done | bytes 262176 | tf_op jit(solution)/shard_map/ppermute | solution.py:191
  (123 shorter events, 23.4 us)
Async XLA Ops:
  4.5 6.6 %collective-permute-start.7 = (bf16[2,1024,256]{2,1,0:T(8,128)(2,1)S(1)}, bf16[2,1024,256]{2,1,0:T(8,128)(2,1)S(1)}, u32[]{:S(2)}, u32[]{:S(2)}) collective-permute-start(bf16[2,1024,256]{2,1,0:T(8,128)(2,1)S(1)} %get-tuple-element.16), channel_id=1, source_target_pairs={{0,1},{1,0},{2,3},{3,2},{4,5},{5,4},{6,7},{7,6},{8,9},{9,8},{10,11... | collective-permute-start | bytes 3145736 | tf_op jit(solution)/shard_map/ppermute | solution.py:191
  5.0 28.8 %collective-permute-start.6 = (bf16[2,1024,256]{2,1,0:T(8,128)(2,1)}, bf16[2,1024,256]{2,1,0:T(8,128)(2,1)}, u32[]{:S(2)}, u32[]{:S(2)}) collective-permute-start(bf16[2,1024,256]{2,1,0:T(8,128)(2,1)} %get-tuple-element.17), channel_id=1, source_target_pairs={{0,8},{2,10},{4,12},{6,14},{8,0},{10,2},{12,4},{14,6},{17,24},{19,... | collective-permute-start | bytes 3145736 | tf_op jit(solution)/shard_map/ppermute | solution.py:191
  9.5 12.2 %collective-permute-start.1 = (bf16[2,1024,256]{2,1,0:T(8,128)(2,1)}, bf16[2,1024,256]{2,1,0:T(8,128)(2,1)}, u32[]{:S(2)}, u32[]{:S(2)}) collective-permute-start(bf16[2,1024,256]{2,1,0:T(8,128)(2,1)} %get-tuple-element.19), channel_id=1, source_target_pairs={{1,17},{3,19},{5,21},{7,23},{9,25},{11,27},{13,29},{15,31},{16,1},... | collective-permute-start | bytes 3145736 | tf_op jit(solution)/shard_map/ppermute | solution.py:191
  12.4 23.2 %collective-permute-start.8 = (bf16[2,1024,256]{2,1,0:T(8,128)(2,1)S(1)}, bf16[2,1024,256]{2,1,0:T(8,128)(2,1)S(1)}, u32[]{:S(2)}, u32[]{:S(2)}) collective-permute-start(bf16[2,1024,256]{2,1,0:T(8,128)(2,1)S(1)} %bitcast_select_fusion.ket_ref.refs_4_), channel_id=1, source_target_pairs={{0,2},{1,3},{2,0},{3,1},{4,6},{5,7},{6,4},{7,5},{8,10},{9,11},{10,... | collective-permute-start | bytes 3145736 | tf_op jit(solution)/shard_map/ppermute | solution.py:191
  14.0 23.4 %collective-permute-start.9 = (bf16[2,1024,256]{2,1,0:T(8,128)(2,1)S(1)}, bf16[2,1024,256]{2,1,0:T(8,128)(2,1)S(1)}, u32[]{:S(2)}, u32[]{:S(2)}) collective-permute-start(bf16[2,1024,256]{2,1,0:T(8,128)(2,1)S(1)} %bitcast_select_fusion.ket_ref.refs_4_), channel_id=1, source_target_pairs={{0,4},{1,5},{2,6},{3,7},{4,0},{5,1},{6,2},{7,3},{8,12},{9,13},{10,... | collective-permute-start | bytes 3145736 | tf_op jit(solution)/shard_map/ppermute | solution.py:191
  15.5 33.4 %collective-permute-start.5 = (bf16[2,1024,256]{2,1,0:T(8,128)(2,1)}, bf16[2,1024,256]{2,1,0:T(8,128)(2,1)}, u32[]{:S(2)}, u32[]{:S(2)}) collective-permute-start(bf16[2,1024,256]{2,1,0:T(8,128)(2,1)} %get-tuple-element.18), channel_id=1, source_target_pairs={{0,9},{2,11},{4,13},{6,15},{8,1},{10,3},{12,5},{14,7},{17,25},{19,... | collective-permute-start | bytes 3145736 | tf_op jit(solution)/shard_map/ppermute | solution.py:191
  21.7 42.8 %collective-permute-start.4 = (bf16[2,1024,256]{2,1,0:T(8,128)(2,1)}, bf16[2,1024,256]{2,1,0:T(8,128)(2,1)}, u32[]{:S(2)}, u32[]{:S(2)}) collective-permute-start(bf16[2,1024,256]{2,1,0:T(8,128)(2,1)} %get-tuple-element.15), channel_id=1, source_target_pairs={{1,16},{3,18},{5,20},{7,22},{9,24},{11,26},{13,28},{15,30},{16,0},... | collective-permute-start | bytes 3145736 | tf_op jit(solution)/shard_map/ppermute | solution.py:191
  35.6 23.4 %copy-start.12 = (bf16[2,1024,256]{2,1,0:T(8,128)(2,1)}, bf16[2,1024,256]{2,1,0:T(8,128)(2,1)S(1)}, u32[]{:S(2)}) copy-start(bf16[2,1024,256]{2,1,0:T(8,128)(2,1)S(1)} %collective-permute-done.8.refs_5_) | copy-start | bytes 3145732
  50.2 147.5 %copy-start = (bf16[2,1024,256]{2,1,0:T(8,128)(2,1)}, bf16[2,1024,256]{2,1,0:T(8,128)(2,1)S(1)}, u32[]{:S(2)}) copy-start(bf16[2,1024,256]{2,1,0:T(8,128)(2,1)S(1)} %broadcast_select_fusion.2.ket_ref.refs_9_) | copy-start | bytes 3145732
  50.2 46.8 %collective-permute-start.10 = (bf16[2,1024,256]{2,1,0:T(8,128)(2,1)S(1)}, bf16[2,1024,256]{2,1,0:T(8,128)(2,1)S(1)}, u32[]{:S(2)}, u32[]{:S(2)}) collective-permute-start(bf16[2,1024,256]{2,1,0:T(8,128)(2,1)S(1)} %broadcast_select_fusion.2.ket_ref.refs_9_), channel_id=1, source_target_pairs={{0,2},{1,3},{2,0},{3,1},{4,6},{5,7},{6,4},{7,5},{8,10},{9,11},{10,... | collective-permute-start | bytes 3145736 | tf_op jit(solution)/shard_map/ppermute | solution.py:191
  51.8 49.8 %collective-permute-start.11 = (bf16[2,1024,256]{2,1,0:T(8,128)(2,1)S(1)}, bf16[2,1024,256]{2,1,0:T(8,128)(2,1)S(1)}, u32[]{:S(2)}, u32[]{:S(2)}) collective-permute-start(bf16[2,1024,256]{2,1,0:T(8,128)(2,1)S(1)} %broadcast_select_fusion.2.ket_ref.refs_9_), channel_id=1, source_target_pairs={{0,4},{1,5},{2,6},{3,7},{4,0},{5,1},{6,2},{7,3},{8,12},{9,13},{10,... | collective-permute-start | bytes 3145736 | tf_op jit(solution)/shard_map/ppermute | solution.py:191
  53.4 10.0 %copy-start.11 = (bf16[2,4096,256]{2,1,0:T(8,128)(2,1)S(1)}, bf16[2,4096,256]{2,1,0:T(8,128)(2,1)}, u32[]{:S(2)}) copy-start(bf16[2,4096,256]{2,1,0:T(8,128)(2,1)} %param.6) | copy-start | bytes 12582916
  53.4 31.9 %collective-permute-start.12 = (bf16[1,1024,256]{2,1,0:T(8,128)(2,1)S(1)}, bf16[1,1024,256]{2,1,0:T(8,128)(2,1)S(1)}, u32[]{:S(2)}, u32[]{:S(2)}) collective-permute-start(bf16[1,1024,256]{2,1,0:T(8,128)(2,1)S(1)} %slice.88), channel_id=1, source_target_pairs={{0,4},{1,5},{2,6},{3,7},{4,0},{5,1},{6,2},{7,3},{8,12},{9,13},{10,... | collective-permute-start | bytes 1572872 | tf_op jit(solution)/shard_map/ppermute | solution.py:191
  59.0 38.0 %copy-start.23 = (s32[2]{0:T(128)S(1)}, s32[2]{0:T(128)}, u32[]{:S(2)}) copy-start(s32[2]{0:T(128)} %param.10) | copy-start | bytes 28
  59.0 49.9 %copy-start.20 = (s32[2,32]{1,0:T(2,128)S(1)}, s32[2,32]{1,0:T(2,128)}, u32[]{:S(2)}) copy-start(s32[2,32]{1,0:T(2,128)} %param.11) | copy-start | bytes 772
  59.0 50.7 %copy-start.21 = (s32[3,32,8]{1,2,0:T(8,128)S(1)}, s32[3,32,8]{1,2,0:T(8,128)}, u32[]{:S(2)}) copy-start(s32[3,32,8]{1,2,0:T(8,128)} %param.9) | copy-start | bytes 9220
  59.0 50.7 %copy-start.22 = (s32[32,8]{0,1:T(8,128)S(1)}, s32[32,8]{0,1:T(8,128)}, u32[]{:S(2)}) copy-start(s32[32,8]{0,1:T(8,128)} %param.8) | copy-start | bytes 3076
  59.1 120.4 %collective-permute-start.20 = (bf16[2,8,8,128,128]{4,3,2,1,0:T(8,128)(2,1)}, bf16[2,8,8,128,128]{4,3,2,1,0:T(8,128)(2,1)}, u32[]{:S(2)}, u32[]{:S(2)}) collective-permute-start(bf16[2,8,8,128,128]{4,3,2,1,0:T(8,128)(2,1)} %constant_dynamic-slice_fusion), channel_id=1, source_target_pairs={{0,1},{1,0},{2,3},{3,2},{4,5},{5,4},{6,7},{7,6},{8,9},{9,8},{10,11... | collective-permute-start | bytes 12582920 | tf_op jit(solution)/shard_map/ppermute | solution.py:191
  64.5 41.9 %collective-permute-start.3 = (bf16[2,1024,256]{2,1,0:T(8,128)(2,1)S(1)}, bf16[2,1024,256]{2,1,0:T(8,128)(2,1)S(1)}, u32[]{:S(2)}, u32[]{:S(2)}) collective-permute-start(bf16[2,1024,256]{2,1,0:T(8,128)(2,1)S(1)} %get-tuple-element.20), channel_id=1, source_target_pairs={{1,24},{3,26},{5,28},{7,30},{9,16},{11,18},{13,20},{15,22},{16,8},... | collective-permute-start | bytes 3145736 | tf_op jit(solution)/shard_map/ppermute | solution.py:191
  85.3 20.9 %copy-start.7 = (bf16[1,1024,256]{2,1,0:T(8,128)(2,1)}, bf16[1,1024,256]{2,1,0:T(8,128)(2,1)S(1)}, u32[]{:S(2)}) copy-start(bf16[1,1024,256]{2,1,0:T(8,128)(2,1)S(1)} %collective-permute-done.12.refs_7_) | copy-start | bytes 1572868
  85.3 11.8 %collective-permute-start.13 = (bf16[1,1024,256]{2,1,0:T(8,128)(2,1)S(1)}, bf16[1,1024,256]{2,1,0:T(8,128)(2,1)S(1)}, u32[]{:S(2)}, u32[]{:S(2)}) collective-permute-start(bf16[1,1024,256]{2,1,0:T(8,128)(2,1)S(1)} %slice.89), channel_id=1, source_target_pairs={{0,2},{1,3},{2,0},{3,1},{4,6},{5,7},{6,4},{7,5},{8,10},{9,11},{10,... | collective-permute-start | bytes 1572872 | tf_op jit(solution)/shard_map/ppermute | solution.py:191
  97.1 8.5 %collective-permute-start.25 = (s32[2]{0:T(128)S(1)}, s32[2]{0:T(128)S(1)}, u32[]{:S(2)}, u32[]{:S(2)}) collective-permute-start(s32[2]{0:T(128)S(1)} %copy-done.23), channel_id=1, source_target_pairs={{0,24},{1,25},{2,26},{3,27},{4,28},{5,29},{6,30},{7,31},{8,16},{9,... | collective-permute-start | bytes 32 | tf_op jit(solution)/shard_map/ppermute | solution.py:191
  97.1 9.0 %collective-permute-start.21 = (s32[2]{0:T(128)S(1)}, s32[2]{0:T(128)S(1)}, u32[]{:S(2)}, u32[]{:S(2)}) collective-permute-start(s32[2]{0:T(128)S(1)} %copy-done.23), channel_id=1, source_target_pairs={{0,8},{1,9},{2,10},{3,11},{4,12},{5,13},{6,14},{7,15},{8,0},{9,1},... | collective-permute-start | bytes 32 | tf_op jit(solution)/shard_map/ppermute | solution.py:191
  102.5 15.2 %collective-permute-start.16 = (bf16[1,1024,256]{2,1,0:T(8,128)(2,1)}, bf16[1,1024,256]{2,1,0:T(8,128)(2,1)}, u32[]{:S(2)}, u32[]{:S(2)}) collective-permute-start(bf16[1,1024,256]{2,1,0:T(8,128)(2,1)} %slice.90), channel_id=1, source_target_pairs={{0,4},{1,5},{2,6},{3,7},{4,0},{5,1},{6,2},{7,3},{8,12},{9,13},{10,... | collective-permute-start | bytes 1572872 | tf_op jit(solution)/shard_map/ppermute | solution.py:191
  105.5 101.5 %copy-start.1 = (bf16[2,1024,256]{2,1,0:T(8,128)(2,1)}, bf16[2,1024,256]{2,1,0:T(8,128)(2,1)S(1)}, u32[]{:S(2)}) copy-start(bf16[2,1024,256]{2,1,0:T(8,128)(2,1)S(1)} %broadcast_select_fusion.1.ket_ref.refs_14_) | copy-start | bytes 3145732
  105.5 38.5 %collective-permute-start.14 = (bf16[2,1024,256]{2,1,0:T(8,128)(2,1)S(1)}, bf16[2,1024,256]{2,1,0:T(8,128)(2,1)}, u32[]{:S(2)}, u32[]{:S(2)}) collective-permute-start(bf16[2,1024,256]{2,1,0:T(8,128)(2,1)S(1)} %broadcast_select_fusion.1.ket_ref.refs_14_), channel_id=1, source_target_pairs={{0,2},{1,3},{2,0},{3,1},{4,6},{5,7},{6,4},{7,5},{8,10},{9,11},{10,... | collective-permute-start | bytes 3145736 | tf_op jit(solution)/shard_map/ppermute | solution.py:191
  106.1 37.9 %collective-permute-start.15 = (bf16[2,1024,256]{2,1,0:T(8,128)(2,1)S(1)}, bf16[2,1024,256]{2,1,0:T(8,128)(2,1)}, u32[]{:S(2)}, u32[]{:S(2)}) collective-permute-start(bf16[2,1024,256]{2,1,0:T(8,128)(2,1)S(1)} %broadcast_select_fusion.1.ket_ref.refs_14_), channel_id=1, source_target_pairs={{0,4},{1,5},{2,6},{3,7},{4,0},{5,1},{6,2},{7,3},{8,12},{9,13},{10,... | collective-permute-start | bytes 3145736 | tf_op jit(solution)/shard_map/ppermute | solution.py:191
  107.3 36.7 %collective-permute-start.2 = (bf16[2,1024,256]{2,1,0:T(8,128)(2,1)}, bf16[2,1024,256]{2,1,0:T(8,128)(2,1)}, u32[]{:S(2)}, u32[]{:S(2)}) collective-permute-start(bf16[2,1024,256]{2,1,0:T(8,128)(2,1)} %get-tuple-element.21), channel_id=1, source_target_pairs={{1,25},{3,27},{5,29},{7,31},{9,17},{11,19},{13,21},{15,23},{16,9},... | collective-permute-start | bytes 3145736 | tf_op jit(solution)/shard_map/ppermute | solution.py:191
  117.7 22.7 %collective-permute-start.17 = (bf16[1,1024,256]{2,1,0:T(8,128)(2,1)S(1)}, bf16[1,1024,256]{2,1,0:T(8,128)(2,1)S(1)}, u32[]{:S(2)}, u32[]{:S(2)}) collective-permute-start(bf16[1,1024,256]{2,1,0:T(8,128)(2,1)S(1)} %slice.91), channel_id=1, source_target_pairs={{0,2},{1,3},{2,0},{3,1},{4,6},{5,7},{6,4},{7,5},{8,10},{9,11},{10,... | collective-permute-start | bytes 1572872 | tf_op jit(solution)/shard_map/ppermute | solution.py:191
  140.4 5.4 %collective-permute-start.23 = (s32[2]{0:T(128)S(1)}, s32[2]{0:T(128)S(1)}, u32[]{:S(2)}, u32[]{:S(2)}) collective-permute-start(s32[2]{0:T(128)S(1)} %copy-done.23), channel_id=1, source_target_pairs={{0,16},{1,17},{2,18},{3,19},{4,20},{5,21},{6,22},{7,23},{8,24},{9,... | collective-permute-start | bytes 32 | tf_op jit(solution)/shard_map/ppermute | solution.py:191
  144.0 1.8 collective-permute-start
  145.4 71.0 %copy-start.2 = (bf16[2,1024,256]{2,1,0:T(8,128)(2,1)}, bf16[2,1024,256]{2,1,0:T(8,128)(2,1)S(1)}, u32[]{:S(2)}) copy-start(bf16[2,1024,256]{2,1,0:T(8,128)(2,1)S(1)} %broadcast_select_fusion.ket_ref.refs_19_) | copy-start | bytes 3145732
  145.4 25.6 %collective-permute-start.28 = (bf16[2,1024,256]{2,1,0:T(8,128)(2,1)S(1)}, bf16[2,1024,256]{2,1,0:T(8,128)(2,1)S(1)}, u32[]{:S(2)}, u32[]{:S(2)}) collective-permute-start(bf16[2,1024,256]{2,1,0:T(8,128)(2,1)S(1)} %broadcast_select_fusion.ket_ref.refs_19_), channel_id=1, source_target_pairs={{0,2},{1,3},{2,0},{3,1},{4,6},{5,7},{6,4},{7,5},{8,10},{9,11},{10,... | collective-permute-start | bytes 3145736 | tf_op jit(solution)/shard_map/ppermute | solution.py:191
  145.8 27.0 %collective-permute-start.29 = (bf16[2,1024,256]{2,1,0:T(8,128)(2,1)S(1)}, bf16[2,1024,256]{2,1,0:T(8,128)(2,1)S(1)}, u32[]{:S(2)}, u32[]{:S(2)}) collective-permute-start(bf16[2,1024,256]{2,1,0:T(8,128)(2,1)S(1)} %broadcast_select_fusion.ket_ref.refs_19_), channel_id=1, source_target_pairs={{0,4},{1,5},{2,6},{3,7},{4,0},{5,1},{6,2},{7,3},{8,12},{9,13},{10,... | collective-permute-start | bytes 3145736 | tf_op jit(solution)/shard_map/ppermute | solution.py:191
  147.5 37.0 %collective-permute-start.18 = (bf16[2,2,512,256]{3,2,1,0:T(8,128)(2,1)S(1)}, bf16[2,2,512,256]{3,2,1,0:T(8,128)(2,1)S(1)}, u32[]{:S(2)}, u32[]{:S(2)}) collective-permute-start(bf16[2,2,512,256]{3,2,1,0:T(8,128)(2,1)S(1)} %pad_maximum_fusion), channel_id=1, source_target_pairs={{1,8},{3,10},{5,12},{7,14},{8,1},{9,16},{10,3},{11,18},{12,5},{13,... | collective-permute-start | bytes 3145736 | tf_op jit(solution)/shard_map/ppermute | solution.py:191
  148.3 36.6 %collective-permute-start.19 = (bf16[2,2,512,256]{3,2,1,0:T(8,128)(2,1)S(1)}, bf16[2,2,512,256]{3,2,1,0:T(8,128)(2,1)S(1)}, u32[]{:S(2)}, u32[]{:S(2)}) collective-permute-start(bf16[2,2,512,256]{3,2,1,0:T(8,128)(2,1)S(1)} %pad_maximum_fusion.1), channel_id=1, source_target_pairs={{0,1},{1,0},{2,3},{3,2},{4,5},{5,4},{6,7},{7,6},{8,9},{9,8},{10,11... | collective-permute-start | bytes 3145736 | tf_op jit(solution)/shard_map/ppermute | solution.py:191
  171.0 13.5 %copy-start.17 = (bf16[2,1024,256]{2,1,0:T(8,128)(2,1)}, bf16[2,1024,256]{2,1,0:T(8,128)(2,1)S(1)}, u32[]{:S(2)}) copy-start(bf16[2,1024,256]{2,1,0:T(8,128)(2,1)S(1)} %collective-permute-done.28.refs_20_) | copy-start | bytes 3145732
  171.0 24.9 %collective-permute-start.22 = (bf16[2,2,512,256]{3,2,1,0:T(8,128)(2,1)}, bf16[2,2,512,256]{3,2,1,0:T(8,128)(2,1)S(1)}, u32[]{:S(2)}, u32[]{:S(2)}) collective-permute-start(bf16[2,2,512,256]{3,2,1,0:T(8,128)(2,1)} %pad_maximum_fusion.2), channel_id=1, source_target_pairs={{1,8},{3,10},{5,12},{7,14},{8,1},{9,16},{10,3},{11,18},{12,5},{13,... | collective-permute-start | bytes 3145736 | tf_op jit(solution)/shard_map/ppermute | solution.py:191
  172.9 11.6 %copy-start.18 = (bf16[2,1024,256]{2,1,0:T(8,128)(2,1)}, bf16[2,1024,256]{2,1,0:T(8,128)(2,1)S(1)}, u32[]{:S(2)}) copy-start(bf16[2,1024,256]{2,1,0:T(8,128)(2,1)S(1)} %collective-permute-done.29.refs_21_) | copy-start | bytes 3145732
  172.9 34.2 %collective-permute-start.24 = (bf16[2,2,512,256]{3,2,1,0:T(8,128)(2,1)}, bf16[2,2,512,256]{3,2,1,0:T(8,128)(2,1)S(1)}, u32[]{:S(2)}, u32[]{:S(2)}) collective-permute-start(bf16[2,2,512,256]{3,2,1,0:T(8,128)(2,1)} %pad_maximum_fusion.3), channel_id=1, source_target_pairs={{0,1},{1,0},{2,3},{3,2},{4,5},{5,4},{6,7},{7,6},{8,9},{9,8},{10,11... | collective-permute-start | bytes 3145736 | tf_op jit(solution)/shard_map/ppermute | solution.py:191
  179.5 46.2 %collective-permute-start.26 = (bf16[1,1024,256]{2,1,0:T(8,128)(2,1)}, bf16[1,1024,256]{2,1,0:T(8,128)(2,1)S(1)}, u32[]{:S(2)}, u32[]{:S(2)}) collective-permute-start(bf16[1,1024,256]{2,1,0:T(8,128)(2,1)} %slice.92), channel_id=1, source_target_pairs={{0,4},{1,5},{2,6},{3,7},{4,0},{5,1},{6,2},{7,3},{8,12},{9,13},{10,... | collective-permute-start | bytes 1572872 | tf_op jit(solution)/shard_map/ppermute | solution.py:191
  184.5 41.2 %collective-permute-start.27 = (bf16[1,1024,256]{2,1,0:T(8,128)(2,1)}, bf16[1,1024,256]{2,1,0:T(8,128)(2,1)S(1)}, u32[]{:S(2)}, u32[]{:S(2)}) collective-permute-start(bf16[1,1024,256]{2,1,0:T(8,128)(2,1)} %slice.93), channel_id=1, source_target_pairs={{0,2},{1,3},{2,0},{3,1},{4,6},{5,7},{6,4},{7,5},{8,10},{9,11},{10,... | collective-permute-start | bytes 1572872 | tf_op jit(solution)/shard_map/ppermute | solution.py:191
  184.9 40.9 %collective-permute-start.30 = (bf16[1,1024,256]{2,1,0:T(8,128)(2,1)}, bf16[1,1024,256]{2,1,0:T(8,128)(2,1)S(1)}, u32[]{:S(2)}, u32[]{:S(2)}) collective-permute-start(bf16[1,1024,256]{2,1,0:T(8,128)(2,1)} %slice.94), channel_id=1, source_target_pairs={{0,4},{1,5},{2,6},{3,7},{4,0},{5,1},{6,2},{7,3},{8,12},{9,13},{10,... | collective-permute-start | bytes 1572872 | tf_op jit(solution)/shard_map/ppermute | solution.py:191
  195.9 29.8 %collective-permute-start.31 = (bf16[1,1024,256]{2,1,0:T(8,128)(2,1)S(1)}, bf16[1,1024,256]{2,1,0:T(8,128)(2,1)S(1)}, u32[]{:S(2)}, u32[]{:S(2)}) collective-permute-start(bf16[1,1024,256]{2,1,0:T(8,128)(2,1)S(1)} %slice.95), channel_id=1, source_target_pairs={{0,2},{1,3},{2,0},{3,1},{4,6},{5,7},{6,4},{7,5},{8,10},{9,11},{10,... | collective-permute-start | bytes 1572872 | tf_op jit(solution)/shard_map/ppermute | solution.py:191
  238.4 2.7 %collective-permute-start.32 = (f32[16,2,64,128]{3,2,1,0:T(8,128)S(1)}, f32[16,2,64,128]{3,2,1,0:T(8,128)S(1)}, u32[]{:S(2)}, u32[]{:S(2)}) collective-permute-start(f32[16,2,64,128]{3,2,1,0:T(8,128)S(1)} %dynamic-slice_bitcast_fusion), channel_id=1, source_target_pairs={{0,1},{1,0},{2,3},{3,2},{4,5},{5,4},{6,7},{7,6},{8,9},{9,8},{10,11... | collective-permute-start | bytes 3145736 | tf_op jit(solution)/shard_map/ppermute | solution.py:191
  242.6 11.1 %collective-permute-start.35 = (f32[2,2,2,64,128]{4,3,2,1,0:T(8,128)S(1)}, f32[2,2,2,64,128]{4,3,2,1,0:T(8,128)S(1)}, u32[]{:S(2)}, u32[]{:S(2)}) collective-permute-start(f32[2,2,2,64,128]{4,3,2,1,0:T(8,128)S(1)} %bitcast.93), channel_id=1, source_target_pairs={{0,24},{1,25},{2,26},{3,27},{4,28},{5,29},{6,30},{7,31},{8,16},{9,... | collective-permute-start | bytes 786440 | tf_op jit(solution)/shard_map/ppermute | solution.py:191
  244.6 24.3 %collective-permute-start.34 = (f32[2,2,2,64,128]{4,3,2,1,0:T(8,128)S(1)}, f32[2,2,2,64,128]{4,3,2,1,0:T(8,128)S(1)}, u32[]{:S(2)}, u32[]{:S(2)}) collective-permute-start(f32[2,2,2,64,128]{4,3,2,1,0:T(8,128)S(1)} %bitcast.92), channel_id=1, source_target_pairs={{0,16},{1,17},{2,18},{3,19},{4,20},{5,21},{6,22},{7,23},{8,24},{9,... | collective-permute-start | bytes 786440 | tf_op jit(solution)/shard_map/ppermute | solution.py:191
  245.5 23.4 %collective-permute-start.33 = (f32[2,2,2,64,128]{4,3,2,1,0:T(8,128)S(1)}, f32[2,2,2,64,128]{4,3,2,1,0:T(8,128)S(1)}, u32[]{:S(2)}, u32[]{:S(2)}) collective-permute-start(f32[2,2,2,64,128]{4,3,2,1,0:T(8,128)S(1)} %bitcast.91), channel_id=1, source_target_pairs={{0,8},{1,9},{2,10},{3,11},{4,12},{5,13},{6,14},{7,15},{8,0},{9,1},... | collective-permute-start | bytes 786440 | tf_op jit(solution)/shard_map/ppermute | solution.py:191
  (12 other events, 56.0 us)

commit v3 on v0

v3 whole, which is shorter than its diff:
```python
import functools
import math

import jax
import jax.numpy as jnp
from jax import lax
from jax.experimental import pallas as pl
from jax.experimental.pallas import tpu as pltpu
from jax.sharding import PartitionSpec as P

BLK = 128
HALO = 4
KGRID = 32
VMEM = 48 * 1024 * 1024
KETCOST = 1
SPLIT = (2, 3)
PLAN = {
    "trade1": ["trade0"],
    "rows20": ["tables"],
    "rows21": ["rows20"],
    "rows30": ["rows21"],
    "second0": ["rows20"],
    "first1": ["first0", "second0", "rows21"],
    "weights": ["first0", "second0"],
    "first2": ["first1"],
    "second2": ["rows30"],
    "inner_low": ["second1"],
    "outer_odd": ["second1"],
    "inner_high": ["first2"],
    "outer_even": ["first2"],
    "first3": ["first2", "second1"],
    "second3": ["second2", "images_odd"],
    "rows31": ["rows30"],
}


def phases(kpoints, images):
    first_coord = kpoints // (KGRID * KGRID)
    second_coord = kpoints // KGRID % KGRID
    third_coord = kpoints % KGRID
    turn_count = (
        first_coord[:, None, None] * images[0][None]
        + second_coord[:, None, None] * images[1][None]
        + third_coord[:, None, None] * images[2][None]
    ) % KGRID
    angles = turn_count.astype(jnp.float32) * (2.0 * math.pi / KGRID)
    return (jnp.cos(angles), jnp.sin(angles))


def image_kernel(outer_places, inner_places, where, columns, cosine, sine, *refs):
    groups = len(outer_places)
    outer_refs, ket_refs, inner_refs = (refs[i * groups : (i + 1) * groups] for i in range(3))
    held_ref, sent_ref = refs[3 * groups : 3 * groups + 2]
    out_refs = refs[3 * groups + 2 : 4 * groups + 2]
    kets, weights, images, ket_sem, weight_sem, image_sem = refs[4 * groups + 2 :]
    points, rows, width = ket_refs[0].shape
    momenta, blocks, slots, size, _ = sent_ref.shape
    reach = outer_refs[0].shape[2]
    bands = width // 2
    core, is_home, first = where[0], where[1], where[2]

    def part(group, source, start, length, number):
        spot = pl.ds(pl.multiple_of(start, size), length)
        return pltpu.make_async_copy(source, kets.at[group, :, spot], ket_sem.at[group, number])

    parts = [
        [
            part(g, ket_refs[g], reach, rows, 0),
            part(g, outer_refs[g].at[outer_places[g]], core * (reach + rows), reach, 1),
            part(g, inner_refs[g].at[inner_places[g]], (1 - core) * (reach + rows), reach, 2),
        ]
        for g in range(groups)
    ]

    def weight_copy(block):
        return pltpu.make_async_copy(sent_ref.at[:, block], weights.at[:, block], weight_sem.at[block])

    def fetch_weights(count, start):
        @pl.when(is_home == 1)
        def _():
            for block in range(start, start + count):
                pltpu.make_async_copy(
                    held_ref.at[:, first + block], weights.at[:, block], weight_sem.at[block]
                ).start()

        @pl.when(is_home == 0)
        def _():
            for block in range(start, start + count):
                weight_copy(block).start()

    fetch_weights(1, 0)
    for copy in parts[0]:
        copy.start()
    fetch_weights(blocks - 1, 1)
    for copies in parts[1:]:
        for copy in copies:
            copy.start()

    def image_copy(group, block):
        spot = pl.ds(pl.multiple_of(block * size, size), size)
        return pltpu.make_async_copy(
            images.at[group, :, :, spot], out_refs[group].at[:, :, spot], image_sem.at[group, block]
        )

    for group in range(groups):
        for copy in parts[group]:
            copy.wait()

        @pl.loop(0, blocks)
        def _(block, group=group):
            if group == 0:
                weight_copy(block).wait()
            row = jnp.concatenate(
                [
                    jnp.concatenate([weights[q, block, s] for s in range(slots)], axis=1)
                    for q in range(momenta)
                ],
                axis=0,
            )
            spot = pl.ds(pl.multiple_of(block * size, size), size)
            for point in range(points):
                turned = []
                for s in range(slots):
                    start = pl.multiple_of(columns[block, s] * size, size)
                    real = kets[group, point, pl.ds(start, size), :bands].astype(jnp.float32)
                    imag = kets[group, point, pl.ds(start, size), bands:].astype(jnp.float32)
                    c, d = cosine[group * points + point, block, s], sine[group * points + point, block, s]
                    both = jnp.concatenate([c * real - d * imag, d * real + c * imag], axis=1)
                    turned.append(both.astype(jnp.bfloat16))
                image = jnp.dot(
                    row, jnp.concatenate(turned, axis=0), preferred_element_type=jnp.float32
                )
                for q in range(momenta):
                    images[group, point, q, spot] = image[q * size : (q + 1) * size].astype(images.dtype)
            image_copy(group, block).start()

    for group in range(groups):
        for block in range(blocks):
            image_copy(group, block).wait()


def ket_images(where, columns, cosine, sine, outer, kets, inner, held, sent):
    groups = len(kets)
    momenta, blocks, slots, size, _ = sent.shape
    points, rows, width = kets[0].shape
    reach = outer[0][0].shape[2]
    shape = (points, momenta, rows, width)
    places = [tuple(place for _, place in ends) for ends in (outer, inner)]
    return pl.pallas_call(
        functools.partial(image_kernel, *places),
        in_specs=[pl.BlockSpec(memory_space=pltpu.SMEM)] * 4
        + [pl.BlockSpec(memory_space=pl.ANY)] * (3 * groups + 2),
        out_specs=[pl.BlockSpec(memory_space=pl.ANY)] * groups,
        out_shape=[jax.ShapeDtypeStruct(shape, jnp.bfloat16)] * groups,
        scratch_shapes=[
            pltpu.VMEM((groups, points, rows + 2 * reach, width), jnp.bfloat16),
            pltpu.VMEM(sent.shape, jnp.bfloat16),
            pltpu.VMEM((groups, *shape), jnp.bfloat16),
            pltpu.SemaphoreType.DMA((groups, 3)),
            pltpu.SemaphoreType.DMA((blocks,)),
            pltpu.SemaphoreType.DMA((groups, blocks)),
        ],
        compiler_params=pltpu.CompilerParams(vmem_limit_bytes=VMEM),
        cost_estimate=pl.CostEstimate(
            flops=KETCOST * groups * 2 * points * momenta * blocks * slots * size * size * width,
            bytes_accessed=sent.size * 2 + groups * kets[0].size * 10,
            transcendentals=0,
        ),
        name="ket_images",
    )(where, columns, cosine, sine, *[x for x, _ in outer], *kets, *[x for x, _ in inner], held, sent)


def product_kernel(groups, places, choice, where, *refs):
    image_refs, bra_refs = refs[:groups], refs[groups:-6]
    kept_ref, given_ref, image_buf, bra_buf, image_sem, bra_sem = refs[-6:]
    pairs = choice.shape[0]
    per_group = pairs // groups
    half = kept_ref.shape[2]
    bands = 2 * half

    @pl.loop(0, pairs)
    def _(pair):
        wanted = choice[pair]
        for number, (array, point) in enumerate(places):

            @pl.when(wanted == number)
            def _():
                source = bra_refs[array].at[point]
                pltpu.make_async_copy(source, bra_buf.at[pair], bra_sem.at[pair]).start()

    def image_copy(pair):
        point, momentum = divmod(pair % per_group, image_refs[0].shape[1])
        source = image_refs[pair // per_group].at[point, momentum]
        return pltpu.make_async_copy(source, image_buf.at[pair], image_sem.at[pair])

    for pair in range(pairs):
        image_copy(pair).start()
    low = where[0] == 0
    for pair in range(pairs):
        image_copy(pair).wait()
        pltpu.make_async_copy(bra_refs[0].at[0], bra_buf.at[pair], bra_sem.at[pair]).wait()
        value = lax.dot_general(
            bra_buf[pair],
            image_buf[pair],
            (((0,), (0,)), ((), ())),
            preferred_element_type=jnp.float32,
        )
        real = value[:bands, :bands] + value[bands:, bands:]
        imag = value[:bands, bands:] - value[bands:, :bands]
        for part, x in enumerate((real, imag)):
            kept_ref[pair, part] = jnp.where(low, x[:half], x[half:])
            given_ref[pair, part] = jnp.where(low, x[half:], x[:half])


def products(choice, where, images, bras, places):
    groups = len(images)
    _, rows, width = bras[0].shape
    pairs = choice.shape[0]
    bands = width // 2
    half = jax.ShapeDtypeStruct((pairs, 2, bands // 2, bands), jnp.float32)
    return pl.pallas_call(
        functools.partial(product_kernel, groups, places),
        in_specs=[pl.BlockSpec(memory_space=pltpu.SMEM)] * 2
        + [pl.BlockSpec(memory_space=pl.ANY)] * (groups + len(bras)),
        out_specs=[pl.BlockSpec(memory_space=pltpu.VMEM)] * 2,
        out_shape=[half, half],
        scratch_shapes=[
            pltpu.VMEM((pairs, rows, width), jnp.bfloat16),
            pltpu.VMEM((pairs, rows, width), jnp.bfloat16),
            pltpu.SemaphoreType.DMA((pairs,)),
            pltpu.SemaphoreType.DMA((pairs,)),
        ],
        compiler_params=pltpu.CompilerParams(vmem_limit_bytes=VMEM),
        cost_estimate=pl.CostEstimate(
            flops=2 * pairs * rows * width * width,
            bytes_accessed=4 * pairs * rows * width,
            transcendentals=0,
        ),
        name="products",
    )(choice, where, *images, *bras)


def per_device(coeffs, perturbation, columns, images, kpoints, matching):
    n_ka, n_orb = lax.axis_size("ka"), lax.axis_size("orb")
    points, row_count, width = coeffs.shape
    block_count = row_count // BLK
    momenta = perturbation.shape[0]
    bits_of = lambda n: n.bit_length() - 1
    n_rows = min(n_ka, block_count // (2 * HALO))
    n_side = n_ka // n_rows
    blocks = block_count // n_rows
    share = n_rows // n_orb
    rows = blocks * BLK
    me, core = lax.axis_index("ka"), lax.axis_index("orb")
    z, side = me // n_side, me % n_side

    def flat(zi, gi, ci):
        return (zi * n_side + gi) * n_orb + ci

    every = [(zi, gi, ci) for zi in range(n_rows) for gi in range(n_side) for ci in range(n_orb)]

    def send(x, to):
        moves = [(flat(*spot), to(*spot)) for spot in every]
        return lax.ppermute(x, ("ka", "orb"), [(a, flat(*b)) for a, b in moves if b is not None])

    def on_core(x, d):
        return send(x, lambda zi, gi, ci: (zi, gi, (ci + d) % n_orb))

    def across_rows(x, s):
        return send(x, lambda zi, gi, ci: (zi ^ s, gi, ci))

    def across_side(x, bit):
        return send(x, lambda zi, gi, ci: (zi, gi ^ (1 << bit), ci))

    def pick(x, index, axis):
        return lax.dynamic_index_in_dim(x, index, axis, keepdims=False)

    def after(x, *arrived):
        return lax.optimization_barrier((x, *arrived))[0] if arrived else x

    done, todo = {}, []

    def step(name, needs, run):
        known = [other for other in PLAN.get(name, ()) if other not in needs]
        todo.append((name, [*needs, *known], known, run))

    def run_steps():
        while todo:
            for entry in todo:
                name, needs, known, run = entry
                if all(other in done for other in needs):
                    done[name] = run([x for other in known for x in jax.tree.leaves(done[other])])
                    todo.remove(entry)
                    break
            else:
                raise ValueError("circular plan")

    held = coeffs.reshape(points, share, n_orb, rows, width)
    is_home = core == z // share

    def trade(j, arrived):
        mine = pick(after(held, *arrived), (z ^ j) % share, 1)
        kept, given = pick(mine, core, 1), pick(mine, 1 - core, 1)
        came = on_core(given, 1)
        return lax.optimization_barrier((jnp.where(is_home, kept, came), jnp.where(is_home, came, kept)))

    for j in range(share):
        step(f"trade{j}", [], functools.partial(trade, j))

    def to_send(s):
        return done[f"trade{s % share}"][s // share]

    def tables(arrived):
        table = after(jnp.concatenate([columns[None], images]), *arrived)
        table = jnp.where(is_home, table, on_core(table, 1))
        table = lax.dynamic_slice_in_dim(table, (n_orb * z + core) % n_rows * blocks, blocks, 1)
        owned = after(kpoints[None], table)
        for bit in range(bits_of(n_rows)):
            owned = jnp.concatenate([owned, across_rows(owned, 1 << bit)])
        return table, owned

    step("tables", [], tables)

    first_mine = (n_orb * z + core) % n_rows * blocks

    def trade_weights(arrived):
        first_sent = (n_orb * z + 1 - core) % n_rows * blocks
        given = lax.dynamic_slice_in_dim(after(perturbation, *arrived), first_sent, blocks, 1)
        return on_core(given, 1)

    step("weights", [], trade_weights)

    for s in range(1, n_rows):
        size = 1 if s in SPLIT else points
        for i in range(points // size):

            def rows_from(arrived, s=s, i=i, size=size):
                return across_rows(after(to_send(s), *arrived)[i * size : (i + 1) * size], s)

            step(f"rows{s}{i}", [f"trade{s % share}"], rows_from)

        def whole(arrived, s=s, count=points // size):
            came = [done[f"rows{s}{i}"] for i in range(count)]
            return lax.optimization_barrier(jnp.concatenate(came) if count > 1 else came[0])

        step(f"group{s}", [f"rows{s}{i}" for i in range(points // size)], whole)
    step("group0", ["trade0"], lambda arrived: to_send(0))

    bits = list(range(bits_of(n_side)))
    bras, number_of = {}, {}

    def first_hops(s, arrived):
        group = after(done[f"group{s}"], *arrived)
        return [across_side(group, bit) for bit in bits]

    def second_hops(s, arrived):
        arrays = [done[f"group{s}"], *done[f"first{s}"]]
        came = []
        found = {(0, point): (0, point) for point in range(points)}
        found |= {(1 << bit, point): (1 + bit, point) for bit in bits for point in range(points)}
        for p in sorted(range(n_side), key=lambda n: n.bit_count()):
            for point in range(points):
                if (p, point) not in found:
                    bit = [bit for bit in bits if p >> bit & 1][-1 if point % 2 == 0 else 0]
                    array, place = found[p ^ (1 << bit), point]
                    came.append(across_side(after(arrays[array][place : place + 1], *arrived), bit))
                    found[p, point] = (len(arrays), 0)
                    arrays.append(came[-1])
        bras[s] = arrays
        number_of[s] = [found[p, point] for p in range(n_side) for point in range(points)]
        return came

    for s in range(n_rows):
        step(f"first{s}", [f"group{s}"], functools.partial(first_hops, s))
        step(f"second{s}", [f"first{s}"], functools.partial(second_hops, s))

    reach = HALO * BLK
    lead = rows - reach
    flips = sorted({a ^ (a + 1) for a in range(n_rows - 1)})

    def ends(members, start, arrived):
        return jnp.stack([lax.dynamic_slice_in_dim(after(x, *arrived), start, reach, 1) for x in members])

    def outer_ends(wanted, arrived):
        flip = jnp.where(core == 0, z ^ (z - 1), z ^ (z + 1))
        members = []
        for s in wanted:
            out = done[f"group{s ^ flips[0]}"]
            for x in flips[1:]:
                out = jnp.where(flip == x, done[f"group{s ^ x}"], out)
            members.append(out)

        def to(zi, gi, ci):
            zt = zi + 2 * ci - 1
            return (zt, gi, 1 - ci) if 0 <= zt < n_rows else None

        return send(ends(members, core * lead, arrived), to)

    def inner_ends(wanted, arrived):
        return on_core(ends([done[f"group{s}"] for s in wanted], (1 - core) * lead, arrived), 1)

    outer, inner = {}, {}
    parts = {"low": range(share), "high": range(share, n_rows), "odd": range(1, n_rows, 2), "even": range(0, n_rows, 2)}
    for name, part in parts.items():
        if name in ("low", "high"):
            needs = {f"group{s}" for s in part}
            step(f"inner_{name}", sorted(needs), functools.partial(inner_ends, part))
            inner |= {s: (f"inner_{name}", i) for i, s in enumerate(part)}
        else:
            needs = {f"group{s ^ x}" for s in part for x in flips}
            step(f"outer_{name}", sorted(needs), functools.partial(outer_ends, part))
            outer |= {s: (f"outer_{name}", i) for i, s in enumerate(part)}

    def images_of(part, arrived):
        table, owned = done["tables"]
        cosine, sine = phases(jnp.concatenate([owned[s] for s in part]), table[1:])
        return ket_images(
            jnp.stack([core, is_home.astype(core.dtype), first_mine]),
            table[0] - (n_orb * z + core) * blocks + HALO,
            cosine,
            sine,
            [(done[outer[s][0]], outer[s][1]) for s in part],
            [after(done[f"group{s}"], *arrived) for s in part],
            [(done[inner[s][0]], inner[s][1]) for s in part],
            perturbation,
            done["weights"],
        )

    for name in ("odd", "even"):
        needs = {need for s in parts[name] for need in (f"group{s}", outer[s][0], inner[s][0])}
        needs = sorted(needs) + ["tables", "weights"]
        step(f"images_{name}", needs, functools.partial(images_of, parts[name]))
    run_steps()

    places, arrays, choices = [], [], []
    for s in range(n_rows):
        places += [(len(arrays) + array, place) for array, place in number_of[s]]
        arrays += bras[s]
        first = ((z ^ s) * n_side + side) * points
        found = lax.dynamic_slice_in_dim(matching, first, points, 1)
        owner = found // points
        number = ((owner // n_side) ^ z) * n_side + ((owner % n_side) ^ side)
        choices.append((number * points + found % points).T.reshape(-1))

    kets = [None] * n_rows
    for name in ("odd", "even"):
        for s, x in zip(parts[name], done[f"images_{name}"]):
            kets[s] = x
    kept, given = products(jnp.concatenate(choices), core[None], kets, arrays, places)
    total = (kept + on_core(given, 1)).reshape(n_rows, points, momenta, *kept.shape[1:])
    out = total[0]
    for s in range(1, n_rows):
        out = out + across_rows(total[s].astype(jnp.bfloat16), s).astype(jnp.float32)
    return out


def solution(mesh):
    in_specs = (
        P("ka", "orb", None),
        P(None, "orb", None, None, None),
        P("orb", None),
        P(None, "orb", None),
        P("ka"),
        P(),
    )
    out_specs = P("ka", None, None, "orb", None)
    return jax.shard_map(
        per_device, mesh=mesh, in_specs=in_specs, out_specs=out_specs, check_vma=False
    )
```

time: 377 us -> 222 us (0.59)
  other arithmetic: 72.5 us -> 9.29 us
  local copies, waits for them, and re-layouts: 83.2 us -> 25.9 us
  Pallas kernels: 0 us -> 35.4 us
  matrix products: 28.1 us -> 0 us
  waiting for transfers between devices: 128 us -> 111 us
  between operations: 13.6 us -> 0.59 us
  starting transfers between devices: 50.6 us -> 39 us
    all_to_all x3 -> x0, waiting for transfers between devices: 117 us -> none  [the longest x1 79.7 us: per_device(): lax.all_to_all(coeffs, 'ka', split_axis=1, concat_axis=0, tiled=True)]
    ppermute x2 -> x35, waiting for transfers between devices: 1.81 us -> 111 us  [send(): lax.ppermute(x, ('ka', 'orb'), [(a, flat(*b)) for a, b in moves if b is n...]
    all_to_all x3 -> x0, starting transfers between devices: 47.7 us -> none  [the longest x2 39.4 us: fetch_bra(): lax.all_to_all(jnp.take(spread_rows, matched_order, axis=0), 'ka', split_...]
    ppermute x2 -> x35, starting transfers between devices: 2.61 us -> 39 us  [send(): lax.ppermute(x, ('ka', 'orb'), [(a, flat(*b)) for a, b in moves if b is n...]
    pallas_call x0 -> x3, Pallas kernels: none -> 35.4 us  [the longest x2 23.1 us: ket_images(): pl.pallas_call(functools.partial(image_kernel, *places), in_specs=[pl.Blo...]
    another operation x3 -> x6, other arithmetic: 31.1 us -> 1.66 us  [the longest x4 1.37 us: ends(): jnp.stack([lax.dynamic_slice_in_dim(after(x, *arrived), start, reach, 1)...]
    dot_general x2 -> x0, matrix products: 28.1 us -> none  [the longest x1 21 us: per_device(): jnp.einsum('qistu,kisuc->qkitc', perturbation, phased, preferred_element_...]
    select_n x3 -> x6, other arithmetic: 32.1 us -> 4.88 us  [the longest x2 4.57 us: trade(): jnp.where(is_home, came, kept)]
  transfers between devices with their start and end apart: 6 -> 35, of which waited for: 4 -> 17; matrix products, arithmetic and copies ran while one was open for 36% -> 10% of each run, Pallas kernels for 0% -> 10%
where the time goes in v3:
time: 222 us
  waiting for transfers between devices  111 us (50%)
  starting transfers between devices  39 us (18%)
  Pallas kernels  35.4 us (16%)
  local copies, waits for them, and re-layouts  25.9 us (12%)
  other arithmetic  9.29 us (4%)
    ppermute x35, waiting for transfers between devices, send(): lax.ppermute(x, ('ka', 'orb'), [(a, flat(*b)) for a, b in moves if b is n...  111 us
    ppermute x35, starting transfers between devices, send(): lax.ppermute(x, ('ka', 'orb'), [(a, flat(*b)) for a, b in moves if b is n...  39 us
    pallas_call x2, Pallas kernels, ket_images(): pl.pallas_call(functools.partial(image_kernel, *places), in_specs=[pl.Blo...  23.1 us
    pallas_call x1, Pallas kernels, products(): pl.pallas_call(functools.partial(product_kernel, groups, places), in_spec...  12.3 us
    slice x8, local copies, waits for them, and re-layouts, second_hops(): arrays[array][place:place + 1]  5.62 us
    unnamed x66, local copies, waits for them, and re-layouts  5.39 us
    dynamic_slice x1, local copies, waits for them, and re-layouts, trade_weights(): lax.dynamic_slice_in_dim(after(perturbation, *arrived), first_sent, block...  4.99 us
    select_n x2, other arithmetic, trade(): jnp.where(is_home, came, kept)  4.57 us
  transfers between devices with their start and end apart: 35, of which 17 were waited for; matrix products, arithmetic and copies ran while one was open for 10% of the time, Pallas kernels for 10%

profile of v3, /device:TPU:0, one launch (start us, length us, event | category | flops | bytes accessed | tf_op | source)
XLA Modules:
  0.0 221.7 jit_solution(16230025846255875219)
XLA Ops:
  0.0 1.3 dynamic-slice_bitcast_fusion.1
  1.8 2.3 %collective-permute-done.3 = bf16[2,1024,256]{2,1,0:T(8,128)(2,1)S(1)} collective-permute-done((bf16[2,1024,256]{2,1,0:T(8,128)(2,1)S(1)}, bf16[2,1024,256]{2,1,0:T(8,128)(2,1)S(1)}, u32[]{:S(2)}, u32[]{:S(2)}) %collective-permute-start.3) | collective-permute-done | bytes 1048608 | tf_op jit(solution)/shard_map/ppermute | solution.py:264
  4.1 1.4 bitcast_select_fusion
  5.5 3.0 %dynamic-slice_bitcast_fusion = bf16[2,1024,256]{2,1,0:T(8,128)(2,1)} fusion(s32[]{:T(128)S(6)} %select_n.316, s32[]{:T(128)S(6)} %select_n.311, bf16[2,2,2,1024,256]{4,3,2,1,0:T(8,128)(2,1)} %bitcast.64), kind=kLoop, calls=%fused_computation.10 | loop fusion | bytes 2097160 | tf_op jit(solution)/shard_map/jit(dynamic_index_in_dim)/squeeze | solution.py:276
  8.9 2.6 %collective-permute-start.10 = (bf16[2,1024,256]{2,1,0:T(8,128)(2,1)S(1)}, bf16[2,1024,256]{2,1,0:T(8,128)(2,1)S(1)}, u32[]{:S(2)}, u32[]{:S(2)}) collective-permute-start(bf16[2,1024,256]{2,1,0:T(8,128)(2,1)S(1)} %get-tuple-element.55.refs_2_.refs_4_), channel_id=1, source_target_pairs={{0,2},{1,3},{2,0},{3,1},{4,6},{5,7},{6,4},{7,5},{8,10},{9,11},{10,... | collective-permute-start | bytes 3145736 | tf_op jit(solution)/shard_map/ppermute | solution.py:264
  11.5 1.5 collective-permute-start.11
  13.2 1.2 collective-permute-done
  14.5 2.7 %collective-permute-start.5 = (bf16[1,1024,256]{2,1,0:T(8,128)(2,1)S(1)}, bf16[1,1024,256]{2,1,0:T(8,128)(2,1)S(1)}, u32[]{:S(2)}, u32[]{:S(2)}) collective-permute-start(bf16[1,1024,256]{2,1,0:T(8,128)(2,1)S(1)} %slice.87), channel_id=1, source_target_pairs={{0,16},{1,17},{2,18},{3,19},{4,20},{5,21},{6,22},{7,23},{8,24},{9,... | collective-permute-start | bytes 1572872 | tf_op jit(solution)/shard_map/ppermute | solution.py:264
  17.2 3.2 %bitcast_select_fusion.2 = (bf16[2,1024,256]{2,1,0:T(8,128)(2,1)}, bf16[2,1024,256]{2,1,0:T(8,128)(2,1)}) fusion(bf16[2,1024,256]{2,1,0:T(8,128)(2,1)} %collective-permute-done.4, pred[]{:T(512)S(6)} %eq.37, s32[]{:T(128)S(6)} %select_n.316, s32[]{:T(128)S(6)} %select_n.309, bf16[2,2,2,1024,256]{4,3,2,1,0:T(8,128)(2,1)} %bitcast.65), kind=kLoop, calls=%fused_computation.8 | loop fusion | flops 1048576 | bytes 4194313 | tf_op jit(solution)/shard_map/jit(_where)/select_n | solution.py:305
  20.4 1.6 collective-permute-start.9
  21.9 13.3 %collective-permute-done.10.refs_5_ = bf16[2,1024,256]{2,1,0:T(8,128)(2,1)S(1)} collective-permute-done((bf16[2,1024,256]{2,1,0:T(8,128)(2,1)S(1)}, bf16[2,1024,256]{2,1,0:T(8,128)(2,1)S(1)}, u32[]{:S(2)}, u32[]{:S(2)}) %collective-permute-start.10) | collective-permute-done | bytes 1048608 | tf_op jit(solution)/shard_map/ppermute | solution.py:264
  36.4 4.4 %collective-permute-done.5 = bf16[1,1024,256]{2,1,0:T(8,128)(2,1)S(1)} collective-permute-done((bf16[1,1024,256]{2,1,0:T(8,128)(2,1)S(1)}, bf16[1,1024,256]{2,1,0:T(8,128)(2,1)S(1)}, u32[]{:S(2)}, u32[]{:S(2)}) %collective-permute-start.5) | collective-permute-done | bytes 524320 | tf_op jit(solution)/shard_map/ppermute | solution.py:264
  41.6 1.9 slice.109
  44.0 1.9 slice.88
  46.0 8.1 %collective-permute-done.12.refs_7_ = bf16[1,1024,256]{2,1,0:T(8,128)(2,1)S(1)} collective-permute-done((bf16[1,1024,256]{2,1,0:T(8,128)(2,1)}, bf16[1,1024,256]{2,1,0:T(8,128)(2,1)S(1)}, u32[]{:S(2)}, u32[]{:S(2)}) %collective-permute-start.12) | collective-permute-done | bytes 524320 | tf_op jit(solution)/shard_map/ppermute | solution.py:264
  54.1 2.7 %collective-permute-done.13.refs_8_ = bf16[1,1024,256]{2,1,0:T(8,128)(2,1)S(1)} collective-permute-done((bf16[1,1024,256]{2,1,0:T(8,128)(2,1)}, bf16[1,1024,256]{2,1,0:T(8,128)(2,1)S(1)}, u32[]{:S(2)}, u32[]{:S(2)}) %collective-permute-start.13) | collective-permute-done | bytes 524320 | tf_op jit(solution)/shard_map/ppermute | solution.py:264
  56.8 5.0 %constant_dynamic-slice_fusion = bf16[2,8,8,128,128]{4,3,2,1,0:T(8,128)(2,1)} fusion(bf16[2,32,8,128,128]{4,3,2,1,0:T(8,128)(2,1)} %refs_6_.3, s32[]{:T(128)S(6)} %select_n.324), kind=kLoop, calls=%fused_computation.43 | loop fusion | bytes 8388612 | tf_op jit(solution)/shard_map/dynamic_slice | solution.py:328
  61.8 9.4 %collective-permute-done.6 = bf16[1,1024,256]{2,1,0:T(8,128)(2,1)} collective-permute-done((bf16[1,1024,256]{2,1,0:T(8,128)(2,1)}, bf16[1,1024,256]{2,1,0:T(8,128)(2,1)}, u32[]{:S(2)}, u32[]{:S(2)}) %collective-permute-start.6) | collective-permute-done | bytes 524320 | tf_op jit(solution)/shard_map/ppermute | solution.py:264
  71.2 1.5 collective-permute-start.14
  73.7 1.4 collective-permute-start.1
  76.1 2.9 %collective-permute-start.7 = (bf16[1,1024,256]{2,1,0:T(8,128)(2,1)S(1)}, bf16[1,1024,256]{2,1,0:T(8,128)(2,1)S(1)}, u32[]{:S(2)}, u32[]{:S(2)}) collective-permute-start(bf16[1,1024,256]{2,1,0:T(8,128)(2,1)S(1)} %slice.89), channel_id=1, source_target_pairs={{0,24},{1,25},{2,26},{3,27},{4,28},{5,29},{6,30},{7,31},{8,16},{9,... | collective-permute-start | bytes 1572872 | tf_op jit(solution)/shard_map/ppermute | solution.py:264
  79.0 15.3 %collective-permute-done.14.refs_10_ = bf16[2,1024,256]{2,1,0:T(8,128)(2,1)S(1)} collective-permute-done((bf16[2,1024,256]{2,1,0:T(8,128)(2,1)S(1)}, bf16[2,1024,256]{2,1,0:T(8,128)(2,1)S(1)}, u32[]{:S(2)}, u32[]{:S(2)}) %collective-permute-start.14) | collective-permute-done | bytes 1048608 | tf_op jit(solution)/shard_map/ppermute | solution.py:264
  95.1 1.8 collective-permute-done.15.refs_11_
  98.1 4.5 %collective-permute-done.2 = s32[2,2]{1,0:T(2,128)S(1)} collective-permute-done((s32[2,2]{1,0:T(2,128)S(1)}, s32[2,2]{1,0:T(2,128)S(1)}, u32[]{:S(2)}, u32[]{:S(2)}) %collective-permute-start.2) | collective-permute-done | bytes 48 | tf_op jit(solution)/shard_map/ppermute | solution.py:264
  102.7 1.3 pad_maximum_fusion.1.refs_3_.refs_14_
  104.0 1.5 slice.90
  105.5 5.1 %collective-permute-start.8 = (bf16[1,1024,256]{2,1,0:T(8,128)(2,1)S(1)}, bf16[1,1024,256]{2,1,0:T(8,128)(2,1)S(1)}, u32[]{:S(2)}, u32[]{:S(2)}) collective-permute-start(bf16[1,1024,256]{2,1,0:T(8,128)(2,1)S(1)} %slice.90), channel_id=1, source_target_pairs={{0,24},{1,25},{2,26},{3,27},{4,28},{5,29},{6,30},{7,31},{8,16},{9,... | collective-permute-start | bytes 1572872 | tf_op jit(solution)/shard_map/ppermute | solution.py:264
  110.5 1.4 collective-permute-start.16
  111.9 1.2 collective-permute-start.17
  114.3 4.9 %collective-permute-done.8 = bf16[1,1024,256]{2,1,0:T(8,128)(2,1)S(1)} collective-permute-done((bf16[1,1024,256]{2,1,0:T(8,128)(2,1)S(1)}, bf16[1,1024,256]{2,1,0:T(8,128)(2,1)S(1)}, u32[]{:S(2)}, u32[]{:S(2)}) %collective-permute-start.8) | collective-permute-done | bytes 524320 | tf_op jit(solution)/shard_map/ppermute | solution.py:264
  120.2 11.5 %collective-permute-done.16.refs_15_ = bf16[2,1024,256]{2,1,0:T(8,128)(2,1)S(1)} collective-permute-done((bf16[2,1024,256]{2,1,0:T(8,128)(2,1)S(1)}, bf16[2,1024,256]{2,1,0:T(8,128)(2,1)S(1)}, u32[]{:S(2)}, u32[]{:S(2)}) %collective-permute-start.16) | collective-permute-done | bytes 1048608 | tf_op jit(solution)/shard_map/ppermute | solution.py:264
  132.3 1.2 collective-permute-start.27
  133.5 1.2 collective-permute-start.28
  136.3 1.7 collective-permute-start.18
  138.1 19.2 %collective-permute-done.27.refs_20_ = bf16[2,1024,256]{2,1,0:T(8,128)(2,1)S(1)} collective-permute-done((bf16[2,1024,256]{2,1,0:T(8,128)(2,1)S(1)}, bf16[2,1024,256]{2,1,0:T(8,128)(2,1)S(1)}, u32[]{:S(2)}, u32[]{:S(2)}) %collective-permute-start.27) | collective-permute-done | bytes 1048608 | tf_op jit(solution)/shard_map/ppermute | solution.py:264
  157.3 1.2 collective-permute-start.25
  161.0 11.5 %ket_images.3 = (bf16[2,2,1024,256]{3,2,1,0:T(8,128)(2,1)}, bf16[2,2,1024,256]{3,2,1,0:T(8,128)(2,1)}) custom-call(s32[3]{0:T(128)S(1)} %pad_add_fusion.3.where, s32[8,8]{1,0:T(8,128)S(1)} %get-tuple-element.93.columns, f32[4,8,8]{2,1,0:T(8,128)S(1)} %get-tuple-element.95.cosine, f32[4,8,8]{2,1,0:T(8,128)S(1)} %get-tuple-element.94.sine, ...), custom_call_target="tpu_custom_call" | custom-call | flops 4294967296 | bytes 14680064 | tf_op jit(solution)/shard_map/ket_images/pallas_call | solution.py:149
  174.2 1.2 collective-permute-start.29
  175.4 1.1 collective-permute-start.30
  177.4 1.2 copy-done.6
  178.6 1.2 copy-done.8
  179.9 11.6 %ket_images.2 = (bf16[2,2,1024,256]{3,2,1,0:T(8,128)(2,1)}, bf16[2,2,1024,256]{3,2,1,0:T(8,128)(2,1)}) custom-call(s32[3]{0:T(128)S(1)} %pad_add_fusion.3.where, s32[8,8]{1,0:T(8,128)S(1)} %get-tuple-element.93.columns, f32[4,8,8]{2,1,0:T(8,128)S(1)} %get-tuple-element.98.cosine, f32[4,8,8]{2,1,0:T(8,128)S(1)} %get-tuple-element.99.sine, ...), custom_call_target="tpu_custom_call" | custom-call | flops 4294967296 | bytes 14680064 | tf_op jit(solution)/shard_map/ket_images/pallas_call | solution.py:149
  191.6 12.3 %products.1 = (f32[16,2,64,128]{3,2,1,0:T(8,128)S(1)}, f32[16,2,64,128]{3,2,1,0:T(8,128)}) custom-call(s32[16]{0:T(128)S(1)} %pad_add_fusion.2.choice, s32[1]{0:T(128)} %bitcast.4.where, bf16[2,2,1024,256]{3,2,1,0:T(8,128)(2,1)} %get-tuple-element.60.refs_0_, bf16[2,2,1024,256]{3,2,1,0:T(8,128)(2,1)} %get-tuple-element.63.refs_1_, ...), custom_call_target="tpu_custom_call" | custom-call | flops 2147483648 | bytes 16777216 | tf_op jit(solution)/shard_map/products/pallas_call | solution.py:221
  204.0 2.9 %collective-permute-done.31 = f32[16,2,64,128]{3,2,1,0:T(8,128)S(1)} collective-permute-done((f32[16,2,64,128]{3,2,1,0:T(8,128)}, f32[16,2,64,128]{3,2,1,0:T(8,128)S(1)}, u32[]{:S(2)}, u32[]{:S(2)}) %collective-permute-start.31) | collective-permute-done | bytes 1048608 | tf_op jit(solution)/shard_map/ppermute | solution.py:264
  207.2 3.1 %collective-permute-start.34 = (bf16[2,2,2,64,128]{4,3,2,1,0:T(8,128)(2,1)S(1)}, bf16[2,2,2,64,128]{4,3,2,1,0:T(8,128)(2,1)S(1)}, u32[]{:S(2)}, u32[]{:S(2)}) collective-permute-start(bf16[2,2,2,64,128]{4,3,2,1,0:T(8,128)(2,1)S(1)} %bitcast.69), channel_id=1, source_target_pairs={{0,24},{1,25},{2,26},{3,27},{4,28},{5,29},{6,30},{7,31},{8,16},{9,... | collective-permute-start | bytes 393224 | tf_op jit(solution)/shard_map/ppermute | solution.py:264
  210.3 1.3 collective-permute-start.32
  211.6 3.8 %collective-permute-done.34 = bf16[2,2,2,64,128]{4,3,2,1,0:T(8,128)(2,1)S(1)} collective-permute-done((bf16[2,2,2,64,128]{4,3,2,1,0:T(8,128)(2,1)S(1)}, bf16[2,2,2,64,128]{4,3,2,1,0:T(8,128)(2,1)S(1)}, u32[]{:S(2)}, u32[]{:S(2)}) %collective-permute-start.34) | collective-permute-done | bytes 131104 | tf_op jit(solution)/shard_map/ppermute | solution.py:264
  215.5 5.5 %collective-permute-done.33 = bf16[2,2,2,64,128]{4,3,2,1,0:T(8,128)(2,1)S(1)} collective-permute-done((bf16[2,2,2,64,128]{4,3,2,1,0:T(8,128)(2,1)S(1)}, bf16[2,2,2,64,128]{4,3,2,1,0:T(8,128)(2,1)S(1)}, u32[]{:S(2)}, u32[]{:S(2)}) %collective-permute-start.33) | collective-permute-done | bytes 131104 | tf_op jit(solution)/shard_map/ppermute | solution.py:264
  (145 shorter events, 18.2 us)
Async XLA Ops:
  0.0 13.1 %copy-start.30 = (s32[3,32,8]{1,2,0:T(8,128)S(1)}, s32[3,32,8]{1,2,0:T(8,128)}, u32[]{:S(2)}) copy-start(s32[3,32,8]{1,2,0:T(8,128)} %param.9) | copy-start | bytes 9220
  0.0 13.1 %copy-start.31 = (s32[32,8]{0,1:T(8,128)S(1)}, s32[32,8]{0,1:T(8,128)}, u32[]{:S(2)}) copy-start(s32[32,8]{0,1:T(8,128)} %param.8) | copy-start | bytes 3076
  1.3 2.8 %collective-permute-start.3 = (bf16[2,1024,256]{2,1,0:T(8,128)(2,1)S(1)}, bf16[2,1024,256]{2,1,0:T(8,128)(2,1)S(1)}, u32[]{:S(2)}, u32[]{:S(2)}) collective-permute-start(bf16[2,1024,256]{2,1,0:T(8,128)(2,1)S(1)} %dynamic-slice_bitcast_fusion.1), channel_id=1, source_target_pairs={{0,1},{1,0},{2,3},{3,2},{4,5},{5,4},{6,7},{7,6},{8,9},{9,8},{10,11... | collective-permute-start | bytes 3145736 | tf_op jit(solution)/shard_map/ppermute | solution.py:264
  5.5 14.9 %copy-start.21 = (bf16[2,1024,256]{2,1,0:T(8,128)(2,1)}, bf16[2,1024,256]{2,1,0:T(8,128)(2,1)S(1)}, u32[]{:S(2)}) copy-start(bf16[2,1024,256]{2,1,0:T(8,128)(2,1)S(1)} %get-tuple-element.45) | copy-start | bytes 3145732
  5.5 171.9 %copy-start = (bf16[2,1024,256]{2,1,0:T(8,128)(2,1)}, bf16[2,1024,256]{2,1,0:T(8,128)(2,1)S(1)}, u32[]{:S(2)}) copy-start(bf16[2,1024,256]{2,1,0:T(8,128)(2,1)S(1)} %get-tuple-element.55.refs_2_.refs_4_) | copy-start | bytes 3145732
  8.5 8.6 %collective-permute-start.4 = (bf16[2,1024,256]{2,1,0:T(8,128)(2,1)}, bf16[2,1024,256]{2,1,0:T(8,128)(2,1)}, u32[]{:S(2)}, u32[]{:S(2)}) collective-permute-start(bf16[2,1024,256]{2,1,0:T(8,128)(2,1)} %dynamic-slice_bitcast_fusion), channel_id=1, source_target_pairs={{0,1},{1,0},{2,3},{3,2},{4,5},{5,4},{6,7},{7,6},{8,9},{9,8},{10,11... | collective-permute-start | bytes 3145736 | tf_op jit(solution)/shard_map/ppermute | solution.py:264
  8.9 26.3 %collective-permute-start.10 = (bf16[2,1024,256]{2,1,0:T(8,128)(2,1)S(1)}, bf16[2,1024,256]{2,1,0:T(8,128)(2,1)S(1)}, u32[]{:S(2)}, u32[]{:S(2)}) collective-permute-start(bf16[2,1024,256]{2,1,0:T(8,128)(2,1)S(1)} %get-tuple-element.55.refs_2_.refs_4_), channel_id=1, source_target_pairs={{0,2},{1,3},{2,0},{3,1},{4,6},{5,7},{6,4},{7,5},{8,10},{9,11},{10,... | collective-permute-start | bytes 3145736 | tf_op jit(solution)/shard_map/ppermute | solution.py:264
  11.5 29.8 %collective-permute-start.11 = (bf16[2,1024,256]{2,1,0:T(8,128)(2,1)S(1)}, bf16[2,1024,256]{2,1,0:T(8,128)(2,1)}, u32[]{:S(2)}, u32[]{:S(2)}) collective-permute-start(bf16[2,1024,256]{2,1,0:T(8,128)(2,1)S(1)} %get-tuple-element.55.refs_2_.refs_4_), channel_id=1, source_target_pairs={{0,4},{1,5},{2,6},{3,7},{4,0},{5,1},{6,2},{7,3},{8,12},{9,13},{10,... | collective-permute-start | bytes 3145736 | tf_op jit(solution)/shard_map/ppermute | solution.py:264
  13.2 1.3 collective-permute-start
  14.5 26.3 %collective-permute-start.5 = (bf16[1,1024,256]{2,1,0:T(8,128)(2,1)S(1)}, bf16[1,1024,256]{2,1,0:T(8,128)(2,1)S(1)}, u32[]{:S(2)}, u32[]{:S(2)}) collective-permute-start(bf16[1,1024,256]{2,1,0:T(8,128)(2,1)S(1)} %slice.87), channel_id=1, source_target_pairs={{0,16},{1,17},{2,18},{3,19},{4,20},{5,21},{6,22},{7,23},{8,24},{9,... | collective-permute-start | bytes 1572872 | tf_op jit(solution)/shard_map/ppermute | solution.py:264
  20.4 41.4 %collective-permute-start.9 = (bf16[2,1024,256]{2,1,0:T(8,128)(2,1)}, bf16[2,1024,256]{2,1,0:T(8,128)(2,1)S(1)}, u32[]{:S(2)}, u32[]{:S(2)}) collective-permute-start(bf16[2,1024,256]{2,1,0:T(8,128)(2,1)} %get-tuple-element.48), channel_id=1, source_target_pairs={{0,8},{1,9},{2,10},{3,11},{4,12},{5,13},{6,14},{7,15},{8,0},{9,1},... | collective-permute-start | bytes 3145736 | tf_op jit(solution)/shard_map/ppermute | solution.py:264
  40.8 13.3 %collective-permute-start.12 = (bf16[1,1024,256]{2,1,0:T(8,128)(2,1)}, bf16[1,1024,256]{2,1,0:T(8,128)(2,1)S(1)}, u32[]{:S(2)}, u32[]{:S(2)}) collective-permute-start(bf16[1,1024,256]{2,1,0:T(8,128)(2,1)} %slice.108), channel_id=1, source_target_pairs={{0,4},{1,5},{2,6},{3,7},{4,0},{5,1},{6,2},{7,3},{8,12},{9,13},{10,... | collective-permute-start | bytes 1572872 | tf_op jit(solution)/shard_map/ppermute | solution.py:264
  43.5 13.3 %collective-permute-start.13 = (bf16[1,1024,256]{2,1,0:T(8,128)(2,1)}, bf16[1,1024,256]{2,1,0:T(8,128)(2,1)S(1)}, u32[]{:S(2)}, u32[]{:S(2)}) collective-permute-start(bf16[1,1024,256]{2,1,0:T(8,128)(2,1)} %slice.109), channel_id=1, source_target_pairs={{0,2},{1,3},{2,0},{3,1},{4,6},{5,7},{6,4},{7,5},{8,10},{9,11},{10,... | collective-permute-start | bytes 1572872 | tf_op jit(solution)/shard_map/ppermute | solution.py:264
  45.9 25.3 %collective-permute-start.6 = (bf16[1,1024,256]{2,1,0:T(8,128)(2,1)}, bf16[1,1024,256]{2,1,0:T(8,128)(2,1)}, u32[]{:S(2)}, u32[]{:S(2)}) collective-permute-start(bf16[1,1024,256]{2,1,0:T(8,128)(2,1)} %slice.88), channel_id=1, source_target_pairs={{0,16},{1,17},{2,18},{3,19},{4,20},{5,21},{6,22},{7,23},{8,24},{9,... | collective-permute-start | bytes 1572872 | tf_op jit(solution)/shard_map/ppermute | solution.py:264
  46.0 27.7 %copy-start.32 = (s32[2]{0:T(128)S(1)}, s32[2]{0:T(128)}, u32[]{:S(2)}) copy-start(s32[2]{0:T(128)} %param.10) | copy-start | bytes 28
  61.8 99.2 %collective-permute-start.23 = (bf16[2,8,8,128,128]{4,3,2,1,0:T(8,128)(2,1)}, bf16[2,8,8,128,128]{4,3,2,1,0:T(8,128)(2,1)}, u32[]{:S(2)}, u32[]{:S(2)}) collective-permute-start(bf16[2,8,8,128,128]{4,3,2,1,0:T(8,128)(2,1)} %constant_dynamic-slice_fusion), channel_id=1, source_target_pairs={{0,1},{1,0},{2,3},{3,2},{4,5},{5,4},{6,7},{7,6},{8,9},{9,8},{10,11... | collective-permute-start | bytes 12582920 | tf_op jit(solution)/shard_map/ppermute | solution.py:264
  61.8 51.4 %copy-start.3 = (bf16[2,1024,256]{2,1,0:T(8,128)(2,1)}, bf16[2,1024,256]{2,1,0:T(8,128)(2,1)S(1)}, u32[]{:S(2)}) copy-start(bf16[2,1024,256]{2,1,0:T(8,128)(2,1)S(1)} %collective-permute-done.9.refs_2_.refs_9_) | copy-start | bytes 3145732
  71.2 23.2 %collective-permute-start.14 = (bf16[2,1024,256]{2,1,0:T(8,128)(2,1)S(1)}, bf16[2,1024,256]{2,1,0:T(8,128)(2,1)S(1)}, u32[]{:S(2)}, u32[]{:S(2)}) collective-permute-start(bf16[2,1024,256]{2,1,0:T(8,128)(2,1)S(1)} %collective-permute-done.9.refs_2_.refs_9_), channel_id=1, source_target_pairs={{0,2},{1,3},{2,0},{3,1},{4,6},{5,7},{6,4},{7,5},{8,10},{9,11},{10,... | collective-permute-start | bytes 3145736 | tf_op jit(solution)/shard_map/ppermute | solution.py:264
  72.7 24.2 %collective-permute-start.15 = (bf16[2,1024,256]{2,1,0:T(8,128)(2,1)S(1)}, bf16[2,1024,256]{2,1,0:T(8,128)(2,1)}, u32[]{:S(2)}, u32[]{:S(2)}) collective-permute-start(bf16[2,1024,256]{2,1,0:T(8,128)(2,1)S(1)} %collective-permute-done.9.refs_2_.refs_9_), channel_id=1, source_target_pairs={{0,4},{1,5},{2,6},{3,7},{4,0},{5,1},{6,2},{7,3},{8,12},{9,13},{10,... | collective-permute-start | bytes 3145736 | tf_op jit(solution)/shard_map/ppermute | solution.py:264
  73.7 24.3 %collective-permute-start.1 = (s32[1,2]{1,0:T(1,128)S(1)}, s32[1,2]{1,0:T(1,128)S(1)}, u32[]{:S(2)}, u32[]{:S(2)}) collective-permute-start(s32[1,2]{1,0:T(1,128)S(1)} %bitcast.71), channel_id=1, source_target_pairs={{0,8},{1,9},{2,10},{3,11},{4,12},{5,13},{6,14},{7,15},{8,0},{9,1},... | collective-permute-start | bytes 32 | tf_op jit(solution)/shard_map/ppermute | solution.py:264
  76.1 27.9 %collective-permute-start.7 = (bf16[1,1024,256]{2,1,0:T(8,128)(2,1)S(1)}, bf16[1,1024,256]{2,1,0:T(8,128)(2,1)S(1)}, u32[]{:S(2)}, u32[]{:S(2)}) collective-permute-start(bf16[1,1024,256]{2,1,0:T(8,128)(2,1)S(1)} %slice.89), channel_id=1, source_target_pairs={{0,24},{1,25},{2,26},{3,27},{4,28},{5,29},{6,30},{7,31},{8,16},{9,... | collective-permute-start | bytes 1572872 | tf_op jit(solution)/shard_map/ppermute | solution.py:264
  94.4 17.5 %collective-permute-start.19 = (bf16[1,1024,256]{2,1,0:T(8,128)(2,1)S(1)}, bf16[1,1024,256]{2,1,0:T(8,128)(2,1)S(1)}, u32[]{:S(2)}, u32[]{:S(2)}) collective-permute-start(bf16[1,1024,256]{2,1,0:T(8,128)(2,1)S(1)} %slice.110), channel_id=1, source_target_pairs={{0,4},{1,5},{2,6},{3,7},{4,0},{5,1},{6,2},{7,3},{8,12},{9,13},{10,... | collective-permute-start | bytes 1572872 | tf_op jit(solution)/shard_map/ppermute | solution.py:264
  98.0 15.2 %collective-permute-start.20 = (bf16[1,1024,256]{2,1,0:T(8,128)(2,1)S(1)}, bf16[1,1024,256]{2,1,0:T(8,128)(2,1)S(1)}, u32[]{:S(2)}, u32[]{:S(2)}) collective-permute-start(bf16[1,1024,256]{2,1,0:T(8,128)(2,1)S(1)} %slice.111), channel_id=1, source_target_pairs={{0,2},{1,3},{2,0},{3,1},{4,6},{5,7},{6,4},{7,5},{8,10},{9,11},{10,... | collective-permute-start | bytes 1572872 | tf_op jit(solution)/shard_map/ppermute | solution.py:264
  98.1 4.5 %collective-permute-start.2 = (s32[2,2]{1,0:T(2,128)S(1)}, s32[2,2]{1,0:T(2,128)S(1)}, u32[]{:S(2)}, u32[]{:S(2)}) collective-permute-start(s32[2,2]{1,0:T(2,128)S(1)} %pad_add_fusion.1), channel_id=1, source_target_pairs={{0,16},{1,17},{2,18},{3,19},{4,20},{5,21},{6,22},{7,23},{8,24},{9,... | collective-permute-start | bytes 56 | tf_op jit(solution)/shard_map/ppermute | solution.py:264
  104.0 73.4 %copy-start.1 = (bf16[2,1024,256]{2,1,0:T(8,128)(2,1)}, bf16[2,1024,256]{2,1,0:T(8,128)(2,1)S(1)}, u32[]{:S(2)}) copy-start(bf16[2,1024,256]{2,1,0:T(8,128)(2,1)S(1)} %pad_maximum_fusion.1.refs_3_.refs_14_) | copy-start | bytes 3145732
  105.5 13.8 %collective-permute-start.8 = (bf16[1,1024,256]{2,1,0:T(8,128)(2,1)S(1)}, bf16[1,1024,256]{2,1,0:T(8,128)(2,1)S(1)}, u32[]{:S(2)}, u32[]{:S(2)}) collective-permute-start(bf16[1,1024,256]{2,1,0:T(8,128)(2,1)S(1)} %slice.90), channel_id=1, source_target_pairs={{0,24},{1,25},{2,26},{3,27},{4,28},{5,29},{6,30},{7,31},{8,16},{9,... | collective-permute-start | bytes 1572872 | tf_op jit(solution)/shard_map/ppermute | solution.py:264
  110.5 21.2 %collective-permute-start.16 = (bf16[2,1024,256]{2,1,0:T(8,128)(2,1)S(1)}, bf16[2,1024,256]{2,1,0:T(8,128)(2,1)S(1)}, u32[]{:S(2)}, u32[]{:S(2)}) collective-permute-start(bf16[2,1024,256]{2,1,0:T(8,128)(2,1)S(1)} %pad_maximum_fusion.1.refs_3_.refs_14_), channel_id=1, source_target_pairs={{0,2},{1,3},{2,0},{3,1},{4,6},{5,7},{6,4},{7,5},{8,10},{9,11},{10,... | collective-permute-start | bytes 3145736 | tf_op jit(solution)/shard_map/ppermute | solution.py:264
  111.9 20.3 %collective-permute-start.17 = (bf16[2,1024,256]{2,1,0:T(8,128)(2,1)S(1)}, bf16[2,1024,256]{2,1,0:T(8,128)(2,1)S(1)}, u32[]{:S(2)}, u32[]{:S(2)}) collective-permute-start(bf16[2,1024,256]{2,1,0:T(8,128)(2,1)S(1)} %pad_maximum_fusion.1.refs_3_.refs_14_), channel_id=1, source_target_pairs={{0,4},{1,5},{2,6},{3,7},{4,0},{5,1},{6,2},{7,3},{8,12},{9,13},{10,... | collective-permute-start | bytes 3145736 | tf_op jit(solution)/shard_map/ppermute | solution.py:264
  114.0 20.9 %collective-permute-start.21 = (bf16[2,2,512,256]{3,2,1,0:T(8,128)(2,1)S(1)}, bf16[2,2,512,256]{3,2,1,0:T(8,128)(2,1)S(1)}, u32[]{:S(2)}, u32[]{:S(2)}) collective-permute-start(bf16[2,2,512,256]{3,2,1,0:T(8,128)(2,1)S(1)} %pad_maximum_fusion.3), channel_id=1, source_target_pairs={{0,1},{1,0},{2,3},{3,2},{4,5},{5,4},{6,7},{7,6},{8,9},{9,8},{10,11... | collective-permute-start | bytes 3145736 | tf_op jit(solution)/shard_map/ppermute | solution.py:264
  114.2 20.8 %copy-start.4 = (bf16[2,1024,256]{2,1,0:T(8,128)(2,1)S(1)}, bf16[2,1024,256]{2,1,0:T(8,128)(2,1)}, u32[]{:S(2)}) copy-start(bf16[2,1024,256]{2,1,0:T(8,128)(2,1)} %copy-done.3) | copy-start | bytes 3145732
  119.3 17.0 %collective-permute-start.24 = (bf16[2,2,512,256]{3,2,1,0:T(8,128)(2,1)S(1)}, bf16[2,2,512,256]{3,2,1,0:T(8,128)(2,1)S(1)}, u32[]{:S(2)}, u32[]{:S(2)}) collective-permute-start(bf16[2,2,512,256]{3,2,1,0:T(8,128)(2,1)S(1)} %pad_maximum_fusion.5), channel_id=1, source_target_pairs={{1,8},{3,10},{5,12},{7,14},{8,1},{9,16},{10,3},{11,18},{12,5},{13,... | collective-permute-start | bytes 3145736 | tf_op jit(solution)/shard_map/ppermute | solution.py:264
  120.2 40.8 %copy-start.2 = (bf16[2,1024,256]{2,1,0:T(8,128)(2,1)}, bf16[2,1024,256]{2,1,0:T(8,128)(2,1)S(1)}, u32[]{:S(2)}) copy-start(bf16[2,1024,256]{2,1,0:T(8,128)(2,1)S(1)} %pad_maximum_fusion.refs_3_.refs_19_) | copy-start | bytes 3145732
  132.3 25.0 %collective-permute-start.27 = (bf16[2,1024,256]{2,1,0:T(8,128)(2,1)S(1)}, bf16[2,1024,256]{2,1,0:T(8,128)(2,1)S(1)}, u32[]{:S(2)}, u32[]{:S(2)}) collective-permute-start(bf16[2,1024,256]{2,1,0:T(8,128)(2,1)S(1)} %pad_maximum_fusion.refs_3_.refs_19_), channel_id=1, source_target_pairs={{0,2},{1,3},{2,0},{3,1},{4,6},{5,7},{6,4},{7,5},{8,10},{9,11},{10,... | collective-permute-start | bytes 3145736 | tf_op jit(solution)/shard_map/ppermute | solution.py:264
  133.5 25.1 %collective-permute-start.28 = (bf16[2,1024,256]{2,1,0:T(8,128)(2,1)S(1)}, bf16[2,1024,256]{2,1,0:T(8,128)(2,1)S(1)}, u32[]{:S(2)}, u32[]{:S(2)}) collective-permute-start(bf16[2,1024,256]{2,1,0:T(8,128)(2,1)S(1)} %pad_maximum_fusion.refs_3_.refs_19_), channel_id=1, source_target_pairs={{0,4},{1,5},{2,6},{3,7},{4,0},{5,1},{6,2},{7,3},{8,12},{9,13},{10,... | collective-permute-start | bytes 3145736 | tf_op jit(solution)/shard_map/ppermute | solution.py:264
  134.9 26.1 %copy-start.5 = (bf16[2,2,512,256]{3,2,1,0:T(8,128)(2,1)}, bf16[2,2,512,256]{3,2,1,0:T(8,128)(2,1)S(1)}, u32[]{:S(2)}) copy-start(bf16[2,2,512,256]{3,2,1,0:T(8,128)(2,1)S(1)} %collective-permute-done.21.refs_4_) | copy-start | bytes 3145732
  134.9 26.1 %collective-permute-start.22 = (bf16[2,2,512,256]{3,2,1,0:T(8,128)(2,1)S(1)}, bf16[2,2,512,256]{3,2,1,0:T(8,128)(2,1)S(1)}, u32[]{:S(2)}, u32[]{:S(2)}) collective-permute-start(bf16[2,2,512,256]{3,2,1,0:T(8,128)(2,1)S(1)} %pad_maximum_fusion.4), channel_id=1, source_target_pairs={{0,1},{1,0},{2,3},{3,2},{4,5},{5,4},{6,7},{7,6},{8,9},{9,8},{10,11... | collective-permute-start | bytes 3145736 | tf_op jit(solution)/shard_map/ppermute | solution.py:264
  136.3 41.1 %collective-permute-start.18 = (bf16[2,2,512,256]{3,2,1,0:T(8,128)(2,1)}, bf16[2,2,512,256]{3,2,1,0:T(8,128)(2,1)}, u32[]{:S(2)}, u32[]{:S(2)}) collective-permute-start(bf16[2,2,512,256]{3,2,1,0:T(8,128)(2,1)} %pad_maximum_fusion.2), channel_id=1, source_target_pairs={{1,8},{3,10},{5,12},{7,14},{8,1},{9,16},{10,3},{11,18},{12,5},{13,... | collective-permute-start | bytes 3145736 | tf_op jit(solution)/shard_map/ppermute | solution.py:264
  157.3 15.2 %copy-start.26 = (bf16[2,1024,256]{2,1,0:T(8,128)(2,1)}, bf16[2,1024,256]{2,1,0:T(8,128)(2,1)S(1)}, u32[]{:S(2)}) copy-start(bf16[2,1024,256]{2,1,0:T(8,128)(2,1)S(1)} %collective-permute-done.27.refs_20_) | copy-start | bytes 3145732
  157.3 15.2 %collective-permute-start.25 = (bf16[1,1024,256]{2,1,0:T(8,128)(2,1)S(1)}, bf16[1,1024,256]{2,1,0:T(8,128)(2,1)S(1)}, u32[]{:S(2)}, u32[]{:S(2)}) collective-permute-start(bf16[1,1024,256]{2,1,0:T(8,128)(2,1)S(1)} %slice.112), channel_id=1, source_target_pairs={{0,4},{1,5},{2,6},{3,7},{4,0},{5,1},{6,2},{7,3},{8,12},{9,13},{10,... | collective-permute-start | bytes 1572872 | tf_op jit(solution)/shard_map/ppermute | solution.py:264
  158.5 14.0 %copy-start.27 = (bf16[2,1024,256]{2,1,0:T(8,128)(2,1)}, bf16[2,1024,256]{2,1,0:T(8,128)(2,1)S(1)}, u32[]{:S(2)}) copy-start(bf16[2,1024,256]{2,1,0:T(8,128)(2,1)S(1)} %collective-permute-done.28.refs_21_) | copy-start | bytes 3145732
  158.5 14.8 %collective-permute-start.26 = (bf16[1,1024,256]{2,1,0:T(8,128)(2,1)S(1)}, bf16[1,1024,256]{2,1,0:T(8,128)(2,1)S(1)}, u32[]{:S(2)}, u32[]{:S(2)}) collective-permute-start(bf16[1,1024,256]{2,1,0:T(8,128)(2,1)S(1)} %slice.113), channel_id=1, source_target_pairs={{0,2},{1,3},{2,0},{3,1},{4,6},{5,7},{6,4},{7,5},{8,10},{9,11},{10,... | collective-permute-start | bytes 1572872 | tf_op jit(solution)/shard_map/ppermute | solution.py:264
  161.0 15.5 %copy-start.29 = (s32[2,32]{1,0:T(2,128)S(1)}, s32[2,32]{1,0:T(2,128)}, u32[]{:S(2)}) copy-start(s32[2,32]{1,0:T(2,128)} %param.11) | copy-start | bytes 772
  174.2 17.4 %collective-permute-start.29 = (bf16[1,1024,256]{2,1,0:T(8,128)(2,1)}, bf16[1,1024,256]{2,1,0:T(8,128)(2,1)S(1)}, u32[]{:S(2)}, u32[]{:S(2)}) collective-permute-start(bf16[1,1024,256]{2,1,0:T(8,128)(2,1)} %slice.114), channel_id=1, source_target_pairs={{0,4},{1,5},{2,6},{3,7},{4,0},{5,1},{6,2},{7,3},{8,12},{9,13},{10,... | collective-permute-start | bytes 1572872 | tf_op jit(solution)/shard_map/ppermute | solution.py:264
  175.4 16.1 %collective-permute-start.30 = (bf16[1,1024,256]{2,1,0:T(8,128)(2,1)}, bf16[1,1024,256]{2,1,0:T(8,128)(2,1)S(1)}, u32[]{:S(2)}, u32[]{:S(2)}) collective-permute-start(bf16[1,1024,256]{2,1,0:T(8,128)(2,1)} %slice.115), channel_id=1, source_target_pairs={{0,2},{1,3},{2,0},{3,1},{4,6},{5,7},{6,4},{7,5},{8,10},{9,11},{10,... | collective-permute-start | bytes 1572872 | tf_op jit(solution)/shard_map/ppermute | solution.py:264
  204.0 2.9 %collective-permute-start.31 = (f32[16,2,64,128]{3,2,1,0:T(8,128)}, f32[16,2,64,128]{3,2,1,0:T(8,128)S(1)}, u32[]{:S(2)}, u32[]{:S(2)}) collective-permute-start(f32[16,2,64,128]{3,2,1,0:T(8,128)} %get-tuple-element.72), channel_id=1, source_target_pairs={{0,1},{1,0},{2,3},{3,2},{4,5},{5,4},{6,7},{7,6},{8,9},{9,8},{10,11... | collective-permute-start | bytes 3145736 | tf_op jit(solution)/shard_map/ppermute | solution.py:264
  207.2 8.3 %collective-permute-start.34 = (bf16[2,2,2,64,128]{4,3,2,1,0:T(8,128)(2,1)S(1)}, bf16[2,2,2,64,128]{4,3,2,1,0:T(8,128)(2,1)S(1)}, u32[]{:S(2)}, u32[]{:S(2)}) collective-permute-start(bf16[2,2,2,64,128]{4,3,2,1,0:T(8,128)(2,1)S(1)} %bitcast.69), channel_id=1, source_target_pairs={{0,24},{1,25},{2,26},{3,27},{4,28},{5,29},{6,30},{7,31},{8,16},{9,... | collective-permute-start | bytes 393224 | tf_op jit(solution)/shard_map/ppermute | solution.py:264
  210.3 10.6 %collective-permute-start.33 = (bf16[2,2,2,64,128]{4,3,2,1,0:T(8,128)(2,1)S(1)}, bf16[2,2,2,64,128]{4,3,2,1,0:T(8,128)(2,1)S(1)}, u32[]{:S(2)}, u32[]{:S(2)}) collective-permute-start(bf16[2,2,2,64,128]{4,3,2,1,0:T(8,128)(2,1)S(1)} %bitcast.68), channel_id=1, source_target_pairs={{0,16},{1,17},{2,18},{3,19},{4,20},{5,21},{6,22},{7,23},{8,24},{9,... | collective-permute-start | bytes 393224 | tf_op jit(solution)/shard_map/ppermute | solution.py:264
  210.3 10.6 %collective-permute-start.32 = (bf16[2,2,2,64,128]{4,3,2,1,0:T(8,128)(2,1)S(1)}, bf16[2,2,2,64,128]{4,3,2,1,0:T(8,128)(2,1)S(1)}, u32[]{:S(2)}, u32[]{:S(2)}) collective-permute-start(bf16[2,2,2,64,128]{4,3,2,1,0:T(8,128)(2,1)S(1)} %bitcast.67), channel_id=1, source_target_pairs={{0,8},{1,9},{2,10},{3,11},{4,12},{5,13},{6,14},{7,15},{8,0},{9,1},... | collective-permute-start | bytes 393224 | tf_op jit(solution)/shard_map/ppermute | solution.py:264
  (20 other events, 123.0 us)

commit v4 on v3

--- a/solution.py
+++ b/solution.py
@@ -178,15 +178,16 @@
     half = kept_ref.shape[2]
     bands = 2 * half
 
-    @pl.loop(0, pairs)
-    def _(pair):
+    def fetch(pair, low, high):
+        if high - low == 1:
+            array, point = places[low]
+            source = bra_refs[array].at[point]
+            pltpu.make_async_copy(source, bra_buf.at[pair], bra_sem.at[pair]).start()
+            return
+        middle = (low + high) // 2
         wanted = choice[pair]
-        for number, (array, point) in enumerate(places):
-
-            @pl.when(wanted == number)
-            def _():
-                source = bra_refs[array].at[point]
-                pltpu.make_async_copy(source, bra_buf.at[pair], bra_sem.at[pair]).start()
+        pl.when(wanted < middle)(lambda: fetch(pair, low, middle))
+        pl.when(wanted >= middle)(lambda: fetch(pair, middle, high))
 
     def image_copy(pair):
         point, momentum = divmod(pair % per_group, image_refs[0].shape[1])
@@ -195,6 +196,7 @@
 
     for pair in range(pairs):
         image_copy(pair).start()
+        fetch(pair, 0, len(places))
     low = where[0] == 0
     for pair in range(pairs):
         image_copy(pair).wait()

time: 222 us -> 220 us (level)
    pallas_call x1, Pallas kernels: 12.3 us -> 10.1 us  [products(): pl.pallas_call(functools.partial(product_kernel, groups, places), in_spec...]
  transfers between devices with their start and end apart: 35 -> 35, of which waited for: 17 -> 17; matrix products, arithmetic and copies ran while one was open for 10% -> 11% of each run, Pallas kernels for 10% -> 11%
where the time goes in v4:
time: 220 us; the launch traced here: 219 us
  waiting for transfers between devices  111 us (50%)
  starting transfers between devices  39 us (18%)
  Pallas kernels  33.2 us (15%)
  local copies, waits for them, and re-layouts  25.9 us (12%)
  other arithmetic  9.29 us (4%)
    ppermute x35, waiting for transfers between devices, send(): lax.ppermute(x, ('ka', 'orb'), [(a, flat(*b)) for a, b in moves if b is n...  111 us
    ppermute x35, starting transfers between devices, send(): lax.ppermute(x, ('ka', 'orb'), [(a, flat(*b)) for a, b in moves if b is n...  39 us
    pallas_call x2, Pallas kernels, ket_images(): pl.pallas_call(functools.partial(image_kernel, *places), in_specs=[pl.Blo...  23.1 us
    pallas_call x1, Pallas kernels, products(): pl.pallas_call(functools.partial(product_kernel, groups, places), in_spec...  10.1 us
    slice x8, local copies, waits for them, and re-layouts, second_hops(): arrays[array][place:place + 1]  5.62 us
    unnamed x66, local copies, waits for them, and re-layouts  5.39 us
    dynamic_slice x1, local copies, waits for them, and re-layouts, trade_weights(): lax.dynamic_slice_in_dim(after(perturbation, *arrived), first_sent, block...  4.99 us
    select_n x2, other arithmetic, trade(): jnp.where(is_home, came, kept)  4.57 us
  transfers between devices with their start and end apart: 35, of which 17 were waited for; matrix products, arithmetic and copies ran while one was open for 11% of the time, Pallas kernels for 11%

profile of v4, /device:TPU:0, one launch (start us, length us, event | category | flops | bytes accessed | tf_op | source)
XLA Modules:
  0.0 219.3 jit_solution(13706044815941716544)
XLA Ops:
  0.0 1.3 dynamic-slice_bitcast_fusion.1
  1.8 2.3 %collective-permute-done.3 = bf16[2,1024,256]{2,1,0:T(8,128)(2,1)S(1)} collective-permute-done((bf16[2,1024,256]{2,1,0:T(8,128)(2,1)S(1)}, bf16[2,1024,256]{2,1,0:T(8,128)(2,1)S(1)}, u32[]{:S(2)}, u32[]{:S(2)}) %collective-permute-start.3) | collective-permute-done | bytes 1048608 | tf_op jit(solution)/shard_map/ppermute | solution.py:266
  4.1 1.4 bitcast_select_fusion
  5.5 3.0 %dynamic-slice_bitcast_fusion = bf16[2,1024,256]{2,1,0:T(8,128)(2,1)} fusion(s32[]{:T(128)S(6)} %select_n.316, s32[]{:T(128)S(6)} %select_n.311, bf16[2,2,2,1024,256]{4,3,2,1,0:T(8,128)(2,1)} %bitcast.64), kind=kLoop, calls=%fused_computation.10 | loop fusion | bytes 2097160 | tf_op jit(solution)/shard_map/jit(dynamic_index_in_dim)/squeeze | solution.py:278
  8.9 2.6 %collective-permute-start.10 = (bf16[2,1024,256]{2,1,0:T(8,128)(2,1)S(1)}, bf16[2,1024,256]{2,1,0:T(8,128)(2,1)S(1)}, u32[]{:S(2)}, u32[]{:S(2)}) collective-permute-start(bf16[2,1024,256]{2,1,0:T(8,128)(2,1)S(1)} %get-tuple-element.55.refs_2_.refs_4_), channel_id=1, source_target_pairs={{0,2},{1,3},{2,0},{3,1},{4,6},{5,7},{6,4},{7,5},{8,10},{9,11},{10,... | collective-permute-start | bytes 3145736 | tf_op jit(solution)/shard_map/ppermute | solution.py:266
  11.5 1.5 collective-permute-start.11
  13.2 1.2 collective-permute-done
  14.5 2.7 %collective-permute-start.5 = (bf16[1,1024,256]{2,1,0:T(8,128)(2,1)S(1)}, bf16[1,1024,256]{2,1,0:T(8,128)(2,1)S(1)}, u32[]{:S(2)}, u32[]{:S(2)}) collective-permute-start(bf16[1,1024,256]{2,1,0:T(8,128)(2,1)S(1)} %slice.87), channel_id=1, source_target_pairs={{0,16},{1,17},{2,18},{3,19},{4,20},{5,21},{6,22},{7,23},{8,24},{9,... | collective-permute-start | bytes 1572872 | tf_op jit(solution)/shard_map/ppermute | solution.py:266
  17.2 3.2 %bitcast_select_fusion.2 = (bf16[2,1024,256]{2,1,0:T(8,128)(2,1)}, bf16[2,1024,256]{2,1,0:T(8,128)(2,1)}) fusion(bf16[2,1024,256]{2,1,0:T(8,128)(2,1)} %collective-permute-done.4, pred[]{:T(512)S(6)} %eq.37, s32[]{:T(128)S(6)} %select_n.316, s32[]{:T(128)S(6)} %select_n.309, bf16[2,2,2,1024,256]{4,3,2,1,0:T(8,128)(2,1)} %bitcast.65), kind=kLoop, calls=%fused_computation.8 | loop fusion | flops 1048576 | bytes 4194313 | tf_op jit(solution)/shard_map/jit(_where)/select_n | solution.py:307
  20.4 1.6 collective-permute-start.9
  21.9 13.3 %collective-permute-done.10.refs_5_ = bf16[2,1024,256]{2,1,0:T(8,128)(2,1)S(1)} collective-permute-done((bf16[2,1024,256]{2,1,0:T(8,128)(2,1)S(1)}, bf16[2,1024,256]{2,1,0:T(8,128)(2,1)S(1)}, u32[]{:S(2)}, u32[]{:S(2)}) %collective-permute-start.10) | collective-permute-done | bytes 1048608 | tf_op jit(solution)/shard_map/ppermute | solution.py:266
  36.4 4.4 %collective-permute-done.5 = bf16[1,1024,256]{2,1,0:T(8,128)(2,1)S(1)} collective-permute-done((bf16[1,1024,256]{2,1,0:T(8,128)(2,1)S(1)}, bf16[1,1024,256]{2,1,0:T(8,128)(2,1)S(1)}, u32[]{:S(2)}, u32[]{:S(2)}) %collective-permute-start.5) | collective-permute-done | bytes 524320 | tf_op jit(solution)/shard_map/ppermute | solution.py:266
  41.6 1.9 slice.109
  44.0 1.9 slice.88
  46.0 8.1 %collective-permute-done.12.refs_7_ = bf16[1,1024,256]{2,1,0:T(8,128)(2,1)S(1)} collective-permute-done((bf16[1,1024,256]{2,1,0:T(8,128)(2,1)}, bf16[1,1024,256]{2,1,0:T(8,128)(2,1)S(1)}, u32[]{:S(2)}, u32[]{:S(2)}) %collective-permute-start.12) | collective-permute-done | bytes 524320 | tf_op jit(solution)/shard_map/ppermute | solution.py:266
  54.1 2.7 %collective-permute-done.13.refs_8_ = bf16[1,1024,256]{2,1,0:T(8,128)(2,1)S(1)} collective-permute-done((bf16[1,1024,256]{2,1,0:T(8,128)(2,1)}, bf16[1,1024,256]{2,1,0:T(8,128)(2,1)S(1)}, u32[]{:S(2)}, u32[]{:S(2)}) %collective-permute-start.13) | collective-permute-done | bytes 524320 | tf_op jit(solution)/shard_map/ppermute | solution.py:266
  56.8 5.0 %constant_dynamic-slice_fusion = bf16[2,8,8,128,128]{4,3,2,1,0:T(8,128)(2,1)} fusion(bf16[2,32,8,128,128]{4,3,2,1,0:T(8,128)(2,1)} %refs_6_.3, s32[]{:T(128)S(6)} %select_n.324), kind=kLoop, calls=%fused_computation.43 | loop fusion | bytes 8388612 | tf_op jit(solution)/shard_map/dynamic_slice | solution.py:330
  61.8 9.4 %collective-permute-done.6 = bf16[1,1024,256]{2,1,0:T(8,128)(2,1)} collective-permute-done((bf16[1,1024,256]{2,1,0:T(8,128)(2,1)}, bf16[1,1024,256]{2,1,0:T(8,128)(2,1)}, u32[]{:S(2)}, u32[]{:S(2)}) %collective-permute-start.6) | collective-permute-done | bytes 524320 | tf_op jit(solution)/shard_map/ppermute | solution.py:266
  71.2 1.5 collective-permute-start.14
  73.7 1.4 collective-permute-start.1
  76.1 2.9 %collective-permute-start.7 = (bf16[1,1024,256]{2,1,0:T(8,128)(2,1)S(1)}, bf16[1,1024,256]{2,1,0:T(8,128)(2,1)S(1)}, u32[]{:S(2)}, u32[]{:S(2)}) collective-permute-start(bf16[1,1024,256]{2,1,0:T(8,128)(2,1)S(1)} %slice.89), channel_id=1, source_target_pairs={{0,24},{1,25},{2,26},{3,27},{4,28},{5,29},{6,30},{7,31},{8,16},{9,... | collective-permute-start | bytes 1572872 | tf_op jit(solution)/shard_map/ppermute | solution.py:266
  79.0 15.3 %collective-permute-done.14.refs_10_ = bf16[2,1024,256]{2,1,0:T(8,128)(2,1)S(1)} collective-permute-done((bf16[2,1024,256]{2,1,0:T(8,128)(2,1)S(1)}, bf16[2,1024,256]{2,1,0:T(8,128)(2,1)S(1)}, u32[]{:S(2)}, u32[]{:S(2)}) %collective-permute-start.14) | collective-permute-done | bytes 1048608 | tf_op jit(solution)/shard_map/ppermute | solution.py:266
  95.1 1.8 collective-permute-done.15.refs_11_
  98.1 4.5 %collective-permute-done.2 = s32[2,2]{1,0:T(2,128)S(1)} collective-permute-done((s32[2,2]{1,0:T(2,128)S(1)}, s32[2,2]{1,0:T(2,128)S(1)}, u32[]{:S(2)}, u32[]{:S(2)}) %collective-permute-start.2) | collective-permute-done | bytes 48 | tf_op jit(solution)/shard_map/ppermute | solution.py:266
  102.7 1.3 pad_maximum_fusion.1.refs_3_.refs_14_
  104.0 1.5 slice.90
  105.5 5.1 %collective-permute-start.8 = (bf16[1,1024,256]{2,1,0:T(8,128)(2,1)S(1)}, bf16[1,1024,256]{2,1,0:T(8,128)(2,1)S(1)}, u32[]{:S(2)}, u32[]{:S(2)}) collective-permute-start(bf16[1,1024,256]{2,1,0:T(8,128)(2,1)S(1)} %slice.90), channel_id=1, source_target_pairs={{0,24},{1,25},{2,26},{3,27},{4,28},{5,29},{6,30},{7,31},{8,16},{9,... | collective-permute-start | bytes 1572872 | tf_op jit(solution)/shard_map/ppermute | solution.py:266
  110.5 1.4 collective-permute-start.16
  111.9 1.2 collective-permute-start.17
  114.3 4.9 %collective-permute-done.8 = bf16[1,1024,256]{2,1,0:T(8,128)(2,1)S(1)} collective-permute-done((bf16[1,1024,256]{2,1,0:T(8,128)(2,1)S(1)}, bf16[1,1024,256]{2,1,0:T(8,128)(2,1)S(1)}, u32[]{:S(2)}, u32[]{:S(2)}) %collective-permute-start.8) | collective-permute-done | bytes 524320 | tf_op jit(solution)/shard_map/ppermute | solution.py:266
  120.2 11.5 %collective-permute-done.16.refs_15_ = bf16[2,1024,256]{2,1,0:T(8,128)(2,1)S(1)} collective-permute-done((bf16[2,1024,256]{2,1,0:T(8,128)(2,1)S(1)}, bf16[2,1024,256]{2,1,0:T(8,128)(2,1)S(1)}, u32[]{:S(2)}, u32[]{:S(2)}) %collective-permute-start.16) | collective-permute-done | bytes 1048608 | tf_op jit(solution)/shard_map/ppermute | solution.py:266
  132.3 1.2 collective-permute-start.27
  133.5 1.2 collective-permute-start.28
  136.3 1.7 collective-permute-start.18
  138.1 19.2 %collective-permute-done.27.refs_20_ = bf16[2,1024,256]{2,1,0:T(8,128)(2,1)S(1)} collective-permute-done((bf16[2,1024,256]{2,1,0:T(8,128)(2,1)S(1)}, bf16[2,1024,256]{2,1,0:T(8,128)(2,1)S(1)}, u32[]{:S(2)}, u32[]{:S(2)}) %collective-permute-start.27) | collective-permute-done | bytes 1048608 | tf_op jit(solution)/shard_map/ppermute | solution.py:266
  157.3 1.2 collective-permute-start.25
  161.0 11.5 %ket_images.3 = (bf16[2,2,1024,256]{3,2,1,0:T(8,128)(2,1)}, bf16[2,2,1024,256]{3,2,1,0:T(8,128)(2,1)}) custom-call(s32[3]{0:T(128)S(1)} %pad_add_fusion.3.where, s32[8,8]{1,0:T(8,128)S(1)} %get-tuple-element.93.columns, f32[4,8,8]{2,1,0:T(8,128)S(1)} %get-tuple-element.95.cosine, f32[4,8,8]{2,1,0:T(8,128)S(1)} %get-tuple-element.94.sine, ...), custom_call_target="tpu_custom_call" | custom-call | flops 4294967296 | bytes 14680064 | tf_op jit(solution)/shard_map/ket_images/pallas_call | solution.py:149
  174.2 1.2 collective-permute-start.29
  175.4 1.1 collective-permute-start.30
  177.4 1.2 copy-done.6
  178.6 1.2 copy-done.8
  179.9 11.6 %ket_images.2 = (bf16[2,2,1024,256]{3,2,1,0:T(8,128)(2,1)}, bf16[2,2,1024,256]{3,2,1,0:T(8,128)(2,1)}) custom-call(s32[3]{0:T(128)S(1)} %pad_add_fusion.3.where, s32[8,8]{1,0:T(8,128)S(1)} %get-tuple-element.93.columns, f32[4,8,8]{2,1,0:T(8,128)S(1)} %get-tuple-element.98.cosine, f32[4,8,8]{2,1,0:T(8,128)S(1)} %get-tuple-element.99.sine, ...), custom_call_target="tpu_custom_call" | custom-call | flops 4294967296 | bytes 14680064 | tf_op jit(solution)/shard_map/ket_images/pallas_call | solution.py:149
  191.6 10.1 %products.1 = (f32[16,2,64,128]{3,2,1,0:T(8,128)S(1)}, f32[16,2,64,128]{3,2,1,0:T(8,128)}) custom-call(s32[16]{0:T(128)S(1)} %pad_add_fusion.2.choice, s32[1]{0:T(128)} %bitcast.4.where, bf16[2,2,1024,256]{3,2,1,0:T(8,128)(2,1)} %get-tuple-element.60.refs_0_, bf16[2,2,1024,256]{3,2,1,0:T(8,128)(2,1)} %get-tuple-element.63.refs_1_, ...), custom_call_target="tpu_custom_call" | custom-call | flops 2147483648 | bytes 16777216 | tf_op jit(solution)/shard_map/products/pallas_call | solution.py:223
  201.8 2.9 %collective-permute-done.31 = f32[16,2,64,128]{3,2,1,0:T(8,128)S(1)} collective-permute-done((f32[16,2,64,128]{3,2,1,0:T(8,128)}, f32[16,2,64,128]{3,2,1,0:T(8,128)S(1)}, u32[]{:S(2)}, u32[]{:S(2)}) %collective-permute-start.31) | collective-permute-done | bytes 1048608 | tf_op jit(solution)/shard_map/ppermute | solution.py:266
  204.9 3.2 %collective-permute-start.34 = (bf16[2,2,2,64,128]{4,3,2,1,0:T(8,128)(2,1)S(1)}, bf16[2,2,2,64,128]{4,3,2,1,0:T(8,128)(2,1)S(1)}, u32[]{:S(2)}, u32[]{:S(2)}) collective-permute-start(bf16[2,2,2,64,128]{4,3,2,1,0:T(8,128)(2,1)S(1)} %bitcast.69), channel_id=1, source_target_pairs={{0,24},{1,25},{2,26},{3,27},{4,28},{5,29},{6,30},{7,31},{8,16},{9,... | collective-permute-start | bytes 393224 | tf_op jit(solution)/shard_map/ppermute | solution.py:266
  208.1 1.3 collective-permute-start.32
  209.4 3.8 %collective-permute-done.34 = bf16[2,2,2,64,128]{4,3,2,1,0:T(8,128)(2,1)S(1)} collective-permute-done((bf16[2,2,2,64,128]{4,3,2,1,0:T(8,128)(2,1)S(1)}, bf16[2,2,2,64,128]{4,3,2,1,0:T(8,128)(2,1)S(1)}, u32[]{:S(2)}, u32[]{:S(2)}) %collective-permute-start.34) | collective-permute-done | bytes 131104 | tf_op jit(solution)/shard_map/ppermute | solution.py:266
  213.2 5.3 %collective-permute-done.33 = bf16[2,2,2,64,128]{4,3,2,1,0:T(8,128)(2,1)S(1)} collective-permute-done((bf16[2,2,2,64,128]{4,3,2,1,0:T(8,128)(2,1)S(1)}, bf16[2,2,2,64,128]{4,3,2,1,0:T(8,128)(2,1)S(1)}, u32[]{:S(2)}, u32[]{:S(2)}) %collective-permute-start.33) | collective-permute-done | bytes 131104 | tf_op jit(solution)/shard_map/ppermute | solution.py:266
  (145 shorter events, 18.2 us)
Async XLA Ops:
  0.0 13.1 %copy-start.30 = (s32[3,32,8]{1,2,0:T(8,128)S(1)}, s32[3,32,8]{1,2,0:T(8,128)}, u32[]{:S(2)}) copy-start(s32[3,32,8]{1,2,0:T(8,128)} %param.9) | copy-start | bytes 9220
  0.0 13.1 %copy-start.31 = (s32[32,8]{0,1:T(8,128)S(1)}, s32[32,8]{0,1:T(8,128)}, u32[]{:S(2)}) copy-start(s32[32,8]{0,1:T(8,128)} %param.8) | copy-start | bytes 3076
  1.3 2.8 %collective-permute-start.3 = (bf16[2,1024,256]{2,1,0:T(8,128)(2,1)S(1)}, bf16[2,1024,256]{2,1,0:T(8,128)(2,1)S(1)}, u32[]{:S(2)}, u32[]{:S(2)}) collective-permute-start(bf16[2,1024,256]{2,1,0:T(8,128)(2,1)S(1)} %dynamic-slice_bitcast_fusion.1), channel_id=1, source_target_pairs={{0,1},{1,0},{2,3},{3,2},{4,5},{5,4},{6,7},{7,6},{8,9},{9,8},{10,11... | collective-permute-start | bytes 3145736 | tf_op jit(solution)/shard_map/ppermute | solution.py:266
  5.5 14.9 %copy-start.21 = (bf16[2,1024,256]{2,1,0:T(8,128)(2,1)}, bf16[2,1024,256]{2,1,0:T(8,128)(2,1)S(1)}, u32[]{:S(2)}) copy-start(bf16[2,1024,256]{2,1,0:T(8,128)(2,1)S(1)} %get-tuple-element.45) | copy-start | bytes 3145732
  5.5 171.9 %copy-start = (bf16[2,1024,256]{2,1,0:T(8,128)(2,1)}, bf16[2,1024,256]{2,1,0:T(8,128)(2,1)S(1)}, u32[]{:S(2)}) copy-start(bf16[2,1024,256]{2,1,0:T(8,128)(2,1)S(1)} %get-tuple-element.55.refs_2_.refs_4_) | copy-start | bytes 3145732
  8.5 8.6 %collective-permute-start.4 = (bf16[2,1024,256]{2,1,0:T(8,128)(2,1)}, bf16[2,1024,256]{2,1,0:T(8,128)(2,1)}, u32[]{:S(2)}, u32[]{:S(2)}) collective-permute-start(bf16[2,1024,256]{2,1,0:T(8,128)(2,1)} %dynamic-slice_bitcast_fusion), channel_id=1, source_target_pairs={{0,1},{1,0},{2,3},{3,2},{4,5},{5,4},{6,7},{7,6},{8,9},{9,8},{10,11... | collective-permute-start | bytes 3145736 | tf_op jit(solution)/shard_map/ppermute | solution.py:266
  8.9 26.3 %collective-permute-start.10 = (bf16[2,1024,256]{2,1,0:T(8,128)(2,1)S(1)}, bf16[2,1024,256]{2,1,0:T(8,128)(2,1)S(1)}, u32[]{:S(2)}, u32[]{:S(2)}) collective-permute-start(bf16[2,1024,256]{2,1,0:T(8,128)(2,1)S(1)} %get-tuple-element.55.refs_2_.refs_4_), channel_id=1, source_target_pairs={{0,2},{1,3},{2,0},{3,1},{4,6},{5,7},{6,4},{7,5},{8,10},{9,11},{10,... | collective-permute-start | bytes 3145736 | tf_op jit(solution)/shard_map/ppermute | solution.py:266
  11.5 29.8 %collective-permute-start.11 = (bf16[2,1024,256]{2,1,0:T(8,128)(2,1)S(1)}, bf16[2,1024,256]{2,1,0:T(8,128)(2,1)}, u32[]{:S(2)}, u32[]{:S(2)}) collective-permute-start(bf16[2,1024,256]{2,1,0:T(8,128)(2,1)S(1)} %get-tuple-element.55.refs_2_.refs_4_), channel_id=1, source_target_pairs={{0,4},{1,5},{2,6},{3,7},{4,0},{5,1},{6,2},{7,3},{8,12},{9,13},{10,... | collective-permute-start | bytes 3145736 | tf_op jit(solution)/shard_map/ppermute | solution.py:266
  13.2 1.3 collective-permute-start
  14.5 26.3 %collective-permute-start.5 = (bf16[1,1024,256]{2,1,0:T(8,128)(2,1)S(1)}, bf16[1,1024,256]{2,1,0:T(8,128)(2,1)S(1)}, u32[]{:S(2)}, u32[]{:S(2)}) collective-permute-start(bf16[1,1024,256]{2,1,0:T(8,128)(2,1)S(1)} %slice.87), channel_id=1, source_target_pairs={{0,16},{1,17},{2,18},{3,19},{4,20},{5,21},{6,22},{7,23},{8,24},{9,... | collective-permute-start | bytes 1572872 | tf_op jit(solution)/shard_map/ppermute | solution.py:266
  20.4 41.4 %collective-permute-start.9 = (bf16[2,1024,256]{2,1,0:T(8,128)(2,1)}, bf16[2,1024,256]{2,1,0:T(8,128)(2,1)S(1)}, u32[]{:S(2)}, u32[]{:S(2)}) collective-permute-start(bf16[2,1024,256]{2,1,0:T(8,128)(2,1)} %get-tuple-element.48), channel_id=1, source_target_pairs={{0,8},{1,9},{2,10},{3,11},{4,12},{5,13},{6,14},{7,15},{8,0},{9,1},... | collective-permute-start | bytes 3145736 | tf_op jit(solution)/shard_map/ppermute | solution.py:266
  40.8 13.3 %collective-permute-start.12 = (bf16[1,1024,256]{2,1,0:T(8,128)(2,1)}, bf16[1,1024,256]{2,1,0:T(8,128)(2,1)S(1)}, u32[]{:S(2)}, u32[]{:S(2)}) collective-permute-start(bf16[1,1024,256]{2,1,0:T(8,128)(2,1)} %slice.108), channel_id=1, source_target_pairs={{0,4},{1,5},{2,6},{3,7},{4,0},{5,1},{6,2},{7,3},{8,12},{9,13},{10,... | collective-permute-start | bytes 1572872 | tf_op jit(solution)/shard_map/ppermute | solution.py:266
  43.5 13.3 %collective-permute-start.13 = (bf16[1,1024,256]{2,1,0:T(8,128)(2,1)}, bf16[1,1024,256]{2,1,0:T(8,128)(2,1)S(1)}, u32[]{:S(2)}, u32[]{:S(2)}) collective-permute-start(bf16[1,1024,256]{2,1,0:T(8,128)(2,1)} %slice.109), channel_id=1, source_target_pairs={{0,2},{1,3},{2,0},{3,1},{4,6},{5,7},{6,4},{7,5},{8,10},{9,11},{10,... | collective-permute-start | bytes 1572872 | tf_op jit(solution)/shard_map/ppermute | solution.py:266
  45.9 25.3 %collective-permute-start.6 = (bf16[1,1024,256]{2,1,0:T(8,128)(2,1)}, bf16[1,1024,256]{2,1,0:T(8,128)(2,1)}, u32[]{:S(2)}, u32[]{:S(2)}) collective-permute-start(bf16[1,1024,256]{2,1,0:T(8,128)(2,1)} %slice.88), channel_id=1, source_target_pairs={{0,16},{1,17},{2,18},{3,19},{4,20},{5,21},{6,22},{7,23},{8,24},{9,... | collective-permute-start | bytes 1572872 | tf_op jit(solution)/shard_map/ppermute | solution.py:266
  46.0 27.7 %copy-start.32 = (s32[2]{0:T(128)S(1)}, s32[2]{0:T(128)}, u32[]{:S(2)}) copy-start(s32[2]{0:T(128)} %param.10) | copy-start | bytes 28
  61.8 99.2 %collective-permute-start.23 = (bf16[2,8,8,128,128]{4,3,2,1,0:T(8,128)(2,1)}, bf16[2,8,8,128,128]{4,3,2,1,0:T(8,128)(2,1)}, u32[]{:S(2)}, u32[]{:S(2)}) collective-permute-start(bf16[2,8,8,128,128]{4,3,2,1,0:T(8,128)(2,1)} %constant_dynamic-slice_fusion), channel_id=1, source_target_pairs={{0,1},{1,0},{2,3},{3,2},{4,5},{5,4},{6,7},{7,6},{8,9},{9,8},{10,11... | collective-permute-start | bytes 12582920 | tf_op jit(solution)/shard_map/ppermute | solution.py:266
  61.8 51.4 %copy-start.3 = (bf16[2,1024,256]{2,1,0:T(8,128)(2,1)}, bf16[2,1024,256]{2,1,0:T(8,128)(2,1)S(1)}, u32[]{:S(2)}) copy-start(bf16[2,1024,256]{2,1,0:T(8,128)(2,1)S(1)} %collective-permute-done.9.refs_2_.refs_9_) | copy-start | bytes 3145732
  71.2 23.2 %collective-permute-start.14 = (bf16[2,1024,256]{2,1,0:T(8,128)(2,1)S(1)}, bf16[2,1024,256]{2,1,0:T(8,128)(2,1)S(1)}, u32[]{:S(2)}, u32[]{:S(2)}) collective-permute-start(bf16[2,1024,256]{2,1,0:T(8,128)(2,1)S(1)} %collective-permute-done.9.refs_2_.refs_9_), channel_id=1, source_target_pairs={{0,2},{1,3},{2,0},{3,1},{4,6},{5,7},{6,4},{7,5},{8,10},{9,11},{10,... | collective-permute-start | bytes 3145736 | tf_op jit(solution)/shard_map/ppermute | solution.py:266
  72.7 24.2 %collective-permute-start.15 = (bf16[2,1024,256]{2,1,0:T(8,128)(2,1)S(1)}, bf16[2,1024,256]{2,1,0:T(8,128)(2,1)}, u32[]{:S(2)}, u32[]{:S(2)}) collective-permute-start(bf16[2,1024,256]{2,1,0:T(8,128)(2,1)S(1)} %collective-permute-done.9.refs_2_.refs_9_), channel_id=1, source_target_pairs={{0,4},{1,5},{2,6},{3,7},{4,0},{5,1},{6,2},{7,3},{8,12},{9,13},{10,... | collective-permute-start | bytes 3145736 | tf_op jit(solution)/shard_map/ppermute | solution.py:266
  73.7 24.3 %collective-permute-start.1 = (s32[1,2]{1,0:T(1,128)S(1)}, s32[1,2]{1,0:T(1,128)S(1)}, u32[]{:S(2)}, u32[]{:S(2)}) collective-permute-start(s32[1,2]{1,0:T(1,128)S(1)} %bitcast.71), channel_id=1, source_target_pairs={{0,8},{1,9},{2,10},{3,11},{4,12},{5,13},{6,14},{7,15},{8,0},{9,1},... | collective-permute-start | bytes 32 | tf_op jit(solution)/shard_map/ppermute | solution.py:266
  76.1 27.9 %collective-permute-start.7 = (bf16[1,1024,256]{2,1,0:T(8,128)(2,1)S(1)}, bf16[1,1024,256]{2,1,0:T(8,128)(2,1)S(1)}, u32[]{:S(2)}, u32[]{:S(2)}) collective-permute-start(bf16[1,1024,256]{2,1,0:T(8,128)(2,1)S(1)} %slice.89), channel_id=1, source_target_pairs={{0,24},{1,25},{2,26},{3,27},{4,28},{5,29},{6,30},{7,31},{8,16},{9,... | collective-permute-start | bytes 1572872 | tf_op jit(solution)/shard_map/ppermute | solution.py:266
  94.4 17.5 %collective-permute-start.19 = (bf16[1,1024,256]{2,1,0:T(8,128)(2,1)S(1)}, bf16[1,1024,256]{2,1,0:T(8,128)(2,1)S(1)}, u32[]{:S(2)}, u32[]{:S(2)}) collective-permute-start(bf16[1,1024,256]{2,1,0:T(8,128)(2,1)S(1)} %slice.110), channel_id=1, source_target_pairs={{0,4},{1,5},{2,6},{3,7},{4,0},{5,1},{6,2},{7,3},{8,12},{9,13},{10,... | collective-permute-start | bytes 1572872 | tf_op jit(solution)/shard_map/ppermute | solution.py:266
  98.0 15.2 %collective-permute-start.20 = (bf16[1,1024,256]{2,1,0:T(8,128)(2,1)S(1)}, bf16[1,1024,256]{2,1,0:T(8,128)(2,1)S(1)}, u32[]{:S(2)}, u32[]{:S(2)}) collective-permute-start(bf16[1,1024,256]{2,1,0:T(8,128)(2,1)S(1)} %slice.111), channel_id=1, source_target_pairs={{0,2},{1,3},{2,0},{3,1},{4,6},{5,7},{6,4},{7,5},{8,10},{9,11},{10,... | collective-permute-start | bytes 1572872 | tf_op jit(solution)/shard_map/ppermute | solution.py:266
  98.1 4.5 %collective-permute-start.2 = (s32[2,2]{1,0:T(2,128)S(1)}, s32[2,2]{1,0:T(2,128)S(1)}, u32[]{:S(2)}, u32[]{:S(2)}) collective-permute-start(s32[2,2]{1,0:T(2,128)S(1)} %pad_add_fusion.1), channel_id=1, source_target_pairs={{0,16},{1,17},{2,18},{3,19},{4,20},{5,21},{6,22},{7,23},{8,24},{9,... | collective-permute-start | bytes 56 | tf_op jit(solution)/shard_map/ppermute | solution.py:266
  104.0 73.4 %copy-start.1 = (bf16[2,1024,256]{2,1,0:T(8,128)(2,1)}, bf16[2,1024,256]{2,1,0:T(8,128)(2,1)S(1)}, u32[]{:S(2)}) copy-start(bf16[2,1024,256]{2,1,0:T(8,128)(2,1)S(1)} %pad_maximum_fusion.1.refs_3_.refs_14_) | copy-start | bytes 3145732
  105.5 13.8 %collective-permute-start.8 = (bf16[1,1024,256]{2,1,0:T(8,128)(2,1)S(1)}, bf16[1,1024,256]{2,1,0:T(8,128)(2,1)S(1)}, u32[]{:S(2)}, u32[]{:S(2)}) collective-permute-start(bf16[1,1024,256]{2,1,0:T(8,128)(2,1)S(1)} %slice.90), channel_id=1, source_target_pairs={{0,24},{1,25},{2,26},{3,27},{4,28},{5,29},{6,30},{7,31},{8,16},{9,... | collective-permute-start | bytes 1572872 | tf_op jit(solution)/shard_map/ppermute | solution.py:266
  110.5 21.2 %collective-permute-start.16 = (bf16[2,1024,256]{2,1,0:T(8,128)(2,1)S(1)}, bf16[2,1024,256]{2,1,0:T(8,128)(2,1)S(1)}, u32[]{:S(2)}, u32[]{:S(2)}) collective-permute-start(bf16[2,1024,256]{2,1,0:T(8,128)(2,1)S(1)} %pad_maximum_fusion.1.refs_3_.refs_14_), channel_id=1, source_target_pairs={{0,2},{1,3},{2,0},{3,1},{4,6},{5,7},{6,4},{7,5},{8,10},{9,11},{10,... | collective-permute-start | bytes 3145736 | tf_op jit(solution)/shard_map/ppermute | solution.py:266
  111.9 20.3 %collective-permute-start.17 = (bf16[2,1024,256]{2,1,0:T(8,128)(2,1)S(1)}, bf16[2,1024,256]{2,1,0:T(8,128)(2,1)S(1)}, u32[]{:S(2)}, u32[]{:S(2)}) collective-permute-start(bf16[2,1024,256]{2,1,0:T(8,128)(2,1)S(1)} %pad_maximum_fusion.1.refs_3_.refs_14_), channel_id=1, source_target_pairs={{0,4},{1,5},{2,6},{3,7},{4,0},{5,1},{6,2},{7,3},{8,12},{9,13},{10,... | collective-permute-start | bytes 3145736 | tf_op jit(solution)/shard_map/ppermute | solution.py:266
  114.0 20.9 %collective-permute-start.21 = (bf16[2,2,512,256]{3,2,1,0:T(8,128)(2,1)S(1)}, bf16[2,2,512,256]{3,2,1,0:T(8,128)(2,1)S(1)}, u32[]{:S(2)}, u32[]{:S(2)}) collective-permute-start(bf16[2,2,512,256]{3,2,1,0:T(8,128)(2,1)S(1)} %pad_maximum_fusion.3), channel_id=1, source_target_pairs={{0,1},{1,0},{2,3},{3,2},{4,5},{5,4},{6,7},{7,6},{8,9},{9,8},{10,11... | collective-permute-start | bytes 3145736 | tf_op jit(solution)/shard_map/ppermute | solution.py:266
  114.2 20.8 %copy-start.4 = (bf16[2,1024,256]{2,1,0:T(8,128)(2,1)S(1)}, bf16[2,1024,256]{2,1,0:T(8,128)(2,1)}, u32[]{:S(2)}) copy-start(bf16[2,1024,256]{2,1,0:T(8,128)(2,1)} %copy-done.3) | copy-start | bytes 3145732
  119.3 17.0 %collective-permute-start.24 = (bf16[2,2,512,256]{3,2,1,0:T(8,128)(2,1)S(1)}, bf16[2,2,512,256]{3,2,1,0:T(8,128)(2,1)S(1)}, u32[]{:S(2)}, u32[]{:S(2)}) collective-permute-start(bf16[2,2,512,256]{3,2,1,0:T(8,128)(2,1)S(1)} %pad_maximum_fusion.5), channel_id=1, source_target_pairs={{1,8},{3,10},{5,12},{7,14},{8,1},{9,16},{10,3},{11,18},{12,5},{13,... | collective-permute-start | bytes 3145736 | tf_op jit(solution)/shard_map/ppermute | solution.py:266
  120.2 40.8 %copy-start.2 = (bf16[2,1024,256]{2,1,0:T(8,128)(2,1)}, bf16[2,1024,256]{2,1,0:T(8,128)(2,1)S(1)}, u32[]{:S(2)}) copy-start(bf16[2,1024,256]{2,1,0:T(8,128)(2,1)S(1)} %pad_maximum_fusion.refs_3_.refs_19_) | copy-start | bytes 3145732
  132.3 25.0 %collective-permute-start.27 = (bf16[2,1024,256]{2,1,0:T(8,128)(2,1)S(1)}, bf16[2,1024,256]{2,1,0:T(8,128)(2,1)S(1)}, u32[]{:S(2)}, u32[]{:S(2)}) collective-permute-start(bf16[2,1024,256]{2,1,0:T(8,128)(2,1)S(1)} %pad_maximum_fusion.refs_3_.refs_19_), channel_id=1, source_target_pairs={{0,2},{1,3},{2,0},{3,1},{4,6},{5,7},{6,4},{7,5},{8,10},{9,11},{10,... | collective-permute-start | bytes 3145736 | tf_op jit(solution)/shard_map/ppermute | solution.py:266
  133.5 25.1 %collective-permute-start.28 = (bf16[2,1024,256]{2,1,0:T(8,128)(2,1)S(1)}, bf16[2,1024,256]{2,1,0:T(8,128)(2,1)S(1)}, u32[]{:S(2)}, u32[]{:S(2)}) collective-permute-start(bf16[2,1024,256]{2,1,0:T(8,128)(2,1)S(1)} %pad_maximum_fusion.refs_3_.refs_19_), channel_id=1, source_target_pairs={{0,4},{1,5},{2,6},{3,7},{4,0},{5,1},{6,2},{7,3},{8,12},{9,13},{10,... | collective-permute-start | bytes 3145736 | tf_op jit(solution)/shard_map/ppermute | solution.py:266
  134.9 26.1 %copy-start.5 = (bf16[2,2,512,256]{3,2,1,0:T(8,128)(2,1)}, bf16[2,2,512,256]{3,2,1,0:T(8,128)(2,1)S(1)}, u32[]{:S(2)}) copy-start(bf16[2,2,512,256]{3,2,1,0:T(8,128)(2,1)S(1)} %collective-permute-done.21.refs_4_) | copy-start | bytes 3145732
  134.9 26.1 %collective-permute-start.22 = (bf16[2,2,512,256]{3,2,1,0:T(8,128)(2,1)S(1)}, bf16[2,2,512,256]{3,2,1,0:T(8,128)(2,1)S(1)}, u32[]{:S(2)}, u32[]{:S(2)}) collective-permute-start(bf16[2,2,512,256]{3,2,1,0:T(8,128)(2,1)S(1)} %pad_maximum_fusion.4), channel_id=1, source_target_pairs={{0,1},{1,0},{2,3},{3,2},{4,5},{5,4},{6,7},{7,6},{8,9},{9,8},{10,11... | collective-permute-start | bytes 3145736 | tf_op jit(solution)/shard_map/ppermute | solution.py:266
  136.3 41.1 %collective-permute-start.18 = (bf16[2,2,512,256]{3,2,1,0:T(8,128)(2,1)}, bf16[2,2,512,256]{3,2,1,0:T(8,128)(2,1)}, u32[]{:S(2)}, u32[]{:S(2)}) collective-permute-start(bf16[2,2,512,256]{3,2,1,0:T(8,128)(2,1)} %pad_maximum_fusion.2), channel_id=1, source_target_pairs={{1,8},{3,10},{5,12},{7,14},{8,1},{9,16},{10,3},{11,18},{12,5},{13,... | collective-permute-start | bytes 3145736 | tf_op jit(solution)/shard_map/ppermute | solution.py:266
  157.3 15.2 %copy-start.26 = (bf16[2,1024,256]{2,1,0:T(8,128)(2,1)}, bf16[2,1024,256]{2,1,0:T(8,128)(2,1)S(1)}, u32[]{:S(2)}) copy-start(bf16[2,1024,256]{2,1,0:T(8,128)(2,1)S(1)} %collective-permute-done.27.refs_20_) | copy-start | bytes 3145732
  157.3 15.2 %collective-permute-start.25 = (bf16[1,1024,256]{2,1,0:T(8,128)(2,1)S(1)}, bf16[1,1024,256]{2,1,0:T(8,128)(2,1)S(1)}, u32[]{:S(2)}, u32[]{:S(2)}) collective-permute-start(bf16[1,1024,256]{2,1,0:T(8,128)(2,1)S(1)} %slice.112), channel_id=1, source_target_pairs={{0,4},{1,5},{2,6},{3,7},{4,0},{5,1},{6,2},{7,3},{8,12},{9,13},{10,... | collective-permute-start | bytes 1572872 | tf_op jit(solution)/shard_map/ppermute | solution.py:266
  158.5 14.0 %copy-start.27 = (bf16[2,1024,256]{2,1,0:T(8,128)(2,1)}, bf16[2,1024,256]{2,1,0:T(8,128)(2,1)S(1)}, u32[]{:S(2)}) copy-start(bf16[2,1024,256]{2,1,0:T(8,128)(2,1)S(1)} %collective-permute-done.28.refs_21_) | copy-start | bytes 3145732
  158.5 14.8 %collective-permute-start.26 = (bf16[1,1024,256]{2,1,0:T(8,128)(2,1)S(1)}, bf16[1,1024,256]{2,1,0:T(8,128)(2,1)S(1)}, u32[]{:S(2)}, u32[]{:S(2)}) collective-permute-start(bf16[1,1024,256]{2,1,0:T(8,128)(2,1)S(1)} %slice.113), channel_id=1, source_target_pairs={{0,2},{1,3},{2,0},{3,1},{4,6},{5,7},{6,4},{7,5},{8,10},{9,11},{10,... | collective-permute-start | bytes 1572872 | tf_op jit(solution)/shard_map/ppermute | solution.py:266
  161.0 15.5 %copy-start.29 = (s32[2,32]{1,0:T(2,128)S(1)}, s32[2,32]{1,0:T(2,128)}, u32[]{:S(2)}) copy-start(s32[2,32]{1,0:T(2,128)} %param.11) | copy-start | bytes 772
  174.2 17.4 %collective-permute-start.29 = (bf16[1,1024,256]{2,1,0:T(8,128)(2,1)}, bf16[1,1024,256]{2,1,0:T(8,128)(2,1)S(1)}, u32[]{:S(2)}, u32[]{:S(2)}) collective-permute-start(bf16[1,1024,256]{2,1,0:T(8,128)(2,1)} %slice.114), channel_id=1, source_target_pairs={{0,4},{1,5},{2,6},{3,7},{4,0},{5,1},{6,2},{7,3},{8,12},{9,13},{10,... | collective-permute-start | bytes 1572872 | tf_op jit(solution)/shard_map/ppermute | solution.py:266
  175.4 16.1 %collective-permute-start.30 = (bf16[1,1024,256]{2,1,0:T(8,128)(2,1)}, bf16[1,1024,256]{2,1,0:T(8,128)(2,1)S(1)}, u32[]{:S(2)}, u32[]{:S(2)}) collective-permute-start(bf16[1,1024,256]{2,1,0:T(8,128)(2,1)} %slice.115), channel_id=1, source_target_pairs={{0,2},{1,3},{2,0},{3,1},{4,6},{5,7},{6,4},{7,5},{8,10},{9,11},{10,... | collective-permute-start | bytes 1572872 | tf_op jit(solution)/shard_map/ppermute | solution.py:266
  201.7 2.9 %collective-permute-start.31 = (f32[16,2,64,128]{3,2,1,0:T(8,128)}, f32[16,2,64,128]{3,2,1,0:T(8,128)S(1)}, u32[]{:S(2)}, u32[]{:S(2)}) collective-permute-start(f32[16,2,64,128]{3,2,1,0:T(8,128)} %get-tuple-element.72), channel_id=1, source_target_pairs={{0,1},{1,0},{2,3},{3,2},{4,5},{5,4},{6,7},{7,6},{8,9},{9,8},{10,11... | collective-permute-start | bytes 3145736 | tf_op jit(solution)/shard_map/ppermute | solution.py:266
  204.9 8.3 %collective-permute-start.34 = (bf16[2,2,2,64,128]{4,3,2,1,0:T(8,128)(2,1)S(1)}, bf16[2,2,2,64,128]{4,3,2,1,0:T(8,128)(2,1)S(1)}, u32[]{:S(2)}, u32[]{:S(2)}) collective-permute-start(bf16[2,2,2,64,128]{4,3,2,1,0:T(8,128)(2,1)S(1)} %bitcast.69), channel_id=1, source_target_pairs={{0,24},{1,25},{2,26},{3,27},{4,28},{5,29},{6,30},{7,31},{8,16},{9,... | collective-permute-start | bytes 393224 | tf_op jit(solution)/shard_map/ppermute | solution.py:266
  208.1 10.4 %collective-permute-start.33 = (bf16[2,2,2,64,128]{4,3,2,1,0:T(8,128)(2,1)S(1)}, bf16[2,2,2,64,128]{4,3,2,1,0:T(8,128)(2,1)S(1)}, u32[]{:S(2)}, u32[]{:S(2)}) collective-permute-start(bf16[2,2,2,64,128]{4,3,2,1,0:T(8,128)(2,1)S(1)} %bitcast.68), channel_id=1, source_target_pairs={{0,16},{1,17},{2,18},{3,19},{4,20},{5,21},{6,22},{7,23},{8,24},{9,... | collective-permute-start | bytes 393224 | tf_op jit(solution)/shard_map/ppermute | solution.py:266
  208.1 10.4 %collective-permute-start.32 = (bf16[2,2,2,64,128]{4,3,2,1,0:T(8,128)(2,1)S(1)}, bf16[2,2,2,64,128]{4,3,2,1,0:T(8,128)(2,1)S(1)}, u32[]{:S(2)}, u32[]{:S(2)}) collective-permute-start(bf16[2,2,2,64,128]{4,3,2,1,0:T(8,128)(2,1)S(1)} %bitcast.67), channel_id=1, source_target_pairs={{0,8},{1,9},{2,10},{3,11},{4,12},{5,13},{6,14},{7,15},{8,0},{9,1},... | collective-permute-start | bytes 393224 | tf_op jit(solution)/shard_map/ppermute | solution.py:266
  (20 other events, 123.0 us)

commit v5 on v4

--- a/solution.py
+++ b/solution.py
@@ -211,7 +211,7 @@
         imag = value[:bands, bands:] - value[bands:, :bands]
         for part, x in enumerate((real, imag)):
             kept_ref[pair, part] = jnp.where(low, x[:half], x[half:])
-            given_ref[pair, part] = jnp.where(low, x[half:], x[:half])
+            given_ref[pair, part] = jnp.where(low, x[half:], x[:half]).astype(given_ref.dtype)
 
 
 def products(choice, where, images, bras, places):
@@ -219,13 +219,16 @@
     _, rows, width = bras[0].shape
     pairs = choice.shape[0]
     bands = width // 2
-    half = jax.ShapeDtypeStruct((pairs, 2, bands // 2, bands), jnp.float32)
+    shape = (pairs, 2, bands // 2, bands)
     return pl.pallas_call(
         functools.partial(product_kernel, groups, places),
         in_specs=[pl.BlockSpec(memory_space=pltpu.SMEM)] * 2
         + [pl.BlockSpec(memory_space=pl.ANY)] * (groups + len(bras)),
         out_specs=[pl.BlockSpec(memory_space=pltpu.VMEM)] * 2,
-        out_shape=[half, half],
+        out_shape=[
+            jax.ShapeDtypeStruct(shape, jnp.float32),
+            jax.ShapeDtypeStruct(shape, jnp.bfloat16),
+        ],
         scratch_shapes=[
             pltpu.VMEM((pairs, rows, width), jnp.bfloat16),
             pltpu.VMEM((pairs, rows, width), jnp.bfloat16),
@@ -449,7 +452,7 @@
         for s, x in zip(parts[name], done[f"images_{name}"]):
             kets[s] = x
     kept, given = products(jnp.concatenate(choices), core[None], kets, arrays, places)
-    total = (kept + on_core(given, 1)).reshape(n_rows, points, momenta, *kept.shape[1:])
+    total = (kept + on_core(given, 1).astype(jnp.float32)).reshape(n_rows, points, momenta, *kept.shape[1:])
     out = total[0]
     for s in range(1, n_rows):
         out = out + across_rows(total[s].astype(jnp.bfloat16), s).astype(jnp.float32)

time: 220 us -> 218 us (level)
  no operation moved by 1% of the time
where the time goes in v5:
time: 218 us; the launch traced here: 217 us
  waiting for transfers between devices  110 us (50%)
  starting transfers between devices  39.2 us (18%)
  Pallas kernels  32.3 us (15%)
  local copies, waits for them, and re-layouts  25.9 us (12%)
  other arithmetic  9.27 us (4%)
    ppermute x35, waiting for transfers between devices, send(): lax.ppermute(x, ('ka', 'orb'), [(a, flat(*b)) for a, b in moves if b is n...  110 us
    ppermute x35, starting transfers between devices, send(): lax.ppermute(x, ('ka', 'orb'), [(a, flat(*b)) for a, b in moves if b is n...  39.2 us
    pallas_call x2, Pallas kernels, ket_images(): pl.pallas_call(functools.partial(image_kernel, *places), in_specs=[pl.Blo...  23.1 us
    pallas_call x1, Pallas kernels, products(): pl.pallas_call(functools.partial(product_kernel, groups, places), in_spec...  9.17 us
    slice x8, local copies, waits for them, and re-layouts, second_hops(): arrays[array][place:place + 1]  5.62 us
    unnamed x66, local copies, waits for them, and re-layouts  5.39 us
    dynamic_slice x1, local copies, waits for them, and re-layouts, trade_weights(): lax.dynamic_slice_in_dim(after(perturbation, *arrived), first_sent, block...  4.99 us
    select_n x2, other arithmetic, trade(): jnp.where(is_home, came, kept)  4.57 us
  transfers between devices with their start and end apart: 35, of which 17 were waited for; matrix products, arithmetic and copies ran while one was open for 11% of the time, Pallas kernels for 11%

profile of v5, /device:TPU:0, one launch (start us, length us, event | category | flops | bytes accessed | tf_op | source)
XLA Modules:
  0.0 217.4 jit_solution(9485270601319254547)
XLA Ops:
  0.0 1.3 dynamic-slice_bitcast_fusion.1
  1.8 2.3 %collective-permute-done.3 = bf16[2,1024,256]{2,1,0:T(8,128)(2,1)S(1)} collective-permute-done((bf16[2,1024,256]{2,1,0:T(8,128)(2,1)S(1)}, bf16[2,1024,256]{2,1,0:T(8,128)(2,1)S(1)}, u32[]{:S(2)}, u32[]{:S(2)}) %collective-permute-start.3) | collective-permute-done | bytes 1048608 | tf_op jit(solution)/shard_map/ppermute | solution.py:269
  4.1 1.4 bitcast_select_fusion
  5.5 3.0 %dynamic-slice_bitcast_fusion = bf16[2,1024,256]{2,1,0:T(8,128)(2,1)} fusion(s32[]{:T(128)S(6)} %select_n.316, s32[]{:T(128)S(6)} %select_n.311, bf16[2,2,2,1024,256]{4,3,2,1,0:T(8,128)(2,1)} %bitcast.64), kind=kLoop, calls=%fused_computation.11 | loop fusion | bytes 2097160 | tf_op jit(solution)/shard_map/jit(dynamic_index_in_dim)/squeeze | solution.py:281
  8.9 2.6 %collective-permute-start.10 = (bf16[2,1024,256]{2,1,0:T(8,128)(2,1)S(1)}, bf16[2,1024,256]{2,1,0:T(8,128)(2,1)S(1)}, u32[]{:S(2)}, u32[]{:S(2)}) collective-permute-start(bf16[2,1024,256]{2,1,0:T(8,128)(2,1)S(1)} %get-tuple-element.55.refs_2_.refs_4_), channel_id=1, source_target_pairs={{0,2},{1,3},{2,0},{3,1},{4,6},{5,7},{6,4},{7,5},{8,10},{9,11},{10,... | collective-permute-start | bytes 3145736 | tf_op jit(solution)/shard_map/ppermute | solution.py:269
  11.5 1.5 collective-permute-start.11
  13.2 1.2 collective-permute-done
  14.5 2.7 %collective-permute-start.5 = (bf16[1,1024,256]{2,1,0:T(8,128)(2,1)S(1)}, bf16[1,1024,256]{2,1,0:T(8,128)(2,1)S(1)}, u32[]{:S(2)}, u32[]{:S(2)}) collective-permute-start(bf16[1,1024,256]{2,1,0:T(8,128)(2,1)S(1)} %slice.87), channel_id=1, source_target_pairs={{0,16},{1,17},{2,18},{3,19},{4,20},{5,21},{6,22},{7,23},{8,24},{9,... | collective-permute-start | bytes 1572872 | tf_op jit(solution)/shard_map/ppermute | solution.py:269
  17.2 3.2 %bitcast_select_fusion.2 = (bf16[2,1024,256]{2,1,0:T(8,128)(2,1)}, bf16[2,1024,256]{2,1,0:T(8,128)(2,1)}) fusion(bf16[2,1024,256]{2,1,0:T(8,128)(2,1)} %collective-permute-done.4, pred[]{:T(512)S(6)} %eq.37, s32[]{:T(128)S(6)} %select_n.316, s32[]{:T(128)S(6)} %select_n.309, bf16[2,2,2,1024,256]{4,3,2,1,0:T(8,128)(2,1)} %bitcast.65), kind=kLoop, calls=%fused_computation.8 | loop fusion | flops 1048576 | bytes 4194313 | tf_op jit(solution)/shard_map/jit(_where)/select_n | solution.py:310
  20.4 1.6 collective-permute-start.9
  21.9 13.3 %collective-permute-done.10.refs_5_ = bf16[2,1024,256]{2,1,0:T(8,128)(2,1)S(1)} collective-permute-done((bf16[2,1024,256]{2,1,0:T(8,128)(2,1)S(1)}, bf16[2,1024,256]{2,1,0:T(8,128)(2,1)S(1)}, u32[]{:S(2)}, u32[]{:S(2)}) %collective-permute-start.10) | collective-permute-done | bytes 1048608 | tf_op jit(solution)/shard_map/ppermute | solution.py:269
  36.4 4.4 %collective-permute-done.5 = bf16[1,1024,256]{2,1,0:T(8,128)(2,1)S(1)} collective-permute-done((bf16[1,1024,256]{2,1,0:T(8,128)(2,1)S(1)}, bf16[1,1024,256]{2,1,0:T(8,128)(2,1)S(1)}, u32[]{:S(2)}, u32[]{:S(2)}) %collective-permute-start.5) | collective-permute-done | bytes 524320 | tf_op jit(solution)/shard_map/ppermute | solution.py:269
  41.6 1.9 slice.109
  44.0 1.9 slice.88
  46.0 8.1 %collective-permute-done.12.refs_7_ = bf16[1,1024,256]{2,1,0:T(8,128)(2,1)S(1)} collective-permute-done((bf16[1,1024,256]{2,1,0:T(8,128)(2,1)}, bf16[1,1024,256]{2,1,0:T(8,128)(2,1)S(1)}, u32[]{:S(2)}, u32[]{:S(2)}) %collective-permute-start.12) | collective-permute-done | bytes 524320 | tf_op jit(solution)/shard_map/ppermute | solution.py:269
  54.1 2.7 %collective-permute-done.13.refs_8_ = bf16[1,1024,256]{2,1,0:T(8,128)(2,1)S(1)} collective-permute-done((bf16[1,1024,256]{2,1,0:T(8,128)(2,1)}, bf16[1,1024,256]{2,1,0:T(8,128)(2,1)S(1)}, u32[]{:S(2)}, u32[]{:S(2)}) %collective-permute-start.13) | collective-permute-done | bytes 524320 | tf_op jit(solution)/shard_map/ppermute | solution.py:269
  56.8 5.0 %constant_dynamic-slice_fusion = bf16[2,8,8,128,128]{4,3,2,1,0:T(8,128)(2,1)} fusion(bf16[2,32,8,128,128]{4,3,2,1,0:T(8,128)(2,1)} %refs_6_.3, s32[]{:T(128)S(6)} %select_n.324), kind=kLoop, calls=%fused_computation.44 | loop fusion | bytes 8388612 | tf_op jit(solution)/shard_map/dynamic_slice | solution.py:333
  61.8 9.4 %collective-permute-done.6 = bf16[1,1024,256]{2,1,0:T(8,128)(2,1)} collective-permute-done((bf16[1,1024,256]{2,1,0:T(8,128)(2,1)}, bf16[1,1024,256]{2,1,0:T(8,128)(2,1)}, u32[]{:S(2)}, u32[]{:S(2)}) %collective-permute-start.6) | collective-permute-done | bytes 524320 | tf_op jit(solution)/shard_map/ppermute | solution.py:269
  71.2 1.5 collective-permute-start.14
  73.7 1.4 collective-permute-start.1
  76.1 2.9 %collective-permute-start.7 = (bf16[1,1024,256]{2,1,0:T(8,128)(2,1)S(1)}, bf16[1,1024,256]{2,1,0:T(8,128)(2,1)S(1)}, u32[]{:S(2)}, u32[]{:S(2)}) collective-permute-start(bf16[1,1024,256]{2,1,0:T(8,128)(2,1)S(1)} %slice.89), channel_id=1, source_target_pairs={{0,24},{1,25},{2,26},{3,27},{4,28},{5,29},{6,30},{7,31},{8,16},{9,... | collective-permute-start | bytes 1572872 | tf_op jit(solution)/shard_map/ppermute | solution.py:269
  79.0 15.3 %collective-permute-done.14.refs_10_ = bf16[2,1024,256]{2,1,0:T(8,128)(2,1)S(1)} collective-permute-done((bf16[2,1024,256]{2,1,0:T(8,128)(2,1)S(1)}, bf16[2,1024,256]{2,1,0:T(8,128)(2,1)S(1)}, u32[]{:S(2)}, u32[]{:S(2)}) %collective-permute-start.14) | collective-permute-done | bytes 1048608 | tf_op jit(solution)/shard_map/ppermute | solution.py:269
  95.1 1.8 collective-permute-done.15.refs_11_
  96.9 1.1 slice.111
  98.1 4.5 %collective-permute-done.2 = s32[2,2]{1,0:T(2,128)S(1)} collective-permute-done((s32[2,2]{1,0:T(2,128)S(1)}, s32[2,2]{1,0:T(2,128)S(1)}, u32[]{:S(2)}, u32[]{:S(2)}) %collective-permute-start.2) | collective-permute-done | bytes 48 | tf_op jit(solution)/shard_map/ppermute | solution.py:269
  102.7 1.3 pad_maximum_fusion.1.refs_3_.refs_14_
  104.0 1.5 slice.90
  105.5 5.1 %collective-permute-start.8 = (bf16[1,1024,256]{2,1,0:T(8,128)(2,1)S(1)}, bf16[1,1024,256]{2,1,0:T(8,128)(2,1)S(1)}, u32[]{:S(2)}, u32[]{:S(2)}) collective-permute-start(bf16[1,1024,256]{2,1,0:T(8,128)(2,1)S(1)} %slice.90), channel_id=1, source_target_pairs={{0,24},{1,25},{2,26},{3,27},{4,28},{5,29},{6,30},{7,31},{8,16},{9,... | collective-permute-start | bytes 1572872 | tf_op jit(solution)/shard_map/ppermute | solution.py:269
  110.5 1.4 collective-permute-start.16
  111.9 1.2 collective-permute-start.17
  114.3 4.9 %collective-permute-done.8 = bf16[1,1024,256]{2,1,0:T(8,128)(2,1)S(1)} collective-permute-done((bf16[1,1024,256]{2,1,0:T(8,128)(2,1)S(1)}, bf16[1,1024,256]{2,1,0:T(8,128)(2,1)S(1)}, u32[]{:S(2)}, u32[]{:S(2)}) %collective-permute-start.8) | collective-permute-done | bytes 524320 | tf_op jit(solution)/shard_map/ppermute | solution.py:269
  120.2 11.5 %collective-permute-done.16.refs_15_ = bf16[2,1024,256]{2,1,0:T(8,128)(2,1)S(1)} collective-permute-done((bf16[2,1024,256]{2,1,0:T(8,128)(2,1)S(1)}, bf16[2,1024,256]{2,1,0:T(8,128)(2,1)S(1)}, u32[]{:S(2)}, u32[]{:S(2)}) %collective-permute-start.16) | collective-permute-done | bytes 1048608 | tf_op jit(solution)/shard_map/ppermute | solution.py:269
  132.3 1.2 collective-permute-start.27
  133.5 1.2 collective-permute-start.28
  136.3 1.7 collective-permute-start.18
  138.1 19.2 %collective-permute-done.27.refs_20_ = bf16[2,1024,256]{2,1,0:T(8,128)(2,1)S(1)} collective-permute-done((bf16[2,1024,256]{2,1,0:T(8,128)(2,1)S(1)}, bf16[2,1024,256]{2,1,0:T(8,128)(2,1)S(1)}, u32[]{:S(2)}, u32[]{:S(2)}) %collective-permute-start.27) | collective-permute-done | bytes 1048608 | tf_op jit(solution)/shard_map/ppermute | solution.py:269
  157.3 1.2 collective-permute-start.25
  161.0 11.5 %ket_images.3 = (bf16[2,2,1024,256]{3,2,1,0:T(8,128)(2,1)}, bf16[2,2,1024,256]{3,2,1,0:T(8,128)(2,1)}) custom-call(s32[3]{0:T(128)S(1)} %pad_add_fusion.3.where, s32[8,8]{1,0:T(8,128)S(1)} %get-tuple-element.93.columns, f32[4,8,8]{2,1,0:T(8,128)S(1)} %get-tuple-element.95.cosine, f32[4,8,8]{2,1,0:T(8,128)S(1)} %get-tuple-element.94.sine, ...), custom_call_target="tpu_custom_call" | custom-call | flops 4294967296 | bytes 14680064 | tf_op jit(solution)/shard_map/ket_images/pallas_call | solution.py:149
  174.2 1.2 collective-permute-start.29
  175.4 1.1 collective-permute-start.30
  177.4 1.2 copy-done.6
  178.6 1.2 copy-done.8
  179.9 11.6 %ket_images.2 = (bf16[2,2,1024,256]{3,2,1,0:T(8,128)(2,1)}, bf16[2,2,1024,256]{3,2,1,0:T(8,128)(2,1)}) custom-call(s32[3]{0:T(128)S(1)} %pad_add_fusion.3.where, s32[8,8]{1,0:T(8,128)S(1)} %get-tuple-element.93.columns, f32[4,8,8]{2,1,0:T(8,128)S(1)} %get-tuple-element.98.cosine, f32[4,8,8]{2,1,0:T(8,128)S(1)} %get-tuple-element.99.sine, ...), custom_call_target="tpu_custom_call" | custom-call | flops 4294967296 | bytes 14680064 | tf_op jit(solution)/shard_map/ket_images/pallas_call | solution.py:149
  191.6 9.2 %products.1 = (f32[16,2,64,128]{3,2,1,0:T(8,128)S(1)}, bf16[16,2,64,128]{3,2,1,0:T(8,128)(2,1)S(1)}) custom-call(s32[16]{0:T(128)S(1)} %pad_add_fusion.2.choice, s32[1]{0:T(128)} %bitcast.4.where, bf16[2,2,1024,256]{3,2,1,0:T(8,128)(2,1)} %get-tuple-element.60.refs_0_, bf16[2,2,1024,256]{3,2,1,0:T(8,128)(2,1)} %get-tuple-element.63.refs_1_, ...), custom_call_target="tpu_custom_call" | custom-call | flops 2147483648 | bytes 16777216 | tf_op jit(solution)/shard_map/products/pallas_call | solution.py:223
  200.9 1.9 collective-permute-done.31
  203.0 4.0 %collective-permute-start.34 = (bf16[2,2,2,64,128]{4,3,2,1,0:T(8,128)(2,1)S(1)}, bf16[2,2,2,64,128]{4,3,2,1,0:T(8,128)(2,1)S(1)}, u32[]{:S(2)}, u32[]{:S(2)}) collective-permute-start(bf16[2,2,2,64,128]{4,3,2,1,0:T(8,128)(2,1)S(1)} %bitcast.69), channel_id=1, source_target_pairs={{0,24},{1,25},{2,26},{3,27},{4,28},{5,29},{6,30},{7,31},{8,16},{9,... | collective-permute-start | bytes 393224 | tf_op jit(solution)/shard_map/ppermute | solution.py:269
  207.7 3.7 %collective-permute-done.34 = bf16[2,2,2,64,128]{4,3,2,1,0:T(8,128)(2,1)S(1)} collective-permute-done((bf16[2,2,2,64,128]{4,3,2,1,0:T(8,128)(2,1)S(1)}, bf16[2,2,2,64,128]{4,3,2,1,0:T(8,128)(2,1)S(1)}, u32[]{:S(2)}, u32[]{:S(2)}) %collective-permute-start.34) | collective-permute-done | bytes 131104 | tf_op jit(solution)/shard_map/ppermute | solution.py:269
  211.4 5.2 %collective-permute-done.33 = bf16[2,2,2,64,128]{4,3,2,1,0:T(8,128)(2,1)S(1)} collective-permute-done((bf16[2,2,2,64,128]{4,3,2,1,0:T(8,128)(2,1)S(1)}, bf16[2,2,2,64,128]{4,3,2,1,0:T(8,128)(2,1)S(1)}, u32[]{:S(2)}, u32[]{:S(2)}) %collective-permute-start.33) | collective-permute-done | bytes 131104 | tf_op jit(solution)/shard_map/ppermute | solution.py:269
  (145 shorter events, 17.7 us)
Async XLA Ops:
  0.0 13.1 %copy-start.30 = (s32[3,32,8]{1,2,0:T(8,128)S(1)}, s32[3,32,8]{1,2,0:T(8,128)}, u32[]{:S(2)}) copy-start(s32[3,32,8]{1,2,0:T(8,128)} %param.9) | copy-start | bytes 9220
  0.0 13.1 %copy-start.31 = (s32[32,8]{0,1:T(8,128)S(1)}, s32[32,8]{0,1:T(8,128)}, u32[]{:S(2)}) copy-start(s32[32,8]{0,1:T(8,128)} %param.8) | copy-start | bytes 3076
  1.3 2.8 %collective-permute-start.3 = (bf16[2,1024,256]{2,1,0:T(8,128)(2,1)S(1)}, bf16[2,1024,256]{2,1,0:T(8,128)(2,1)S(1)}, u32[]{:S(2)}, u32[]{:S(2)}) collective-permute-start(bf16[2,1024,256]{2,1,0:T(8,128)(2,1)S(1)} %dynamic-slice_bitcast_fusion.1), channel_id=1, source_target_pairs={{0,1},{1,0},{2,3},{3,2},{4,5},{5,4},{6,7},{7,6},{8,9},{9,8},{10,11... | collective-permute-start | bytes 3145736 | tf_op jit(solution)/shard_map/ppermute | solution.py:269
  5.5 14.9 %copy-start.21 = (bf16[2,1024,256]{2,1,0:T(8,128)(2,1)}, bf16[2,1024,256]{2,1,0:T(8,128)(2,1)S(1)}, u32[]{:S(2)}) copy-start(bf16[2,1024,256]{2,1,0:T(8,128)(2,1)S(1)} %get-tuple-element.45) | copy-start | bytes 3145732
  5.5 171.9 %copy-start = (bf16[2,1024,256]{2,1,0:T(8,128)(2,1)}, bf16[2,1024,256]{2,1,0:T(8,128)(2,1)S(1)}, u32[]{:S(2)}) copy-start(bf16[2,1024,256]{2,1,0:T(8,128)(2,1)S(1)} %get-tuple-element.55.refs_2_.refs_4_) | copy-start | bytes 3145732
  8.5 8.6 %collective-permute-start.4 = (bf16[2,1024,256]{2,1,0:T(8,128)(2,1)}, bf16[2,1024,256]{2,1,0:T(8,128)(2,1)}, u32[]{:S(2)}, u32[]{:S(2)}) collective-permute-start(bf16[2,1024,256]{2,1,0:T(8,128)(2,1)} %dynamic-slice_bitcast_fusion), channel_id=1, source_target_pairs={{0,1},{1,0},{2,3},{3,2},{4,5},{5,4},{6,7},{7,6},{8,9},{9,8},{10,11... | collective-permute-start | bytes 3145736 | tf_op jit(solution)/shard_map/ppermute | solution.py:269
  8.9 26.3 %collective-permute-start.10 = (bf16[2,1024,256]{2,1,0:T(8,128)(2,1)S(1)}, bf16[2,1024,256]{2,1,0:T(8,128)(2,1)S(1)}, u32[]{:S(2)}, u32[]{:S(2)}) collective-permute-start(bf16[2,1024,256]{2,1,0:T(8,128)(2,1)S(1)} %get-tuple-element.55.refs_2_.refs_4_), channel_id=1, source_target_pairs={{0,2},{1,3},{2,0},{3,1},{4,6},{5,7},{6,4},{7,5},{8,10},{9,11},{10,... | collective-permute-start | bytes 3145736 | tf_op jit(solution)/shard_map/ppermute | solution.py:269
  11.5 29.8 %collective-permute-start.11 = (bf16[2,1024,256]{2,1,0:T(8,128)(2,1)S(1)}, bf16[2,1024,256]{2,1,0:T(8,128)(2,1)}, u32[]{:S(2)}, u32[]{:S(2)}) collective-permute-start(bf16[2,1024,256]{2,1,0:T(8,128)(2,1)S(1)} %get-tuple-element.55.refs_2_.refs_4_), channel_id=1, source_target_pairs={{0,4},{1,5},{2,6},{3,7},{4,0},{5,1},{6,2},{7,3},{8,12},{9,13},{10,... | collective-permute-start | bytes 3145736 | tf_op jit(solution)/shard_map/ppermute | solution.py:269
  13.2 1.3 collective-permute-start
  14.5 26.3 %collective-permute-start.5 = (bf16[1,1024,256]{2,1,0:T(8,128)(2,1)S(1)}, bf16[1,1024,256]{2,1,0:T(8,128)(2,1)S(1)}, u32[]{:S(2)}, u32[]{:S(2)}) collective-permute-start(bf16[1,1024,256]{2,1,0:T(8,128)(2,1)S(1)} %slice.87), channel_id=1, source_target_pairs={{0,16},{1,17},{2,18},{3,19},{4,20},{5,21},{6,22},{7,23},{8,24},{9,... | collective-permute-start | bytes 1572872 | tf_op jit(solution)/shard_map/ppermute | solution.py:269
  20.4 41.4 %collective-permute-start.9 = (bf16[2,1024,256]{2,1,0:T(8,128)(2,1)}, bf16[2,1024,256]{2,1,0:T(8,128)(2,1)S(1)}, u32[]{:S(2)}, u32[]{:S(2)}) collective-permute-start(bf16[2,1024,256]{2,1,0:T(8,128)(2,1)} %get-tuple-element.48), channel_id=1, source_target_pairs={{0,8},{1,9},{2,10},{3,11},{4,12},{5,13},{6,14},{7,15},{8,0},{9,1},... | collective-permute-start | bytes 3145736 | tf_op jit(solution)/shard_map/ppermute | solution.py:269
  40.8 13.3 %collective-permute-start.12 = (bf16[1,1024,256]{2,1,0:T(8,128)(2,1)}, bf16[1,1024,256]{2,1,0:T(8,128)(2,1)S(1)}, u32[]{:S(2)}, u32[]{:S(2)}) collective-permute-start(bf16[1,1024,256]{2,1,0:T(8,128)(2,1)} %slice.108), channel_id=1, source_target_pairs={{0,4},{1,5},{2,6},{3,7},{4,0},{5,1},{6,2},{7,3},{8,12},{9,13},{10,... | collective-permute-start | bytes 1572872 | tf_op jit(solution)/shard_map/ppermute | solution.py:269
  43.5 13.3 %collective-permute-start.13 = (bf16[1,1024,256]{2,1,0:T(8,128)(2,1)}, bf16[1,1024,256]{2,1,0:T(8,128)(2,1)S(1)}, u32[]{:S(2)}, u32[]{:S(2)}) collective-permute-start(bf16[1,1024,256]{2,1,0:T(8,128)(2,1)} %slice.109), channel_id=1, source_target_pairs={{0,2},{1,3},{2,0},{3,1},{4,6},{5,7},{6,4},{7,5},{8,10},{9,11},{10,... | collective-permute-start | bytes 1572872 | tf_op jit(solution)/shard_map/ppermute | solution.py:269
  45.9 25.3 %collective-permute-start.6 = (bf16[1,1024,256]{2,1,0:T(8,128)(2,1)}, bf16[1,1024,256]{2,1,0:T(8,128)(2,1)}, u32[]{:S(2)}, u32[]{:S(2)}) collective-permute-start(bf16[1,1024,256]{2,1,0:T(8,128)(2,1)} %slice.88), channel_id=1, source_target_pairs={{0,16},{1,17},{2,18},{3,19},{4,20},{5,21},{6,22},{7,23},{8,24},{9,... | collective-permute-start | bytes 1572872 | tf_op jit(solution)/shard_map/ppermute | solution.py:269
  46.0 27.7 %copy-start.32 = (s32[2]{0:T(128)S(1)}, s32[2]{0:T(128)}, u32[]{:S(2)}) copy-start(s32[2]{0:T(128)} %param.10) | copy-start | bytes 28
  61.8 99.2 %collective-permute-start.23 = (bf16[2,8,8,128,128]{4,3,2,1,0:T(8,128)(2,1)}, bf16[2,8,8,128,128]{4,3,2,1,0:T(8,128)(2,1)}, u32[]{:S(2)}, u32[]{:S(2)}) collective-permute-start(bf16[2,8,8,128,128]{4,3,2,1,0:T(8,128)(2,1)} %constant_dynamic-slice_fusion), channel_id=1, source_target_pairs={{0,1},{1,0},{2,3},{3,2},{4,5},{5,4},{6,7},{7,6},{8,9},{9,8},{10,11... | collective-permute-start | bytes 12582920 | tf_op jit(solution)/shard_map/ppermute | solution.py:269
  61.8 51.4 %copy-start.3 = (bf16[2,1024,256]{2,1,0:T(8,128)(2,1)}, bf16[2,1024,256]{2,1,0:T(8,128)(2,1)S(1)}, u32[]{:S(2)}) copy-start(bf16[2,1024,256]{2,1,0:T(8,128)(2,1)S(1)} %collective-permute-done.9.refs_2_.refs_9_) | copy-start | bytes 3145732
  71.2 23.2 %collective-permute-start.14 = (bf16[2,1024,256]{2,1,0:T(8,128)(2,1)S(1)}, bf16[2,1024,256]{2,1,0:T(8,128)(2,1)S(1)}, u32[]{:S(2)}, u32[]{:S(2)}) collective-permute-start(bf16[2,1024,256]{2,1,0:T(8,128)(2,1)S(1)} %collective-permute-done.9.refs_2_.refs_9_), channel_id=1, source_target_pairs={{0,2},{1,3},{2,0},{3,1},{4,6},{5,7},{6,4},{7,5},{8,10},{9,11},{10,... | collective-permute-start | bytes 3145736 | tf_op jit(solution)/shard_map/ppermute | solution.py:269
  72.7 24.2 %collective-permute-start.15 = (bf16[2,1024,256]{2,1,0:T(8,128)(2,1)S(1)}, bf16[2,1024,256]{2,1,0:T(8,128)(2,1)}, u32[]{:S(2)}, u32[]{:S(2)}) collective-permute-start(bf16[2,1024,256]{2,1,0:T(8,128)(2,1)S(1)} %collective-permute-done.9.refs_2_.refs_9_), channel_id=1, source_target_pairs={{0,4},{1,5},{2,6},{3,7},{4,0},{5,1},{6,2},{7,3},{8,12},{9,13},{10,... | collective-permute-start | bytes 3145736 | tf_op jit(solution)/shard_map/ppermute | solution.py:269
  73.7 24.3 %collective-permute-start.1 = (s32[1,2]{1,0:T(1,128)S(1)}, s32[1,2]{1,0:T(1,128)S(1)}, u32[]{:S(2)}, u32[]{:S(2)}) collective-permute-start(s32[1,2]{1,0:T(1,128)S(1)} %bitcast.71), channel_id=1, source_target_pairs={{0,8},{1,9},{2,10},{3,11},{4,12},{5,13},{6,14},{7,15},{8,0},{9,1},... | collective-permute-start | bytes 32 | tf_op jit(solution)/shard_map/ppermute | solution.py:269
  76.1 27.9 %collective-permute-start.7 = (bf16[1,1024,256]{2,1,0:T(8,128)(2,1)S(1)}, bf16[1,1024,256]{2,1,0:T(8,128)(2,1)S(1)}, u32[]{:S(2)}, u32[]{:S(2)}) collective-permute-start(bf16[1,1024,256]{2,1,0:T(8,128)(2,1)S(1)} %slice.89), channel_id=1, source_target_pairs={{0,24},{1,25},{2,26},{3,27},{4,28},{5,29},{6,30},{7,31},{8,16},{9,... | collective-permute-start | bytes 1572872 | tf_op jit(solution)/shard_map/ppermute | solution.py:269
  94.4 17.5 %collective-permute-start.19 = (bf16[1,1024,256]{2,1,0:T(8,128)(2,1)S(1)}, bf16[1,1024,256]{2,1,0:T(8,128)(2,1)S(1)}, u32[]{:S(2)}, u32[]{:S(2)}) collective-permute-start(bf16[1,1024,256]{2,1,0:T(8,128)(2,1)S(1)} %slice.110), channel_id=1, source_target_pairs={{0,4},{1,5},{2,6},{3,7},{4,0},{5,1},{6,2},{7,3},{8,12},{9,13},{10,... | collective-permute-start | bytes 1572872 | tf_op jit(solution)/shard_map/ppermute | solution.py:269
  98.0 15.2 %collective-permute-start.20 = (bf16[1,1024,256]{2,1,0:T(8,128)(2,1)S(1)}, bf16[1,1024,256]{2,1,0:T(8,128)(2,1)S(1)}, u32[]{:S(2)}, u32[]{:S(2)}) collective-permute-start(bf16[1,1024,256]{2,1,0:T(8,128)(2,1)S(1)} %slice.111), channel_id=1, source_target_pairs={{0,2},{1,3},{2,0},{3,1},{4,6},{5,7},{6,4},{7,5},{8,10},{9,11},{10,... | collective-permute-start | bytes 1572872 | tf_op jit(solution)/shard_map/ppermute | solution.py:269
  98.1 4.5 %collective-permute-start.2 = (s32[2,2]{1,0:T(2,128)S(1)}, s32[2,2]{1,0:T(2,128)S(1)}, u32[]{:S(2)}, u32[]{:S(2)}) collective-permute-start(s32[2,2]{1,0:T(2,128)S(1)} %pad_add_fusion.1), channel_id=1, source_target_pairs={{0,16},{1,17},{2,18},{3,19},{4,20},{5,21},{6,22},{7,23},{8,24},{9,... | collective-permute-start | bytes 56 | tf_op jit(solution)/shard_map/ppermute | solution.py:269
  104.0 73.4 %copy-start.1 = (bf16[2,1024,256]{2,1,0:T(8,128)(2,1)}, bf16[2,1024,256]{2,1,0:T(8,128)(2,1)S(1)}, u32[]{:S(2)}) copy-start(bf16[2,1024,256]{2,1,0:T(8,128)(2,1)S(1)} %pad_maximum_fusion.1.refs_3_.refs_14_) | copy-start | bytes 3145732
  105.5 13.8 %collective-permute-start.8 = (bf16[1,1024,256]{2,1,0:T(8,128)(2,1)S(1)}, bf16[1,1024,256]{2,1,0:T(8,128)(2,1)S(1)}, u32[]{:S(2)}, u32[]{:S(2)}) collective-permute-start(bf16[1,1024,256]{2,1,0:T(8,128)(2,1)S(1)} %slice.90), channel_id=1, source_target_pairs={{0,24},{1,25},{2,26},{3,27},{4,28},{5,29},{6,30},{7,31},{8,16},{9,... | collective-permute-start | bytes 1572872 | tf_op jit(solution)/shard_map/ppermute | solution.py:269
  110.5 21.2 %collective-permute-start.16 = (bf16[2,1024,256]{2,1,0:T(8,128)(2,1)S(1)}, bf16[2,1024,256]{2,1,0:T(8,128)(2,1)S(1)}, u32[]{:S(2)}, u32[]{:S(2)}) collective-permute-start(bf16[2,1024,256]{2,1,0:T(8,128)(2,1)S(1)} %pad_maximum_fusion.1.refs_3_.refs_14_), channel_id=1, source_target_pairs={{0,2},{1,3},{2,0},{3,1},{4,6},{5,7},{6,4},{7,5},{8,10},{9,11},{10,... | collective-permute-start | bytes 3145736 | tf_op jit(solution)/shard_map/ppermute | solution.py:269
  111.9 20.3 %collective-permute-start.17 = (bf16[2,1024,256]{2,1,0:T(8,128)(2,1)S(1)}, bf16[2,1024,256]{2,1,0:T(8,128)(2,1)S(1)}, u32[]{:S(2)}, u32[]{:S(2)}) collective-permute-start(bf16[2,1024,256]{2,1,0:T(8,128)(2,1)S(1)} %pad_maximum_fusion.1.refs_3_.refs_14_), channel_id=1, source_target_pairs={{0,4},{1,5},{2,6},{3,7},{4,0},{5,1},{6,2},{7,3},{8,12},{9,13},{10,... | collective-permute-start | bytes 3145736 | tf_op jit(solution)/shard_map/ppermute | solution.py:269
  114.0 20.9 %collective-permute-start.21 = (bf16[2,2,512,256]{3,2,1,0:T(8,128)(2,1)S(1)}, bf16[2,2,512,256]{3,2,1,0:T(8,128)(2,1)S(1)}, u32[]{:S(2)}, u32[]{:S(2)}) collective-permute-start(bf16[2,2,512,256]{3,2,1,0:T(8,128)(2,1)S(1)} %pad_maximum_fusion.3), channel_id=1, source_target_pairs={{0,1},{1,0},{2,3},{3,2},{4,5},{5,4},{6,7},{7,6},{8,9},{9,8},{10,11... | collective-permute-start | bytes 3145736 | tf_op jit(solution)/shard_map/ppermute | solution.py:269
  114.2 20.8 %copy-start.4 = (bf16[2,1024,256]{2,1,0:T(8,128)(2,1)S(1)}, bf16[2,1024,256]{2,1,0:T(8,128)(2,1)}, u32[]{:S(2)}) copy-start(bf16[2,1024,256]{2,1,0:T(8,128)(2,1)} %copy-done.3) | copy-start | bytes 3145732
  119.3 17.0 %collective-permute-start.24 = (bf16[2,2,512,256]{3,2,1,0:T(8,128)(2,1)S(1)}, bf16[2,2,512,256]{3,2,1,0:T(8,128)(2,1)S(1)}, u32[]{:S(2)}, u32[]{:S(2)}) collective-permute-start(bf16[2,2,512,256]{3,2,1,0:T(8,128)(2,1)S(1)} %pad_maximum_fusion.5), channel_id=1, source_target_pairs={{1,8},{3,10},{5,12},{7,14},{8,1},{9,16},{10,3},{11,18},{12,5},{13,... | collective-permute-start | bytes 3145736 | tf_op jit(solution)/shard_map/ppermute | solution.py:269
  120.2 40.8 %copy-start.2 = (bf16[2,1024,256]{2,1,0:T(8,128)(2,1)}, bf16[2,1024,256]{2,1,0:T(8,128)(2,1)S(1)}, u32[]{:S(2)}) copy-start(bf16[2,1024,256]{2,1,0:T(8,128)(2,1)S(1)} %pad_maximum_fusion.refs_3_.refs_19_) | copy-start | bytes 3145732
  132.3 25.0 %collective-permute-start.27 = (bf16[2,1024,256]{2,1,0:T(8,128)(2,1)S(1)}, bf16[2,1024,256]{2,1,0:T(8,128)(2,1)S(1)}, u32[]{:S(2)}, u32[]{:S(2)}) collective-permute-start(bf16[2,1024,256]{2,1,0:T(8,128)(2,1)S(1)} %pad_maximum_fusion.refs_3_.refs_19_), channel_id=1, source_target_pairs={{0,2},{1,3},{2,0},{3,1},{4,6},{5,7},{6,4},{7,5},{8,10},{9,11},{10,... | collective-permute-start | bytes 3145736 | tf_op jit(solution)/shard_map/ppermute | solution.py:269
  133.5 25.1 %collective-permute-start.28 = (bf16[2,1024,256]{2,1,0:T(8,128)(2,1)S(1)}, bf16[2,1024,256]{2,1,0:T(8,128)(2,1)S(1)}, u32[]{:S(2)}, u32[]{:S(2)}) collective-permute-start(bf16[2,1024,256]{2,1,0:T(8,128)(2,1)S(1)} %pad_maximum_fusion.refs_3_.refs_19_), channel_id=1, source_target_pairs={{0,4},{1,5},{2,6},{3,7},{4,0},{5,1},{6,2},{7,3},{8,12},{9,13},{10,... | collective-permute-start | bytes 3145736 | tf_op jit(solution)/shard_map/ppermute | solution.py:269
  134.9 26.1 %copy-start.5 = (bf16[2,2,512,256]{3,2,1,0:T(8,128)(2,1)}, bf16[2,2,512,256]{3,2,1,0:T(8,128)(2,1)S(1)}, u32[]{:S(2)}) copy-start(bf16[2,2,512,256]{3,2,1,0:T(8,128)(2,1)S(1)} %collective-permute-done.21.refs_4_) | copy-start | bytes 3145732
  134.9 26.1 %collective-permute-start.22 = (bf16[2,2,512,256]{3,2,1,0:T(8,128)(2,1)S(1)}, bf16[2,2,512,256]{3,2,1,0:T(8,128)(2,1)S(1)}, u32[]{:S(2)}, u32[]{:S(2)}) collective-permute-start(bf16[2,2,512,256]{3,2,1,0:T(8,128)(2,1)S(1)} %pad_maximum_fusion.4), channel_id=1, source_target_pairs={{0,1},{1,0},{2,3},{3,2},{4,5},{5,4},{6,7},{7,6},{8,9},{9,8},{10,11... | collective-permute-start | bytes 3145736 | tf_op jit(solution)/shard_map/ppermute | solution.py:269
  136.3 41.1 %collective-permute-start.18 = (bf16[2,2,512,256]{3,2,1,0:T(8,128)(2,1)}, bf16[2,2,512,256]{3,2,1,0:T(8,128)(2,1)}, u32[]{:S(2)}, u32[]{:S(2)}) collective-permute-start(bf16[2,2,512,256]{3,2,1,0:T(8,128)(2,1)} %pad_maximum_fusion.2), channel_id=1, source_target_pairs={{1,8},{3,10},{5,12},{7,14},{8,1},{9,16},{10,3},{11,18},{12,5},{13,... | collective-permute-start | bytes 3145736 | tf_op jit(solution)/shard_map/ppermute | solution.py:269
  157.3 15.2 %copy-start.26 = (bf16[2,1024,256]{2,1,0:T(8,128)(2,1)}, bf16[2,1024,256]{2,1,0:T(8,128)(2,1)S(1)}, u32[]{:S(2)}) copy-start(bf16[2,1024,256]{2,1,0:T(8,128)(2,1)S(1)} %collective-permute-done.27.refs_20_) | copy-start | bytes 3145732
  157.3 15.2 %collective-permute-start.25 = (bf16[1,1024,256]{2,1,0:T(8,128)(2,1)S(1)}, bf16[1,1024,256]{2,1,0:T(8,128)(2,1)S(1)}, u32[]{:S(2)}, u32[]{:S(2)}) collective-permute-start(bf16[1,1024,256]{2,1,0:T(8,128)(2,1)S(1)} %slice.112), channel_id=1, source_target_pairs={{0,4},{1,5},{2,6},{3,7},{4,0},{5,1},{6,2},{7,3},{8,12},{9,13},{10,... | collective-permute-start | bytes 1572872 | tf_op jit(solution)/shard_map/ppermute | solution.py:269
  158.5 14.0 %copy-start.27 = (bf16[2,1024,256]{2,1,0:T(8,128)(2,1)}, bf16[2,1024,256]{2,1,0:T(8,128)(2,1)S(1)}, u32[]{:S(2)}) copy-start(bf16[2,1024,256]{2,1,0:T(8,128)(2,1)S(1)} %collective-permute-done.28.refs_21_) | copy-start | bytes 3145732
  158.5 14.8 %collective-permute-start.26 = (bf16[1,1024,256]{2,1,0:T(8,128)(2,1)S(1)}, bf16[1,1024,256]{2,1,0:T(8,128)(2,1)S(1)}, u32[]{:S(2)}, u32[]{:S(2)}) collective-permute-start(bf16[1,1024,256]{2,1,0:T(8,128)(2,1)S(1)} %slice.113), channel_id=1, source_target_pairs={{0,2},{1,3},{2,0},{3,1},{4,6},{5,7},{6,4},{7,5},{8,10},{9,11},{10,... | collective-permute-start | bytes 1572872 | tf_op jit(solution)/shard_map/ppermute | solution.py:269
  161.0 15.5 %copy-start.29 = (s32[2,32]{1,0:T(2,128)S(1)}, s32[2,32]{1,0:T(2,128)}, u32[]{:S(2)}) copy-start(s32[2,32]{1,0:T(2,128)} %param.11) | copy-start | bytes 772
  174.2 17.4 %collective-permute-start.29 = (bf16[1,1024,256]{2,1,0:T(8,128)(2,1)}, bf16[1,1024,256]{2,1,0:T(8,128)(2,1)S(1)}, u32[]{:S(2)}, u32[]{:S(2)}) collective-permute-start(bf16[1,1024,256]{2,1,0:T(8,128)(2,1)} %slice.114), channel_id=1, source_target_pairs={{0,4},{1,5},{2,6},{3,7},{4,0},{5,1},{6,2},{7,3},{8,12},{9,13},{10,... | collective-permute-start | bytes 1572872 | tf_op jit(solution)/shard_map/ppermute | solution.py:269
  175.4 16.1 %collective-permute-start.30 = (bf16[1,1024,256]{2,1,0:T(8,128)(2,1)}, bf16[1,1024,256]{2,1,0:T(8,128)(2,1)S(1)}, u32[]{:S(2)}, u32[]{:S(2)}) collective-permute-start(bf16[1,1024,256]{2,1,0:T(8,128)(2,1)} %slice.115), channel_id=1, source_target_pairs={{0,2},{1,3},{2,0},{3,1},{4,6},{5,7},{6,4},{7,5},{8,10},{9,11},{10,... | collective-permute-start | bytes 1572872 | tf_op jit(solution)/shard_map/ppermute | solution.py:269
  200.8 2.0 collective-permute-start.31
  203.0 8.4 %collective-permute-start.34 = (bf16[2,2,2,64,128]{4,3,2,1,0:T(8,128)(2,1)S(1)}, bf16[2,2,2,64,128]{4,3,2,1,0:T(8,128)(2,1)S(1)}, u32[]{:S(2)}, u32[]{:S(2)}) collective-permute-start(bf16[2,2,2,64,128]{4,3,2,1,0:T(8,128)(2,1)S(1)} %bitcast.69), channel_id=1, source_target_pairs={{0,24},{1,25},{2,26},{3,27},{4,28},{5,29},{6,30},{7,31},{8,16},{9,... | collective-permute-start | bytes 393224 | tf_op jit(solution)/shard_map/ppermute | solution.py:269
  207.0 9.6 %collective-permute-start.33 = (bf16[2,2,2,64,128]{4,3,2,1,0:T(8,128)(2,1)S(1)}, bf16[2,2,2,64,128]{4,3,2,1,0:T(8,128)(2,1)S(1)}, u32[]{:S(2)}, u32[]{:S(2)}) collective-permute-start(bf16[2,2,2,64,128]{4,3,2,1,0:T(8,128)(2,1)S(1)} %bitcast.68), channel_id=1, source_target_pairs={{0,16},{1,17},{2,18},{3,19},{4,20},{5,21},{6,22},{7,23},{8,24},{9,... | collective-permute-start | bytes 393224 | tf_op jit(solution)/shard_map/ppermute | solution.py:269
  207.0 9.6 %collective-permute-start.32 = (bf16[2,2,2,64,128]{4,3,2,1,0:T(8,128)(2,1)S(1)}, bf16[2,2,2,64,128]{4,3,2,1,0:T(8,128)(2,1)S(1)}, u32[]{:S(2)}, u32[]{:S(2)}) collective-permute-start(bf16[2,2,2,64,128]{4,3,2,1,0:T(8,128)(2,1)S(1)} %bitcast.67), channel_id=1, source_target_pairs={{0,8},{1,9},{2,10},{3,11},{4,12},{5,13},{6,14},{7,15},{8,0},{9,1},... | collective-permute-start | bytes 393224 | tf_op jit(solution)/shard_map/ppermute | solution.py:269
  (20 other events, 123.0 us)
